TPU v7x, 32 devices: a whole 2x2x4 slice. The times are simulated.
32 devices in a mesh: req: 8 (over z, y), mlp: 4 (over x, core).
Axes of the slice: x: 2, y: 2, z: 4, core: 2. Of those that a mesh axis runs over, the one named last changes fastest.
Arguments:
- tokens: bfloat16 [2048, 2048], P('req', 'mlp'), may hold values from -5 to 5
- attn_gain: float32 [2048], replicated, may hold values from 0.5 to 1.5
- mlp_gain: float32 [2048], replicated, may hold values from 0.5 to 1.5
- final_gain: float32 [2048], replicated, may hold values from 0.25 to 4
- q_gain: float32 [64], replicated, may hold values from 0.5 to 1.5
- k_gain: float32 [64], replicated, may hold values from 0.25 to 4
- w_query: bfloat16 [2048, 2048], P(None, 'mlp'), may hold values from -0.125 to 0.125
- w_keyval: bfloat16 [2048, 1024], P(None, 'mlp'), may hold values from -0.125 to 0.125
- w_out: bfloat16 [2048, 2048], P('mlp'), may hold values from -0.125 to 0.125
- w_gate: bfloat16 [2048, 8192], P(None, 'mlp'), may hold values from -0.125 to 0.125
- w_up: bfloat16 [2048, 8192], P(None, 'mlp'), may hold values from -0.125 to 0.125
- w_down: bfloat16 [8192, 2048], P('mlp'), may hold values from -0.0625 to 0.0625
- w_head: bfloat16 [2048, 65536], P('req', 'mlp'), may hold values from -0.42 to 0.42
- targets: int32 [2048], P('req'), may hold values from 0 to 65535
- req_lengths: int32 [8, 4], P('req'), may hold values from 1 to 128, 256 in all within a row
- req_tenant: int32 [8, 4], P('req'), may hold values from 0 to 3
- prefix_piece: int32 [8], replicated, may hold values from 0 to 7, each once
- prefix_kv: bfloat16 [8, 2048, 1024], P('req', None, 'mlp'), may hold values from -160 to 160
Outputs:
- hidden_out: bfloat16 [2048, 2048], P('req', 'mlp')
- logprob: float32 [2048], P('req')
Inputs may be any that keep to these rules, and one draw needn't show every extreme that they name: `req_lengths`: each row sums to 256; its longest request has exactly 128 tokens. `prefix_piece`: every piece number appears once; piece n is part n % 2 of the prefix of tenant n // 2.
All inputs are finite; a program needn't handle non-finite values.
Results may differ from a plain program's by a relative error of at most 0.023.
Values may be sent and summed in bfloat16 or wider, within the bound.
No kernel may reach another device: no remote copies, remote signals or barrier semaphores. Data moves between devices by JAX's collectives and lax.ppermute only.
A program may use at most 192 MiB of HBM per device.

v0:
```python
import math

import jax
import jax.numpy as jnp
from jax import lax
from jax.sharding import PartitionSpec as P

TENANTS = 4
PLEN = 4096


EPS = 1e-05
LOG_THETA = math.log(1000000.0)
NEG = -1e30


def rms_norm(values, gain):
    return values * lax.rsqrt(jnp.mean(values * values, axis=-1, keepdims=True) + EPS) * gain


def rope_tables(position, size):
    half = size // 2
    freq = jnp.exp(jnp.arange(half, dtype=jnp.float32) * (-2.0 * LOG_THETA / size))
    angle = position[:, None] * freq[None, :]
    return (jnp.cos(angle), jnp.sin(angle))


def rotate(values, cosine, sine):
    half = values.shape[-1] // 2
    first = values[..., :half]
    second = values[..., half:]
    cosine = cosine[:, None, :]
    sine = sine[:, None, :]
    return jnp.concatenate(
        [first * cosine - second * sine, first * sine + second * cosine], axis=-1
    )


def row_layout(lengths, tenants, count):
    ends = jnp.cumsum(lengths)
    row_ids = jnp.arange(count, dtype=jnp.int32)
    request = jnp.sum((row_ids[:, None] >= ends[None, :]).astype(jnp.int32), axis=1)
    onehot = (request[:, None] == jnp.arange(lengths.shape[0], dtype=jnp.int32)[None, :]).astype(
        jnp.int32
    )
    starts = ends - lengths
    offset = row_ids - jnp.sum(onehot * starts[None, :], axis=1)
    tenant = jnp.sum(onehot * tenants[None, :], axis=1)
    return (request, offset, tenant)


def absorb(state, queries, keys, values, seen, scale):
    best, total, accum = state
    scores = jnp.einsum("kqd,knd->kqn", queries, keys, preferred_element_type=jnp.float32) * scale
    scores = jnp.where(seen[None], scores, NEG)
    new_best = jnp.maximum(best, jnp.max(scores, axis=-1))
    keep = jnp.exp(best - new_best)
    weights = jnp.where(seen[None], jnp.exp(scores - new_best[..., None]), 0.0)
    total = total * keep + jnp.sum(weights, axis=-1)
    accum = accum * keep[..., None] + jnp.einsum(
        "kqn,knd->kqd", weights.astype(jnp.bfloat16), values, preferred_element_type=jnp.float32
    )
    return (new_best, total, accum)


def body(
    tokens,
    attn_gain,
    mlp_gain,
    final_gain,
    q_gain,
    k_gain,
    w_query,
    w_keyval,
    w_out,
    w_gate,
    w_up,
    w_down,
    w_head,
    targets,
    req_lengths,
    req_tenant,
    prefix_piece,
    prefix_kv,
):
    rows = tokens.shape[0]
    head_size = q_gain.shape[0]
    local_kv = w_keyval.shape[1] // (2 * head_size)
    local_q = w_query.shape[1] // head_size
    group = local_q // local_kv
    split_count = lax.axis_size("req") // TENANTS
    scale = head_size ** (-0.5)
    stream = lax.all_gather(tokens, "mlp", axis=1, tiled=True)
    stream_f = stream.astype(jnp.float32)
    normed = rms_norm(stream_f, attn_gain).astype(jnp.bfloat16)
    query = jnp.dot(normed, w_query, preferred_element_type=jnp.float32).reshape(
        rows, local_q, head_size
    )
    keyval = jnp.dot(normed, w_keyval, preferred_element_type=jnp.float32).reshape(
        rows, local_kv, 2, head_size
    )
    request, offset, tenant = row_layout(req_lengths[0], req_tenant[0], rows)
    cosine, sine = rope_tables((PLEN + offset).astype(jnp.float32), head_size)
    query = rotate(rms_norm(query, q_gain), cosine, sine).astype(jnp.bfloat16)
    own_keys = (
        rotate(rms_norm(keyval[:, :, 0], k_gain), cosine, sine)
        .astype(jnp.bfloat16)
        .transpose(1, 0, 2)
    )
    own_vals = keyval[:, :, 1].astype(jnp.bfloat16).transpose(1, 0, 2)
    queries = (
        query.reshape(rows, local_kv, group, head_size)
        .transpose(1, 2, 0, 3)
        .reshape(local_kv, group * rows, head_size)
    )
    start_state = (
        jnp.full((local_kv, group * rows), NEG, jnp.float32),
        jnp.zeros((local_kv, group * rows), jnp.float32),
        jnp.zeros((local_kv, group * rows, head_size), jnp.float32),
    )
    piece = lax.all_gather(prefix_kv, "req", axis=0, tiled=True)
    slab = piece.shape[1]

    def one_piece(index, inner_state):
        block = lax.dynamic_index_in_dim(piece, index, 0, keepdims=False).reshape(
            slab, local_kv, 2, head_size
        )
        block_keys = block[:, :, 0].transpose(1, 0, 2)
        block_vals = block[:, :, 1].transpose(1, 0, 2)
        owner_tenant = (
            lax.dynamic_index_in_dim(prefix_piece, index, 0, keepdims=False) // split_count
        )
        seen = jnp.tile(tenant == owner_tenant, group)[:, None]
        return absorb(inner_state, queries, block_keys, block_vals, seen, scale)

    state = lax.fori_loop(0, piece.shape[0], one_piece, start_state)
    row_ids = jnp.arange(rows, dtype=jnp.int32)
    causal = (request[:, None] == request[None, :]) & (row_ids[None, :] <= row_ids[:, None])
    best, total, accum = absorb(
        state, queries, own_keys, own_vals, jnp.tile(causal, (group, 1)), scale
    )
    attended = (
        (accum / total[..., None])
        .reshape(local_kv, group, rows, head_size)
        .transpose(2, 0, 1, 3)
        .reshape(rows, local_q * head_size)
        .astype(jnp.bfloat16)
    )
    attn_proj = jnp.dot(attended, w_out, preferred_element_type=jnp.float32)
    attn_part = lax.psum_scatter(
        attn_proj.astype(jnp.bfloat16), "mlp", scatter_dimension=1, tiled=True
    ).astype(jnp.float32)
    mid_share = (tokens.astype(jnp.float32) + attn_part).astype(jnp.bfloat16)
    middle = lax.all_gather(mid_share, "mlp", axis=1, tiled=True)
    middle_f = middle.astype(jnp.float32)
    normed_mid = rms_norm(middle_f, mlp_gain).astype(jnp.bfloat16)
    gate = jnp.dot(normed_mid, w_gate, preferred_element_type=jnp.float32)
    upper = jnp.dot(normed_mid, w_up, preferred_element_type=jnp.float32)
    inner = (jax.nn.silu(gate) * upper).astype(jnp.bfloat16)
    down = jnp.dot(inner, w_down, preferred_element_type=jnp.float32)
    down_part = lax.psum_scatter(
        down.astype(jnp.bfloat16), "mlp", scatter_dimension=1, tiled=True
    ).astype(jnp.float32)
    out_share = (mid_share.astype(jnp.float32) + down_part).astype(jnp.bfloat16)
    hidden_full = lax.all_gather(out_share, "mlp", axis=1, tiled=True)
    normed_out = rms_norm(hidden_full.astype(jnp.float32), final_gain).astype(jnp.bfloat16)
    vocab_local = w_head.shape[1]
    logits = jnp.dot(
        normed_out,
        lax.all_gather(w_head, "req", axis=0, tiled=True),
        preferred_element_type=jnp.float32,
    )
    vocab_start = lax.axis_index("mlp") * vocab_local
    top = lax.pmax(jnp.max(logits, axis=1), "mlp")
    hit = targets[:, None] - vocab_start == jnp.arange(vocab_local, dtype=jnp.int32)[None, :]
    totals, picked = lax.psum(
        (
            jnp.sum(jnp.exp(logits - top[:, None]), axis=1),
            jnp.sum(jnp.where(hit, logits, 0.0), axis=1),
        ),
        "mlp",
    )
    logprob = picked - top - jnp.log(totals)
    return (out_share, logprob)


def solution(mesh):
    in_specs = (
        P("req", "mlp"),
        P(),
        P(),
        P(),
        P(),
        P(),
        P(None, "mlp"),
        P(None, "mlp"),
        P("mlp", None),
        P(None, "mlp"),
        P(None, "mlp"),
        P("mlp", None),
        P("req", "mlp"),
        P("req"),
        P("req", None),
        P("req", None),
        P(),
        P("req", None, "mlp"),
    )
    out_specs = (P("req", "mlp"), P("req"))
    return jax.shard_map(body, mesh=mesh, in_specs=in_specs, out_specs=out_specs, check_vma=False)
```

profile of v0, /device:TPU:0, one launch (start us, length us, event | category | flops | bytes accessed | tf_op | source)
XLA Modules:
  0.0 1834.6 jit_solution(14934852212568790938)
XLA Ops:
  10.5 18.5 %all-gather.8.cloned.1.call-done = bf16[256,2048]{1,0:T(8,128)(2,1)} async-done(((bf16[256,512]{1,0:T(8,128)(2,1)}), bf16[256,2048]{1,0:T(8,128)(2,1)}) %all-gather.8.cloned.1.call-update) | async-done | bytes 1048592 | tf_op jit(solution)/shard_map/all_gather | solution.py:93
  29.1 1.5 fusion.18
  30.6 2.9 multiply_reduce_fusion
  34.4 2.2 fusion.45
  36.8 2.0 fusion.27
  38.7 117.4 %all-gather.6.cloned.1.call-done = bf16[8,2048,256]{2,1,0:T(8,128)(2,1)} async-done(((bf16[1,2048,256]{2,1,0:T(8,128)(2,1)}), bf16[8,2048,256]{2,1,0:T(8,128)(2,1)}) %all-gather.6.cloned.1.call-update) | async-done | bytes 8388624 | tf_op jit(solution)/shard_map/all_gather | solution.py:121
  156.2 236.9 %while.20 = (s32[]{:T(128)}, f32[2,1024]{1,0:T(2,128)S(1)}, f32[2,1024]{1,0:T(2,128)S(1)}, f32[2,1024,64]{1,2,0:T(8,128)}, s32[8]{0:T(128)S(1)}, /*index=5*/s32[...) while((s32[]{:T(128)}, f32[2,1024]{1,0:T(2,128)S(1)}, ...), condition=%wide.region_9.10_spmd.clone, body=%wide.region_6.0_spmd.clone.sunk | while | flops 1128671488 | bytes 128328536 | solution.py:136
  160.3 1.4 copy.83
  161.7 8.2 bitcast_reduce_fusion.2
  170.0 8.1 fusion.84
  178.1 2.6 copy-done.1
  180.6 4.3 fusion.86
  189.1 1.4 copy.83
  190.5 8.2 bitcast_reduce_fusion.2
  198.7 8.1 fusion.84
  206.8 2.6 copy-done.1
  209.4 5.3 fusion.86
  218.8 1.4 copy.83
  220.2 8.2 bitcast_reduce_fusion.2
  228.5 8.1 fusion.84
  236.6 2.6 copy-done.1
  239.1 5.3 fusion.86
  248.5 1.4 copy.83
  250.0 8.2 bitcast_reduce_fusion.2
  258.2 8.1 fusion.84
  266.3 2.6 copy-done.1
  268.9 5.3 fusion.86
  278.2 1.4 copy.83
  279.7 8.2 bitcast_reduce_fusion.2
  287.9 8.1 fusion.84
  296.0 2.6 copy-done.1
  298.6 5.3 fusion.86
  309.4 8.2 bitcast_reduce_fusion.2
  317.7 8.1 fusion.84
  325.8 2.6 copy-done.1
  328.3 5.3 fusion.86
  337.7 1.4 copy.83
  339.2 8.2 bitcast_reduce_fusion.2
  347.4 8.1 fusion.84
  355.5 2.6 copy-done.1
  358.1 5.3 fusion.86
  367.4 1.4 copy.83
  368.9 8.2 bitcast_reduce_fusion.2
  377.1 8.1 fusion.84
  385.2 2.6 copy-done.1
  387.8 5.3 fusion.86
  393.1 2.3 fusion.28
  395.4 1.9 fusion.31
  397.4 1.7 convolution_convert_fusion
  399.2 23.1 %reduce-scatter.3.cloned.1.call-done = bf16[256,512]{1,0:T(8,128)(2,1)} async-done(((bf16[256,2048]{1,0:T(8,128)(2,1)}), bf16[256,512]{1,0:T(8,128)(2,1)}) %reduce-scatter.3.cloned.1.call-update) | async-done | bytes 262160 | tf_op jit(solution)/shard_map/reduce_scatter | solution.py:150
  422.3 1.7 add_convert_fusion.1
  424.3 16.9 all-gather.10.cloned.1.call-done
  441.2 1.5 fusion.21
  442.7 7.5 fusion.43
  450.2 12.1 convolution_convert_fusion.1
  462.4 25.0 %reduce-scatter.5.cloned.1.call-done = bf16[256,512]{1,0:T(8,128)(2,1)} async-done(((bf16[256,2048]{1,0:T(8,128)(2,1)}), bf16[256,512]{1,0:T(8,128)(2,1)}) %reduce-scatter.5.cloned.1.call-update) | async-done | bytes 262160 | tf_op jit(solution)/shard_map/reduce_scatter | solution.py:161
  487.4 1.7 add_convert_fusion
  490.0 16.2 all-gather.12.cloned.1.call-done
  506.2 1.5 fusion.24
  507.7 1267.0 %all-gather.14.cloned.1.call-done = bf16[2048,16384]{1,0:T(8,128)(2,1)} async-done(((bf16[256,16384]{1,0:T(8,128)(2,1)}), bf16[2048,16384]{1,0:T(8,128)(2,1)}) %all-gather.14.cloned.1.call-update) | async-done | bytes 67108880 | tf_op jit(solution)/shard_map/all_gather | solution.py:170
  1774.7 31.0 %fusion.61 = (f32[256]{0:T(256)S(1)}, f32[256,16384]{1,0:T(8,128)}) fusion(bf16[2048,16384]{1,0:T(8,128)(2,1)} %all-gather.14.cloned.1.call-done, bf16[256,2048]{1,0:T(8,128)(2,1)} %all-gather.12.cloned.1.call-done, f32[2048]{0:T(1024)S(1)} %copy-done.16, f32[256]{0:T(256)S(1)} %add_rsqrt_fusion.2), kind=kOutput, calls=%fused_computation.111 | convolution fusion | flops 17186160640 | bytes 84944896 | tf_op jit(solution)/shard_map/dot_general | solution.py:168
  1805.6 6.9 pmax.7
  1812.5 8.8 select_reduce_fusion
  1821.3 5.9 all-reduce
  (169 shorter events, 22.7 us)
Async XLA Ops:
  7.2 390.2 %copy-start = (bf16[512,2048]{1,0:T(8,128)(2,1)S(1)}, bf16[512,2048]{1,0:T(8,128)(2,1)}, u32[]{:S(2)}) copy-start(bf16[512,2048]{1,0:T(8,128)(2,1)} %param.28) | copy-start | bytes 6291460
  7.2 3.0 copy-start.17
  7.2 3.0 copy-start.13
  7.2 23.4 %copy-start.14 = (f32[2048]{0:T(1024)S(1)}, f32[2048]{0:T(1024)}, u32[]{:S(2)}) copy-start(f32[2048]{0:T(1024)} %param.21) | copy-start | bytes 24580
  7.2 21.9 %all-gather.8.cloned.1.call-start = ((), (), s32[]{:S(2)}) async-start(), calls=%async_computation.3 | async-start | bytes 1310720 | tf_op jit(solution)/shard_map/all_gather | solution.py:93
  7.9 148.2 %all-gather.6.cloned.1.call-start = ((), (), s32[]{:S(2)}) async-start(), calls=%async_computation.2 | async-start | bytes 9437184 | tf_op jit(solution)/shard_map/all_gather | solution.py:121
  8.7 413.6 %reduce-scatter.3.cloned.1.call-start = ((), (), s32[]{:S(2)}) async-start(), calls=%async_computation.4 | async-start | bytes 1310720 | tf_op jit(solution)/shard_map/reduce_scatter | solution.py:150
  10.2 26.6 %copy-start.6 = (pred[32,8,4,256]{3,1,2,0:T(8,128)(4,1)}, pred[32,8,4,256]{3,1,2,0:T(8,128)(4,1)S(1)}, u32[]{:S(2)}) copy-start(pred[32,8,4,256]{3,1,2,0:T(8,128)(4,1)S(1)} %copy.70) | copy-start | bytes 786436
  30.6 3.0 copy-start.11
  34.0 2.6 copy-start.12
  36.6 119.6 %copy-start.9 = (f32[256,256]{0,1:T(8,128)}, f32[256,256]{0,1:T(8,128)S(1)}, u32[]{:S(2)}) copy-start(f32[256,256]{0,1:T(8,128)S(1)} %fusion.45) | copy-start | bytes 786436
  36.6 119.6 %copy-start.18 = (s32[8]{0:T(128)S(1)}, s32[8]{0:T(128)}, u32[]{:S(2)}) copy-start(s32[8]{0:T(128)} %param.36) | copy-start | bytes 100
  161.7 16.3 copy-start.2
  169.9 10.7 copy-start.1
  190.5 16.3 copy-start.2
  198.7 10.7 copy-start.1
  220.2 16.3 copy-start.2
  228.5 10.7 copy-start.1
  250.0 16.3 copy-start.2
  258.2 10.7 copy-start.1
  279.7 16.3 copy-start.2
  287.9 10.7 copy-start.1
  309.4 16.3 copy-start.2
  317.6 10.7 copy-start.1
  339.1 16.3 copy-start.2
  347.4 10.7 copy-start.1
  368.9 16.3 copy-start.2
  377.1 10.7 copy-start.1
  393.1 2.4 copy-start.4
  393.1 2.4 copy-start.7
  397.4 25.0 %copy-start.5 = (bf16[256,512]{1,0:T(8,128)(2,1)S(1)}, bf16[256,512]{1,0:T(8,128)(2,1)}, u32[]{:S(2)}) copy-start(bf16[256,512]{1,0:T(8,128)(2,1)} %param.20) | copy-start | bytes 786436
  399.1 43.6 %copy-start.15 = (f32[2048]{0:T(1024)S(1)}, f32[2048]{0:T(1024)}, u32[]{:S(2)}) copy-start(f32[2048]{0:T(1024)} %param.22) | copy-start | bytes 24580
  399.1 42.0 %all-gather.10.cloned.1.call-start = ((), (), s32[]{:S(2)}) async-start(), calls=%async_computation.5 | async-start | bytes 1310720 | tf_op jit(solution)/shard_map/all_gather | solution.py:154
  424.1 63.4 %reduce-scatter.5.cloned.1.call-start = ((), (), s32[]{:S(2)}) async-start(), calls=%async_computation.6 | async-start | bytes 1310720 | tf_op jit(solution)/shard_map/reduce_scatter | solution.py:161
  442.7 7.5 copy-start.8
  450.2 37.2 %copy-start.3 = (bf16[256,512]{1,0:T(8,128)(2,1)S(1)}, bf16[256,512]{1,0:T(8,128)(2,1)}, u32[]{:S(2)}) copy-start(bf16[256,512]{1,0:T(8,128)(2,1)} %add_convert_fusion.1) | copy-start | bytes 786436
  462.4 43.8 %all-gather.12.cloned.1.call-start = ((), (), s32[]{:S(2)}) async-start(), calls=%async_computation.7 | async-start | bytes 1310720 | tf_op jit(solution)/shard_map/all_gather | solution.py:165
  489.2 0.8 copy-start.10
  489.2 1285.5 %copy-start.16 = (f32[2048]{0:T(1024)S(1)}, f32[2048]{0:T(1024)}, u32[]{:S(2)}) copy-start(f32[2048]{0:T(1024)} %param.23) | copy-start | bytes 24580
  489.2 1285.5 %all-gather.14.cloned.1.call-start = ((), (), s32[]{:S(2)}) async-start(), calls=%async_computation.8 | async-start | bytes 75497472 | tf_op jit(solution)/shard_map/all_gather | solution.py:170
Sparse Core Ops, SparseCore 0:
  9.6 19.4 all-gather.7
  31.2 124.9 all-gather.5
  399.3 23.0 reduce-scatter.2
  424.4 16.7 all-gather.9
  462.5 24.8 reduce-scatter.4
  489.4 16.7 all-gather.11
  507.7 1266.9 all-gather.13
where the time goes:
time: 1840 us; the launch traced here: 1830 us
  waiting for transfers between devices  1490 us (81%)
  matrix products  168 us (9%)
  other arithmetic  86.4 us (5%)
  local copies, waits for them, and re-layouts  47.9 us (3%)
    all_gather x1, waiting for transfers between devices, body(): lax.all_gather(w_head, 'req', axis=0, tiled=True)  1270 us
    all_gather x1, waiting for transfers between devices, body(): piece = lax.all_gather(prefix_kv, 'req', axis=0, tiled=True)  117 us
    dot_general x9, matrix products, absorb(): jnp.einsum('kqd,knd->kqn', queries, keys, preferred_element_type=jnp.floa...  67.7 us
    reduce_sum x9, other arithmetic, absorb(): total = total * keep + jnp.sum(weights, axis=-1)  66.8 us
    dot_general x9, matrix products, absorb(): jnp.einsum('kqn,knd->kqd', weights.astype(jnp.bfloat16), values, preferre...  43.1 us
  transfers between devices with their start and end apart: 7, of which 7 were waited for; matrix products, arithmetic and copies ran while one was open for 1% of the time, Pallas kernels for 0%

commit v1 on v0

v1 whole, which is shorter than its diff:
```python
import functools
import math

import jax
import jax.numpy as jnp
from jax import lax
from jax.experimental import pallas as pl
from jax.experimental.pallas import tpu as pltpu
from jax.sharding import PartitionSpec as P

TENANTS = 4
PLEN = 4096

EPS = 1e-05
LOG_THETA = math.log(1000000.0)
NEG = -1e30
BF = jnp.bfloat16
F32 = jnp.float32
LANES = 128
BLOCK = 64
KEYS = 1024
MIB = 1 << 20


def params(mib, **more):
    return pltpu.CompilerParams(vmem_limit_bytes=mib * MIB, **more)


def swap(values, axis, bit):
    size = lax.axis_size(axis)
    return lax.ppermute(values, axis, [(i, i ^ bit) for i in range(size)])


def after(values, *events):
    return lax.optimization_barrier((values, *events))[0]


def bits_of(size):
    found = []
    while size > 1:
        size //= 2
        found.append(size)
    return found


def row_layout(lengths, tenants, count):
    ends = jnp.cumsum(lengths)
    row_ids = jnp.arange(count, dtype=jnp.int32)
    request = jnp.sum((row_ids[:, None] >= ends[None, :]).astype(jnp.int32), axis=1)
    onehot = (request[:, None] == jnp.arange(lengths.shape[0], dtype=jnp.int32)[None, :]).astype(
        jnp.int32
    )
    starts = ends - lengths
    offset = row_ids - jnp.sum(onehot * starts[None, :], axis=1)
    tenant = jnp.sum(onehot * tenants[None, :], axis=1)
    return (request, offset, tenant)


def rope_tables(position, size):
    half = size // 2
    freq = jnp.exp(jnp.arange(half, dtype=jnp.float32) * (-2.0 * LOG_THETA / size))
    angle = position[:, None] * freq[None, :]
    cosine, sine = jnp.cos(angle), jnp.sin(angle)
    wide = LANES // size
    return (
        jnp.tile(jnp.concatenate([cosine, cosine], axis=1), (1, wide)),
        jnp.tile(jnp.concatenate([-sine, sine], axis=1), (1, wide)),
    )


def lane_ids(shape):
    return lax.broadcasted_iota(jnp.int32, shape, len(shape) - 1)


def qkv_kernel(place, *refs, width, pieces, scale):
    stream = refs[:pieces]
    gain, wq, wkv, cosine, sine, q_gain, k_gain, q_out, key_out, value_out = refs[pieces:]
    me = place[0]
    model = width * pieces
    loaded = [part[...].astype(F32) for part in stream]
    squares = sum(jnp.sum(part * part, axis=-1, keepdims=True) for part in loaded)
    factor = lax.rsqrt(squares / model + EPS)
    query = None
    keyval = None
    for j in range(pieces):
        quarter = me ^ j
        normed = (loaded[j] * factor * gain[pl.ds(quarter, 1), :]).astype(BF)
        rows = pl.ds(pl.multiple_of(quarter * width, width), width)
        q_part = jnp.dot(normed, wq[rows, :], preferred_element_type=F32)
        kv_part = jnp.dot(normed, wkv[rows, :], preferred_element_type=F32)
        query = q_part if query is None else query + q_part
        keyval = kv_part if keyval is None else keyval + kv_part
    lane = lane_ids((query.shape[0], LANES))
    low = lane < 64
    first = (lane % 64) < 32
    cos_t, sin_t = cosine[...], sine[...]

    def roped(tile, factor_of, head_gain):
        value = tile * factor_of * head_gain
        turned = jnp.where(
            first, pltpu.roll(value, LANES - 32, 1), pltpu.roll(value, 32, 1)
        )
        return value * cos_t + turned * sin_t

    for t in range(query.shape[1] // LANES):
        tile = query[:, t * LANES : (t + 1) * LANES]
        square = tile * tile
        one = jnp.sum(jnp.where(low, square, 0.0), axis=-1, keepdims=True)
        two = jnp.sum(jnp.where(low, 0.0, square), axis=-1, keepdims=True)
        factor_of = lax.rsqrt(jnp.where(low, one, two) / 64.0 + EPS)
        result = roped(tile, factor_of, q_gain[...]).astype(BF)
        q_out[:, t * LANES : (t + 1) * LANES] = (result.astype(F32) * scale).astype(BF)
    heads = keyval.shape[1] // LANES
    keys, values = [], []
    for t in range(heads):
        tile = keyval[:, t * LANES : (t + 1) * LANES]
        one = jnp.sum(jnp.where(low, tile * tile, 0.0), axis=-1, keepdims=True)
        factor_of = lax.rsqrt(one / 64.0 + EPS)
        keys.append(roped(tile, factor_of, k_gain[...]))
        values.append(tile)
    for t in range(0, heads, 2):
        wide = slice(t * 64, min(t + 2, heads) * 64)
        key, value = keys[t], pltpu.roll(values[t], 64, 1)
        if t + 1 < heads:
            key = jnp.where(low, key, pltpu.roll(keys[t + 1], 64, 1))
            value = jnp.where(low, value, values[t + 1])
        count = wide.stop - wide.start
        key_out[:, wide] = key[:, :count].astype(BF)
        value_out[wide, :] = jnp.transpose(value)[:count].astype(BF)


def qkv_call(place, stream, gain, wq, wkv, cosine, sine, q_gain, k_gain):
    pieces = len(stream)
    rows, width = stream[0].shape
    head = q_gain.shape[0]
    twice = LANES // head
    kernel = functools.partial(qkv_kernel, width=width, pieces=pieces, scale=head**-0.5)
    whole = pl.BlockSpec(memory_space=pltpu.VMEM)
    return pl.pallas_call(
        kernel,
        out_shape=(
            jax.ShapeDtypeStruct((rows, wq.shape[1]), BF),
            jax.ShapeDtypeStruct((rows, wkv.shape[1] // 2), BF),
            jax.ShapeDtypeStruct((wkv.shape[1] // 2, rows), BF),
        ),
        in_specs=[pl.BlockSpec(memory_space=pltpu.SMEM)] + [whole] * (pieces + 7),
        out_specs=(whole, whole, whole),
        compiler_params=params(24),
        cost_estimate=pl.CostEstimate(
            flops=2 * rows * width * pieces * (wq.shape[1] + wkv.shape[1]),
            bytes_accessed=2 * (wq.size + wkv.size + rows * width * pieces),
            transcendentals=0,
        ),
        name="qkv",
    )(
        place,
        *stream,
        gain.reshape(pieces, width),
        wq,
        wkv,
        cosine,
        sine,
        jnp.tile(q_gain, twice).reshape(1, LANES),
        jnp.tile(k_gain, twice).reshape(1, LANES),
    )


def split_kernel(kv, key_out, value_out, *, heads):
    low = lane_ids((kv.shape[0], LANES)) < 64
    for t in range(0, heads, 2):
        wide = slice(t * 64, min(t + 2, heads) * 64)
        count = wide.stop - wide.start
        first = kv[:, t * LANES : (t + 1) * LANES].astype(F32)
        key, value = first, pltpu.roll(first, 64, 1)
        if t + 1 < heads:
            second = kv[:, (t + 1) * LANES : (t + 2) * LANES].astype(F32)
            key = jnp.where(low, key, pltpu.roll(second, 64, 1))
            value = jnp.where(low, value, second)
        key_out[:, wide] = key[:, :count].astype(BF)
        value_out[wide, :] = jnp.transpose(value)[:count].astype(BF)


def split_call(kv):
    slab, wide = kv.shape
    rows = 256
    return pl.pallas_call(
        functools.partial(split_kernel, heads=wide // LANES),
        out_shape=(
            jax.ShapeDtypeStruct((slab, wide // 2), BF),
            jax.ShapeDtypeStruct((wide // 2, slab), BF),
        ),
        grid=(slab // rows,),
        in_specs=[pl.BlockSpec((rows, wide), lambda i: (i, 0))],
        out_specs=(
            pl.BlockSpec((rows, wide // 2), lambda i: (i, 0)),
            pl.BlockSpec((wide // 2, rows), lambda i: (0, i)),
        ),
        compiler_params=params(16),
        cost_estimate=pl.CostEstimate(flops=0, bytes_accessed=4 * kv.size, transcendentals=0),
        name="split",
    )(kv)


def attention_kernel(flags, owners, *refs, pieces, heads, group, own, slab):
    q_ref, tenant_ref, kv_refs, rest = refs[0], refs[1], refs[2 : 2 + 2 * pieces], refs[2 + 2 * pieces :]
    if own:
        own_key, own_value, begin_ref = rest[:3]
        rest = rest[3:]
    out, lse_out, qp, best, total, accum = rest
    block = pl.program_id(0)
    count = heads * group
    wide = heads * 64
    low = lane_ids((BLOCK, LANES)) < 64

    for i in range(count):
        tile = q_ref[:, (i // 2) * LANES : (i // 2 + 1) * LANES].astype(F32)
        place = (i // group) % 2
        if i % 2 != place:
            tile = pltpu.roll(tile, 64, 1)
        tile = jnp.where(low if place == 0 else ~low, tile, 0.0).astype(BF)
        rows = slice(i * BLOCK, (i + 1) * BLOCK)
        for t in range(0, wide, LANES):
            here = min(LANES, wide - t)
            mine = t // LANES == i // group // 2
            qp[rows, t : t + here] = tile[:, :here] if mine else jnp.zeros((BLOCK, here), BF)

    tenants = tenant_ref[0]

    def attend(keys, values, span, mask=None):
        found = None
        for c in range(0, span, min(KEYS, span)):
            part = slice(c, c + min(KEYS, span))
            score = lax.dot_general(
                keys[part, :], qp[...], (((1,), (1,)), ((), ())), preferred_element_type=F32
            )
            if mask is not None:
                score = jnp.where(mask, score, NEG)
            top = jnp.max(score, axis=0, keepdims=True)
            if found is not None:
                top = jnp.maximum(top, found[0])
            weight = jnp.exp(score - top)
            if mask is not None:
                weight = jnp.where(mask, weight, 0.0)
            summed = jnp.sum(weight, axis=0, keepdims=True)
            value = jnp.dot(values[:, part], weight.astype(BF), preferred_element_type=F32)
            if found is not None:
                keep = jnp.exp(found[0] - top)
                summed = found[1] * keep + summed
                value = found[2] * keep + value
            found = (top, summed, value)
        return found

    if own:
        span = own_key.shape[0]
        key_id = lax.broadcasted_iota(jnp.int32, (span, count * BLOCK), 0)
        row_id = block * BLOCK + lane_ids((1, count * BLOCK)) % BLOCK
        seen = (key_id <= row_id) & (key_id >= begin_ref[0])
        best[...], total[...], accum[...] = attend(own_key, own_value, span, seen)
    else:
        best[...] = jnp.full(best.shape, NEG, F32)
        total[...] = jnp.zeros(total.shape, F32)
        accum[...] = jnp.zeros(accum.shape, F32)

    for j in range(pieces):

        @pl.when(flags[block, j] > 0)
        def _(j=j):
            top, summed, value = attend(kv_refs[2 * j], kv_refs[2 * j + 1], slab)
            ok = tenants == owners[j]
            old = best[...]
            new = jnp.where(ok, jnp.maximum(old, top), old)
            keep = jnp.where(ok, jnp.exp(old - new), 1.0)
            add = jnp.where(ok, jnp.exp(jnp.where(ok, top - new, 0.0)), 0.0)
            best[...] = new
            total[...] = total[...] * keep + summed * add
            accum[...] = accum[...] * keep + value * add

    row_total = total[...]
    some = row_total > 0.0
    safe = jnp.where(some, row_total, 1.0)
    lse = jnp.where(some, best[...] + jnp.log(safe), NEG)
    inverse = 1.0 / safe
    lane = lane_ids((1, count * BLOCK))
    result = accum[:64, :]
    for h in range(1, heads):
        result = jnp.where(lane < h * group * BLOCK, result, accum[h * 64 : (h + 1) * 64, :])
    result = result * inverse
    if own:
        out[0] = result
        lse_out[0] = lse
    else:
        high = lse.astype(BF).astype(F32)
        middle = (lse - high).astype(BF).astype(F32)
        last = (lse - high - middle).astype(BF).astype(F32)
        line = lax.broadcasted_iota(jnp.int32, (16, count * BLOCK), 0)
        packed = jnp.where(
            line == 0, high, jnp.where(line == 1, middle, jnp.where(line == 2, last, 0.0))
        )
        out[0, :64, :] = result.astype(BF)
        out[0, 64:, :] = packed.astype(BF)
        lse_out[0] = lse


def attention_call(query, tenant, flags, owners, pieces, own_part):
    rows, width = query.shape
    slab, wide = pieces[0][0].shape
    own = own_part is not None
    heads = wide // 64
    group = width // 64 // heads
    stack = heads * group * BLOCK
    blocks = rows // BLOCK
    full = lambda array: pl.BlockSpec(array.shape, lambda b, *_: (0, 0))
    lanes = pl.BlockSpec((1, 1, stack), lambda b, *_: (b, 0, 0))
    operands = [query, tenant] + [array for piece in pieces for array in piece]
    in_specs = [pl.BlockSpec((BLOCK, width), lambda b, *_: (b, 0)), lanes]
    in_specs += [full(array) for piece in pieces for array in piece]
    if own:
        own_key, own_value, begin = own_part
        operands += [own_key, own_value, begin]
        in_specs += [full(own_key), full(own_value), lanes]
    depth = 64 if own else 80
    kernel = functools.partial(
        attention_kernel, pieces=len(pieces), heads=heads, group=group, own=own, slab=slab
    )
    return pl.pallas_call(
        kernel,
        out_shape=(
            jax.ShapeDtypeStruct((blocks, depth, stack), F32 if own else BF),
            jax.ShapeDtypeStruct((blocks, 1, stack), F32),
        ),
        grid_spec=pltpu.PrefetchScalarGridSpec(
            num_scalar_prefetch=2,
            grid=(blocks,),
            in_specs=in_specs,
            out_specs=(pl.BlockSpec((1, depth, stack), lambda b, *_: (b, 0, 0)), lanes),
            scratch_shapes=[
                pltpu.VMEM((stack, wide), BF),
                pltpu.VMEM((1, stack), F32),
                pltpu.VMEM((1, stack), F32),
                pltpu.VMEM((wide, stack), F32),
            ],
        ),
        compiler_params=params(40),
        cost_estimate=pl.CostEstimate(
            flops=4 * rows * group * slab * wide * 4,
            bytes_accessed=4 * slab * wide * len(pieces),
            transcendentals=rows * group * heads * slab,
        ),
        name="attention_own" if own else "attention_partner",
    )(flags, owners, *operands)


def project_kernel(
    place, one, lse_one, two, w_out, kept, sent, attended, *, count, width, pieces
):
    me = place[0]
    for b in range(one.shape[0]):
        first = lse_one[b]
        extra = two[b, 64:, :].astype(F32)
        second = extra[0:1] + extra[1:2] + extra[2:3]
        share_one = 1.0 / (1.0 + jnp.exp(second - first))
        share_two = 1.0 / (1.0 + jnp.exp(first - second))
        merged = one[b] * share_one + two[b, :64, :].astype(F32) * share_two
        rows = jnp.transpose(jnp.concatenate([merged, jnp.zeros_like(merged)], axis=0))
        for t in range(count // 2):
            left = rows[2 * t * BLOCK : (2 * t + 1) * BLOCK]
            right = rows[(2 * t + 1) * BLOCK : (2 * t + 2) * BLOCK]
            attended[b * BLOCK : (b + 1) * BLOCK, t * LANES : (t + 1) * LANES] = (
                left + pltpu.roll(right, 64, 1)
            ).astype(BF)
    for j in range(pieces):
        columns = pl.ds(pl.multiple_of((me ^ j) * width, width), width)
        part = jnp.dot(attended[...], w_out[:, columns], preferred_element_type=F32)
        (sent if j % 2 else kept)[j // 2] = part.astype(BF)


def project_call(place, one, lse_one, two, w_out, pieces):
    rows = one.shape[0] * BLOCK
    model = w_out.shape[1]
    width = model // pieces
    whole = pl.BlockSpec(memory_space=pltpu.VMEM)
    half = jax.ShapeDtypeStruct((pieces // 2, rows, width), BF)
    kernel = functools.partial(
        project_kernel, count=w_out.shape[0] // 64, width=width, pieces=pieces
    )
    return pl.pallas_call(
        kernel,
        out_shape=(half, half),
        in_specs=[pl.BlockSpec(memory_space=pltpu.SMEM)] + [whole] * 4,
        out_specs=(whole, whole),
        scratch_shapes=[pltpu.VMEM((rows, w_out.shape[0]), BF)],
        compiler_params=params(24),
        cost_estimate=pl.CostEstimate(
            flops=2 * rows * w_out.size, bytes_accessed=2 * w_out.size, transcendentals=0
        ),
        name="project",
    )(place, one, lse_one, two, w_out)


def swiglu_kernel(
    place, ours, theirs, gain, w_gate, w_up, w_down, kept, sent, normed, accum, *, pieces, width
):
    step = pl.program_id(0)
    me = place[0]

    @pl.when(step == 0)
    def _():
        loaded = [
            (theirs if j % 2 else ours)[j // 2].astype(F32) for j in range(pieces)
        ]
        squares = sum(jnp.sum(part * part, axis=-1, keepdims=True) for part in loaded)
        factor = lax.rsqrt(squares / (pieces * width) + EPS)
        for j in range(pieces):
            quarter = me ^ j
            columns = pl.ds(pl.multiple_of(quarter * width, width), width)
            normed[:, columns] = (loaded[j] * factor * gain[pl.ds(quarter, 1), :]).astype(BF)
        accum[...] = jnp.zeros_like(accum)

    gate = jnp.dot(normed[...], w_gate[...], preferred_element_type=F32)
    upper = jnp.dot(normed[...], w_up[...], preferred_element_type=F32)
    inner = (gate / (1.0 + jnp.exp(-gate)) * upper).astype(BF)
    accum[...] += jnp.dot(inner, w_down[...], preferred_element_type=F32)

    @pl.when(step == pl.num_programs(0) - 1)
    def _():
        for j in range(pieces):
            columns = pl.ds(pl.multiple_of((me ^ j) * width, width), width)
            (sent if j % 2 else kept)[j // 2] = accum[:, columns].astype(BF)


def swiglu_call(place, ours, theirs, gain, w_gate, w_up, w_down):
    half_pieces, rows, width = ours.shape
    pieces = 2 * half_pieces
    model, units = w_gate.shape
    tile = 256
    whole = pl.BlockSpec((half_pieces, rows, width), lambda s, *_: (0, 0, 0))
    half = jax.ShapeDtypeStruct((half_pieces, rows, width), BF)
    kernel = functools.partial(swiglu_kernel, pieces=pieces, width=width)
    return pl.pallas_call(
        kernel,
        out_shape=(half, half),
        grid_spec=pltpu.PrefetchScalarGridSpec(
            num_scalar_prefetch=1,
            grid=(units // tile,),
            in_specs=[
                whole,
                whole,
                pl.BlockSpec((pieces, width), lambda s, *_: (0, 0)),
                pl.BlockSpec((model, tile), lambda s, *_: (0, s)),
                pl.BlockSpec((model, tile), lambda s, *_: (0, s)),
                pl.BlockSpec((tile, model), lambda s, *_: (s, 0)),
            ],
            out_specs=(whole, whole),
            scratch_shapes=[
                pltpu.VMEM((rows, model), BF),
                pltpu.VMEM((rows, model), F32),
            ],
        ),
        compiler_params=params(40),
        cost_estimate=pl.CostEstimate(
            flops=6 * rows * model * units,
            bytes_accessed=6 * model * units,
            transcendentals=rows * units,
        ),
        name="swiglu",
    )(place, ours, theirs, gain.reshape(pieces, width), w_gate, w_up, w_down)


def head_kernel(place, *refs, depth, offset, span, width, pieces, blocks, cuts, step_cols):
    quads = refs[:4]
    gain, targets = refs[4:6]
    count = blocks * cuts
    w_refs = refs[6 : 6 + count]
    out, w_full, normed, sems = refs[6 + count :]
    me_req, me_mlp = place[1], place[0]
    step = pl.program_id(0)
    columns_here = w_full.shape[1]
    cut = columns_here // cuts

    @pl.when(step == 0)
    def _():
        copies = [
            pltpu.make_async_copy(
                w_refs[n].at[:depth, :],
                w_full.at[
                    pl.ds(pl.multiple_of((me_req ^ (n % blocks)) * depth, depth), depth),
                    pl.ds(n // blocks * cut, cut),
                ],
                sems.at[n],
            )
            for n in range(count)
        ]
        for copy in copies:
            copy.start()
        for copy in copies:
            copy.wait()

    rows_half = quads[0].shape[-2]
    for part in range(2):
        own_ref, other_ref = quads[2 * part], quads[2 * part + 1]
        loaded = []
        for j in range(pieces):
            source = (other_ref if j % 2 else own_ref)[...].reshape(
                pieces // 2, rows_half, width
            )
            loaded.append(source[j // 2].astype(F32))
        squares = sum(jnp.sum(value * value, axis=-1, keepdims=True) for value in loaded)
        factor = lax.rsqrt(squares / (pieces * width) + EPS)
        for j in range(pieces):
            quarter = me_mlp ^ j
            where = pl.ds(pl.multiple_of(quarter * width, width), width)
            normed[part * rows_half : (part + 1) * rows_half, where] = (
                loaded[j] * factor * gain[pl.ds(quarter, 1), :]
            ).astype(BF)

    rows = 2 * rows_half
    lane = lane_ids((rows, LANES))
    base = me_mlp * (span * blocks) + me_req * span + offset
    wanted = targets[...] - base
    best = jnp.full((rows, LANES), NEG, F32)
    total = jnp.zeros((rows, LANES), F32)
    picked = jnp.zeros((rows, LANES), F32)
    for c in range(columns_here // step_cols):
        logits = jnp.dot(
            normed[...],
            w_full[:, c * step_cols : (c + 1) * step_cols],
            preferred_element_type=F32,
        )
        tiles = [logits[:, t * LANES : (t + 1) * LANES] for t in range(step_cols // LANES)]
        new = functools.reduce(jnp.maximum, tiles, best)
        total = total * jnp.exp(best - new)
        for t, tile in enumerate(tiles):
            total = total + jnp.exp(tile - new)
            hit = lane == wanted - (c * step_cols + t * LANES)
            picked = picked + jnp.where(hit, tile, 0.0)
        best = new
    top = jnp.max(best, axis=-1, keepdims=True)
    summed = jnp.sum(total * jnp.exp(best - top), axis=-1, keepdims=True)
    chosen = jnp.sum(picked, axis=-1, keepdims=True)
    joined = jnp.where(lane == 0, top, jnp.where(lane == 1, summed, chosen))
    out[...] = jnp.transpose(joined)[:8][None]


def head_call(place, quads, gain, targets, w_parts, depth, offset, span):
    blocks = len(w_parts[0])
    cut = w_parts[0][0].shape[1]
    columns = cut * len(w_parts)
    half_rows, width = quads[0][0].shape[-2:]
    model = depth * blocks
    pieces = model // width
    rows = 2 * half_rows

    def spec(order):
        def index(s, place_ref):
            where = {"y": s % 2, "z": s // 2, "x": 0}
            return tuple(where[name] for name in order) + (0, 0)

        shape = tuple(pieces // 2 if name == "x" else 1 for name in order)
        return pl.BlockSpec(shape + (half_rows, width), index)

    step_cols = min(512, columns)
    kernel = functools.partial(
        head_kernel,
        depth=depth,
        offset=offset,
        span=span,
        width=width,
        pieces=pieces,
        blocks=blocks,
        cuts=len(w_parts),
        step_cols=step_cols,
    )
    return pl.pallas_call(
        kernel,
        out_shape=jax.ShapeDtypeStruct((blocks, 8, rows), F32),
        grid_spec=pltpu.PrefetchScalarGridSpec(
            num_scalar_prefetch=1,
            grid=(blocks,),
            in_specs=[spec(order) for _, order in quads]
            + [
                pl.BlockSpec((pieces, width), lambda s, place_ref: (0, 0)),
                pl.BlockSpec((rows, 1), lambda s, place_ref: (s, 0)),
            ]
            + [pl.BlockSpec(memory_space=pl.ANY)] * (blocks * len(w_parts)),
            out_specs=pl.BlockSpec((1, 8, rows), lambda s, place_ref: (s ^ place_ref[1], 0, 0)),
            scratch_shapes=[
                pltpu.VMEM((model, columns), BF),
                pltpu.VMEM((rows, model), BF),
                pltpu.SemaphoreType.DMA((blocks * len(w_parts),)),
            ],
        ),
        compiler_params=params(40),
        cost_estimate=pl.CostEstimate(
            flops=2 * rows * blocks * model * columns,
            bytes_accessed=2 * model * columns + 2 * rows * blocks * model,
            transcendentals=rows * blocks * columns,
        ),
        name="head",
    )(place, *[array for array, _ in quads], gain.reshape(pieces, width), targets, *sum(w_parts, []))


def merge_stats(one, two):
    top = jnp.maximum(one[..., 0, :], two[..., 0, :])
    total = one[..., 1, :] * jnp.exp(one[..., 0, :] - top) + two[..., 1, :] * jnp.exp(
        two[..., 0, :] - top
    )
    return jnp.stack([top, total, one[..., 2, :] + two[..., 2, :]], axis=-2)


def body(
    tokens,
    attn_gain,
    mlp_gain,
    final_gain,
    q_gain,
    k_gain,
    w_query,
    w_keyval,
    w_out,
    w_gate,
    w_up,
    w_down,
    w_head,
    targets,
    req_lengths,
    req_tenant,
    prefix_piece,
    prefix_kv,
):
    rows, width = tokens.shape
    groups = lax.axis_size("req")
    parts = lax.axis_size("mlp")
    half = groups // 2
    me_req = lax.axis_index("req")
    me_mlp = lax.axis_index("mlp")
    place = jnp.stack([me_mlp, me_req]).astype(jnp.int32)
    split_count = groups // TENANTS
    head_size = q_gain.shape[0]

    meta = jnp.concatenate([req_lengths, req_tenant], axis=1)
    meta_far = swap(meta, "req", half)
    per = req_lengths.shape[1]

    span = w_head.shape[1] // groups
    parts_of_span = 4
    cut = span // parts_of_span
    coded = jnp.concatenate([targets >> 8, targets & 255]).astype(F32).astype(BF)
    coded = coded.reshape(-1, cut)
    extra = jnp.pad(coded, ((0, 16 - coded.shape[0]), (0, 0)))

    def head_part(part, k):
        block = lax.dynamic_slice_in_dim(w_head, (me_req ^ k) * span + part * cut, cut, 1)
        return jnp.concatenate([block, extra], axis=0) if part == 0 else block

    own_parts = [head_part(part, 0) for part in range(parts_of_span)]
    out_parts = [[head_part(part, k) for k in range(1, groups)] for part in range(parts_of_span)]

    def send_part(part, event):
        blocks = after(tuple(out_parts[part]), event)
        return [own_parts[part]] + [
            swap(block, "req", k) for k, block in zip(range(1, groups), blocks)
        ]

    stream = [tokens]
    for bit in [b for b in bits_of(parts) if b > 1][::-1]:
        got = swap(jnp.concatenate(stream, axis=1), "mlp", bit)
        stream = stream + [got[:, i * width : (i + 1) * width] for i in range(len(stream))]
    got = swap(jnp.concatenate(stream, axis=1), "mlp", 1)
    stream = [
        part
        for i, mine in enumerate(stream)
        for part in (mine, got[:, i * width : (i + 1) * width])
    ]

    stream, own_parts, out_parts = lax.optimization_barrier((stream, own_parts, out_parts))

    pieces = [split_call(prefix_kv[0])]
    for k in range(1, half):
        least, most = k & -k, 1 << (k.bit_length() - 1)
        pieces.append(
            (swap(pieces[k ^ least][0], "req", least), swap(pieces[k ^ most][1], "req", most))
        )

    request, offset, tenant = row_layout(req_lengths[0], req_tenant[0], rows)
    _, _, tenant_far = row_layout(meta_far[0, :per], meta_far[0, per:], rows)
    owners = jnp.stack(
        [
            lax.dynamic_index_in_dim(prefix_piece, me_req ^ k, 0, keepdims=False)
            for k in range(half)
        ]
    ) // split_count
    blocks = rows // BLOCK
    stacked_heads = w_query.shape[1] // head_size

    def by_block(values):
        return jnp.tile(values.reshape(blocks, 1, BLOCK), (1, 1, stacked_heads))

    def flags_of(tenants):
        hit = tenants.reshape(blocks, BLOCK, 1) == owners[None, None, :]
        return jnp.max(hit.astype(jnp.int32), axis=1)

    row_ids = jnp.arange(rows, dtype=jnp.int32)
    cosine, sine = rope_tables((PLEN + offset).astype(jnp.float32), head_size)

    query, own_key, own_value = qkv_call(
        place, stream, attn_gain, w_query, w_keyval, cosine, sine, q_gain, k_gain
    )
    query_far = swap(query, "req", half)
    part_0 = send_part(0, query)
    out_far, _ = attention_call(
        query_far, by_block(tenant_far), flags_of(tenant_far), owners, pieces, None
    )
    back = swap(out_far, "req", half)
    out_near, lse_near = attention_call(
        query,
        by_block(tenant),
        flags_of(tenant),
        owners,
        pieces,
        (own_key, own_value, by_block(row_ids - offset)),
    )
    out_near, part_0 = lax.optimization_barrier((out_near, part_0))
    kept, sent = project_call(place, out_near, lse_near, back, w_out, parts)

    def over_cores(kept, sent):
        return kept.astype(F32) + swap(sent, "mlp", 1).astype(F32)

    part_1 = send_part(1, kept)
    summed = over_cores(kept, sent)
    x_bits = [b // 2 for b in bits_of(parts) if b > 1]
    for bit in x_bits:
        got = swap(summed.astype(BF), "mlp", 2 * bit)
        order = [i ^ bit for i in range(parts // 2)]
        summed = summed.astype(BF).astype(F32) + jnp.stack([got[i] for i in order]).astype(F32)
    residual = jnp.stack(stream[0::2]).astype(F32)
    mid = (residual + summed).astype(BF)
    mid_other = swap(mid, "mlp", 1)

    kept, sent = swiglu_call(place, mid, mid_other, mlp_gain, w_gate, w_up, w_down)
    summed = over_cores(kept, sent)
    for bit in x_bits:
        got = swap(summed[bit:].astype(BF), "mlp", 2 * bit)
        summed = summed[:bit] + got.astype(F32)
    out_share = (mid[0].astype(F32) + summed[0]).astype(BF)

    out_share, part_1 = lax.optimization_barrier((out_share, part_1))

    spread = out_share[None]
    for bit in [b for b in bits_of(groups) if b > 1]:
        got = swap(spread, "req", bit)
        count = spread.shape[0]
        spread = (
            jnp.stack([spread, got], axis=0) if count == 1 else jnp.stack([spread, got], axis=1)
        ).reshape(2 * count, rows, width)
    part_2 = send_part(2, spread)
    part_3 = send_part(3, spread)
    top_rows, low_rows = spread[:, : rows // 2], spread[:, rows // 2 :]

    def add_y(values, axis):
        return jnp.stack([values, swap(values, "req", 1)], axis=axis)

    def add_x(values, axis):
        values = jnp.expand_dims(values, axis)
        for bit in x_bits[::-1]:
            values = jnp.concatenate([values, swap(values, "mlp", 2 * bit)], axis=axis)
        return values

    top_rows = add_x(add_y(top_rows, 0), 0)
    low_rows = add_y(add_x(low_rows, 0), 0)
    quads = [
        (top_rows, "xyz"),
        (swap(top_rows, "mlp", 1), "xyz"),
        (low_rows, "yxz"),
        (swap(low_rows, "mlp", 1), "yxz"),
    ]

    codes = jnp.stack([block[w_head.shape[0] :].reshape(-1)[: 2 * rows] for block in part_0])
    codes = codes.astype(F32).astype(jnp.int32)
    wanted = (codes[:, :rows] * 256 + codes[:, rows:]).reshape(groups * rows, 1)
    stats = None
    for first, group_of in ((0, [part_0, part_1, part_2]), (3, [part_3])):
        found = head_call(
            place, quads, final_gain, wanted, group_of, w_head.shape[0], first * cut, span
        )[:, :3]
        stats = found if stats is None else merge_stats(stats, found)

    spread_stats = lax.all_to_all(stats, "req", 0, 0, tiled=True)
    top = jnp.max(spread_stats[:, 0], axis=0)
    total = jnp.sum(spread_stats[:, 1] * jnp.exp(spread_stats[:, 0] - top[None]), axis=0)
    stats = jnp.stack([top, total, jnp.sum(spread_stats[:, 2], axis=0)])
    for bit in bits_of(parts)[::-1]:
        stats = merge_stats(stats, swap(stats, "mlp", bit))
    logprob = stats[2] - stats[0] - jnp.log(stats[1])
    return (out_share, logprob)


def solution(mesh):
    in_specs = (
        P("req", "mlp"),
        P(),
        P(),
        P(),
        P(),
        P(),
        P(None, "mlp"),
        P(None, "mlp"),
        P("mlp", None),
        P(None, "mlp"),
        P(None, "mlp"),
        P("mlp", None),
        P("req", "mlp"),
        P("req"),
        P("req", None),
        P("req", None),
        P(),
        P("req", None, "mlp"),
    )
    out_specs = (P("req", "mlp"), P("req"))
    return jax.shard_map(body, mesh=mesh, in_specs=in_specs, out_specs=out_specs, check_vma=False)
```

time: 1840 us -> 425 us (0.23)
  waiting for transfers between devices: 1490 us -> 182 us
  matrix products: 168 us -> 0 us
  Pallas kernels: 0 us -> 91.3 us
  starting transfers between devices: 0.46 us -> 91.6 us
  other arithmetic: 86.4 us -> 12.3 us
  local copies, waits for them, and re-layouts: 47.9 us -> 28.3 us
    all_gather x5 -> x0, waiting for transfers between devices: 1440 us -> none  [the longest x1 1270 us: body(): lax.all_gather(w_head, 'req', axis=0, tiled=True)]
    ppermute x0 -> x54, waiting for transfers between devices: none -> 182 us  [swap(): return lax.ppermute(values, axis, [(i, i ^ bit) for i in range(size)])]
    dot_general x24 -> x0, matrix products: 168 us -> none  [the longest x9 67.7 us: absorb(): jnp.einsum('kqd,knd->kqn', queries, keys, preferred_element_type=jnp.floa...]
    ppermute x0 -> x54, starting transfers between devices: none -> 91.6 us  [swap(): return lax.ppermute(values, axis, [(i, i ^ bit) for i in range(size)])]
    pallas_call x0 -> x8, Pallas kernels: none -> 91.3 us  [the longest x2 38.5 us: head_call(): pl.pallas_call(kernel, out_shape=jax.ShapeDtypeStruct((blocks, 8, rows),...]
    reduce_sum x14 -> x2, other arithmetic: 80.2 us -> 0.11 us  [the longest x1 0.09 us: row_layout(): offset = row_ids - jnp.sum(onehot * starts[None, :], axis=1)]
    reduce_scatter x2 -> x0, waiting for transfers between devices: 48.2 us -> none  [the longest x1 25 us: body(): lax.psum_scatter(down.astype(jnp.bfloat16), 'mlp', scatter_dimension=1, t...]
    while x40 -> x0, local copies, waits for them, and re-layouts: 20.5 us -> none
  transfers between devices with their start and end apart: 7 -> 54, of which waited for: 7 -> 28; matrix products, arithmetic and copies ran while one was open for 1% -> 6% of each run, Pallas kernels for 0% -> 11%
where the time goes in v1:
time: 425 us; the launch traced here: 424 us
  waiting for transfers between devices  182 us (43%)
  starting transfers between devices  91.6 us (22%)
  Pallas kernels  91.3 us (21%)
  local copies, waits for them, and re-layouts  28.3 us (7%)
  blocking collectives  16.8 us (4%)
  other arithmetic  12.3 us (3%)
    ppermute x54, waiting for transfers between devices, swap(): return lax.ppermute(values, axis, [(i, i ^ bit) for i in range(size)])  182 us
    ppermute x54, starting transfers between devices, swap(): return lax.ppermute(values, axis, [(i, i ^ bit) for i in range(size)])  91.6 us
    pallas_call x2, Pallas kernels, head_call(): pl.pallas_call(kernel, out_shape=jax.ShapeDtypeStruct((blocks, 8, rows),...  38.5 us
    pallas_call x2, Pallas kernels, attention_call(): pl.pallas_call(kernel, out_shape=(jax.ShapeDtypeStruct((blocks, depth, st...  30 us
    all_to_all x1, blocking collectives, body(): spread_stats = lax.all_to_all(stats, 'req', 0, 0, tiled=True)  16.8 us
    pallas_call x1, Pallas kernels, swiglu_call(): pl.pallas_call(kernel, out_shape=(half, half), grid_spec=pltpu.PrefetchSc...  14.2 us
    unnamed x122, local copies, waits for them, and re-layouts  14.1 us
  transfers between devices with their start and end apart: 54, of which 28 were waited for; matrix products, arithmetic and copies ran while one was open for 6% of the time, Pallas kernels for 11%

profile of v1, /device:TPU:0, one launch (start us, length us, event | category | flops | bytes accessed | tf_op | source)
XLA Modules:
  0.0 424.1 jit_solution(683796065238779839)
XLA Ops:
  1.9 3.5 split.1
  5.3 3.0 collective-permute-start.4
  8.4 1.5 collective-permute-start.2
  11.1 3.0 collective-permute-start.15
  20.1 3.5 constant_dynamic-slice_fusion.1
  25.9 2.2 constant_dynamic-slice_fusion
  28.1 3.1 collective-permute-done.15
  31.1 1.5 collective-permute-start
  33.0 5.2 %collective-permute-done.refs_2_ = bf16[256,512]{1,0:T(8,128)(2,1)S(1)} collective-permute-done((bf16[256,512]{1,0:T(8,128)(2,1)S(1)}, bf16[256,512]{1,0:T(8,128)(2,1)S(1)}, u32[]{:S(2)}, u32[]{:S(2)}) %collective-permute-start) | collective-permute-done | bytes 262176 | tf_op jit(solution)/shard_map/ppermute | solution.py:31
  39.6 1.6 collective-permute-start.6
  41.2 3.1 collective-permute-start.7
  46.6 3.4 qkv.1
  50.1 2.7 and_select_fusion.owners
  53.7 1.6 collective-permute-start.8
  56.1 2.4 collective-permute-start.10
  58.6 3.0 collective-permute-done.7.refs_9_
  62.2 3.1 collective-permute-done.16.refs_0_
  65.8 13.2 %attention_partner.1 = (bf16[4,80,512]{2,1,0:T(8,128)(2,1)S(1)}, f32[4,1,512]{2,1,0:T(1,128)}) custom-call(s32[4,4]{1,0:T(4,128)S(1)} %get-tuple-element.194.flags, s32[4]{0:T(128)S(1)} %and_select_fusion.owners, bf16[256,512]{1,0:T(8,128)(2,1)S(1)} %collective-permute-done.16.refs_0_, s32[4,1,512]{2,1,0:T(1,128)S(1)} %tile.68.refs_1_, ...), custom_call_target="tpu_custom_call" | custom-call | flops 4294967296 | bytes 4194304 | tf_op jit(solution)/shard_map/attention_partner/pallas_call | solution.py:325
  79.0 3.3 collective-permute-start.13
  82.3 10.2 %collective-permute-start.14 = (bf16[272,512]{1,0:T(8,128)(2,1)S(1)}, bf16[272,512]{1,0:T(8,128)(2,1)S(1)}, u32[]{:S(2)}, u32[]{:S(2)}) collective-permute-start(bf16[272,512]{1,0:T(8,128)(2,1)S(1)} %copy-done.45), channel_id=1, source_target_pairs={{0,28},{4,24},{8,20},{12,16},{16,12},{20,8},{24,4},{28,0},{1,29},{... | collective-permute-start | bytes 835592 | tf_op jit(solution)/shard_map/ppermute | solution.py:31
  92.5 16.8 %attention_own.1 = (f32[4,64,512]{2,1,0:T(8,128)S(1)}, f32[4,1,512]{2,1,0:T(1,128)S(1)}) custom-call(s32[4,4]{1,0:T(4,128)S(1)} %get-tuple-element.195.flags, s32[4]{0:T(128)S(1)} %and_select_fusion.owners, bf16[256,512]{1,0:T(8,128)(2,1)} %get-tuple-element.100.refs_0_, s32[4,1,512]{2,1,0:T(1,128)S(1)} %tile.63.refs_1_, ...), custom_call_target="tpu_custom_call" | custom-call | flops 4294967296 | bytes 4194304 | tf_op jit(solution)/shard_map/attention_own/pallas_call | solution.py:325
  109.4 17.4 %collective-permute-done.17.two = bf16[4,80,512]{2,1,0:T(8,128)(2,1)S(1)} collective-permute-done((bf16[4,80,512]{2,1,0:T(8,128)(2,1)S(1)}, bf16[4,80,512]{2,1,0:T(8,128)(2,1)S(1)}, u32[]{:S(2)}, u32[]{:S(2)}) %collective-permute-start.17) | collective-permute-done | bytes 327712 | tf_op jit(solution)/shard_map/ppermute | solution.py:31
  126.8 1.7 project.1
  128.5 1.9 collective-permute-done.18
  130.6 1.5 collective-permute-start.19
  132.1 12.5 %collective-permute-done.19 = bf16[2,256,512]{2,1,0:T(8,128)(2,1)S(1)} collective-permute-done((bf16[2,256,512]{2,1,0:T(8,128)(2,1)S(1)}, bf16[2,256,512]{2,1,0:T(8,128)(2,1)S(1)}, u32[]{:S(2)}, u32[]{:S(2)}) %collective-permute-start.19) | collective-permute-done | bytes 524320 | tf_op jit(solution)/shard_map/ppermute | solution.py:31
  145.0 1.9 collective-permute-done.20.theirs
  146.9 3.4 copy-done
  150.2 14.2 %swiglu.1 = (bf16[2,256,512]{2,1,0:T(8,128)(2,1)S(1)}, bf16[2,256,512]{2,1,0:T(8,128)(2,1)S(1)}) custom-call(s32[2]{0:T(128)S(1)} %pad_add_fusion.place, bf16[2,256,512]{2,1,0:T(8,128)(2,1)S(1)} %add_convert_fusion.ours, bf16[2,256,512]{2,1,0:T(8,128)(2,1)S(1)} %collective-permute-done.20.theirs, f32[4,512]{1,0:T(4,128)S(1)} %reshape.292.gain, ...), custom_call_target="tpu_custom_call" | custom-call | flops 6442450944 | bytes 25165824 | tf_op jit(solution)/shard_map/swiglu/pallas_call | solution.py:439
  166.7 1.5 collective-permute-start.22
  168.2 1.7 collective-permute-start.25
  170.8 2.5 collective-permute-done.23.refs_15_
  173.3 7.9 %collective-permute-done.24.refs_16_ = bf16[256,512]{1,0:T(8,128)(2,1)S(1)} collective-permute-done((bf16[256,512]{1,0:T(8,128)(2,1)S(1)}, bf16[256,512]{1,0:T(8,128)(2,1)S(1)}, u32[]{:S(2)}, u32[]{:S(2)}) %collective-permute-start.24) | collective-permute-done | bytes 262176 | tf_op jit(solution)/shard_map/ppermute | solution.py:31
  181.2 1.7 collective-permute-start.28
  183.0 4.0 collective-permute-start.29
  187.9 14.7 %collective-permute-done.26.refs_18_ = bf16[256,512]{1,0:T(8,128)(2,1)S(1)} collective-permute-done((bf16[256,512]{1,0:T(8,128)(2,1)S(1)}, bf16[256,512]{1,0:T(8,128)(2,1)S(1)}, u32[]{:S(2)}, u32[]{:S(2)}) %collective-permute-start.26) | collective-permute-done | bytes 262176 | tf_op jit(solution)/shard_map/ppermute | solution.py:31
  202.6 4.8 %collective-permute-done.27.refs_19_ = bf16[256,512]{1,0:T(8,128)(2,1)S(1)} collective-permute-done((bf16[256,512]{1,0:T(8,128)(2,1)S(1)}, bf16[256,512]{1,0:T(8,128)(2,1)S(1)}, u32[]{:S(2)}, u32[]{:S(2)}) %collective-permute-start.27) | collective-permute-done | bytes 262176 | tf_op jit(solution)/shard_map/ppermute | solution.py:31
  208.3 11.2 %collective-permute-start.30 = (bf16[1,256,512]{2,1,0:T(8,128)(2,1)S(1)}, bf16[1,256,512]{2,1,0:T(8,128)(2,1)S(1)}, u32[]{:S(2)}, u32[]{:S(2)}) collective-permute-start(bf16[1,256,512]{2,1,0:T(8,128)(2,1)S(1)} %bitcast.74), channel_id=1, source_target_pairs={{0,16},{4,20},{8,24},{12,28},{16,0},{20,4},{24,8},{28,12},{1,17},{... | collective-permute-start | bytes 786440 | tf_op jit(solution)/shard_map/ppermute | solution.py:31
  219.5 11.2 %collective-permute-done.30 = bf16[1,256,512]{2,1,0:T(8,128)(2,1)S(1)} collective-permute-done((bf16[1,256,512]{2,1,0:T(8,128)(2,1)S(1)}, bf16[1,256,512]{2,1,0:T(8,128)(2,1)S(1)}, u32[]{:S(2)}, u32[]{:S(2)}) %collective-permute-start.30) | collective-permute-done | bytes 262176 | tf_op jit(solution)/shard_map/ppermute | solution.py:31
  230.8 12.3 %collective-permute-done.31 = bf16[2,256,512]{2,1,0:T(8,128)(2,1)S(1)} collective-permute-done((bf16[2,256,512]{2,1,0:T(8,128)(2,1)S(1)}, bf16[2,256,512]{2,1,0:T(8,128)(2,1)S(1)}, u32[]{:S(2)}, u32[]{:S(2)}) %collective-permute-start.31) | collective-permute-done | bytes 524320 | tf_op jit(solution)/shard_map/ppermute | solution.py:31
  245.4 9.6 %collective-permute-done.32 = bf16[4,128,512]{2,1,0:T(8,128)(2,1)S(1)} collective-permute-done((bf16[4,128,512]{2,1,0:T(8,128)(2,1)S(1)}, bf16[4,128,512]{2,1,0:T(8,128)(2,1)S(1)}, u32[]{:S(2)}, u32[]{:S(2)}) %collective-permute-start.32) | collective-permute-done | bytes 524320 | tf_op jit(solution)/shard_map/ppermute | solution.py:31
  256.6 1.7 collective-permute-start.36
  258.2 19.6 %collective-permute-done.33 = bf16[1,2,4,128,512]{4,3,2,1,0:T(8,128)(2,1)S(1)} collective-permute-done((bf16[1,2,4,128,512]{4,3,2,1,0:T(8,128)(2,1)S(1)}, bf16[1,2,4,128,512]{4,3,2,1,0:T(8,128)(2,1)S(1)}, u32[]{:S(2)}, u32[]{:S(2)}) %collective-permute-start.33) | collective-permute-done | bytes 1048608 | tf_op jit(solution)/shard_map/ppermute | solution.py:31
  278.2 1.5 pad_maximum_fusion.1.refs_2_
  282.0 1.7 collective-permute-start.47
  283.7 4.8 %collective-permute-done.45.refs_7_ = bf16[256,512]{1,0:T(8,128)(2,1)S(1)} collective-permute-done((bf16[256,512]{1,0:T(8,128)(2,1)S(1)}, bf16[256,512]{1,0:T(8,128)(2,1)S(1)}, u32[]{:S(2)}, u32[]{:S(2)}) %collective-permute-start.45) | collective-permute-done | bytes 262176 | tf_op jit(solution)/shard_map/ppermute | solution.py:31
  291.3 2.2 collective-permute-start.49
  293.5 4.2 collective-permute-done.47.refs_9_
  298.4 2.1 collective-permute-start.50
  303.4 13.1 %collective-permute-done.48.refs_10_ = bf16[256,512]{1,0:T(8,128)(2,1)} collective-permute-done((bf16[256,512]{1,0:T(8,128)(2,1)}, bf16[256,512]{1,0:T(8,128)(2,1)}, u32[]{:S(2)}, u32[]{:S(2)}) %collective-permute-start.48) | collective-permute-done | bytes 262176 | tf_op jit(solution)/shard_map/ppermute | solution.py:31
  316.5 2.4 collective-permute-start.51
  318.9 9.1 %collective-permute-done.49.refs_11_ = bf16[256,512]{1,0:T(8,128)(2,1)} collective-permute-done((bf16[256,512]{1,0:T(8,128)(2,1)}, bf16[256,512]{1,0:T(8,128)(2,1)}, u32[]{:S(2)}, u32[]{:S(2)}) %collective-permute-start.49) | collective-permute-done | bytes 262176 | tf_op jit(solution)/shard_map/ppermute | solution.py:31
  329.2 4.7 %collective-permute-start.39 = (bf16[256,512]{1,0:T(8,128)(2,1)}, bf16[256,512]{1,0:T(8,128)(2,1)}, u32[]{:S(2)}, u32[]{:S(2)}) collective-permute-start(bf16[256,512]{1,0:T(8,128)(2,1)} %get-tuple-element.169), channel_id=1, source_target_pairs={{0,8},{4,12},{8,0},{12,4},{16,24},{20,28},{24,16},{28,20},{1,9},{5... | collective-permute-start | bytes 786440 | tf_op jit(solution)/shard_map/ppermute | solution.py:31
  334.3 4.4 %collective-permute-start.40 = (bf16[256,512]{1,0:T(8,128)(2,1)}, bf16[256,512]{1,0:T(8,128)(2,1)S(1)}, u32[]{:S(2)}, u32[]{:S(2)}) collective-permute-start(bf16[256,512]{1,0:T(8,128)(2,1)} %get-tuple-element.170), channel_id=1, source_target_pairs={{0,12},{4,8},{8,4},{12,0},{16,28},{20,24},{24,20},{28,16},{1,13},{... | collective-permute-start | bytes 786440 | tf_op jit(solution)/shard_map/ppermute | solution.py:31
  339.6 2.7 collective-permute-start.42
  342.3 1.8 collective-permute-start.43
  344.0 2.3 collective-permute-start.44
  350.3 14.8 %head.3 = f32[8,8,256]{2,1,0:T(8,128)S(1)} custom-call(s32[2]{0:T(128)S(1)} %pad_add_fusion.place, bf16[2,2,4,128,512]{4,3,2,1,0:T(8,128)(2,1)S(1)} %pad_maximum_fusion.refs_0_, bf16[2,2,4,128,512]{4,3,2,1,0:T(8,128)(2,1)} %collective-permute-done.34.refs_1_, bf16[2,2,4,128,512]{4,3,2,1,0:T(8,128)(2,1)} %pad_maximum_fusion.1.refs_2_, ...), custom_call_target="tpu_custom_call" | custom-call | flops 4294967296 | bytes 10485760 | tf_op jit(solution)/shard_map/head/pallas_call | solution.py:573
  365.1 6.4 %collective-permute-done.41.refs_26_ = bf16[256,512]{1,0:T(8,128)(2,1)S(1)} collective-permute-done((bf16[256,512]{1,0:T(8,128)(2,1)}, bf16[256,512]{1,0:T(8,128)(2,1)S(1)}, u32[]{:S(2)}, u32[]{:S(2)}) %collective-permute-start.41) | collective-permute-done | bytes 262176 | tf_op jit(solution)/shard_map/ppermute | solution.py:31
  371.5 6.3 %collective-permute-done.42.refs_27_ = bf16[256,512]{1,0:T(8,128)(2,1)S(1)} collective-permute-done((bf16[256,512]{1,0:T(8,128)(2,1)}, bf16[256,512]{1,0:T(8,128)(2,1)S(1)}, u32[]{:S(2)}, u32[]{:S(2)}) %collective-permute-start.42) | collective-permute-done | bytes 262176 | tf_op jit(solution)/shard_map/ppermute | solution.py:31
  377.9 23.7 %head.2 = f32[8,8,256]{2,1,0:T(8,128)S(1)} custom-call(s32[2]{0:T(128)S(1)} %pad_add_fusion.place, bf16[2,2,4,128,512]{4,3,2,1,0:T(8,128)(2,1)S(1)} %pad_maximum_fusion.refs_0_, bf16[2,2,4,128,512]{4,3,2,1,0:T(8,128)(2,1)} %collective-permute-done.34.refs_1_, bf16[2,2,4,128,512]{4,3,2,1,0:T(8,128)(2,1)} %pad_maximum_fusion.1.refs_2_, ...), custom_call_target="tpu_custom_call" | custom-call | flops 12884901888 | bytes 14680064 | tf_op jit(solution)/shard_map/head/pallas_call | solution.py:573
  401.7 16.8 %all_to_all.5 = f32[8,3,256]{2,1,0:T(4,128)S(1)} all-to-all(f32[8,3,256]{2,1,0:T(4,128)S(1)} %pad_maximum_fusion.7), channel_id=1, replica_groups=mesh['req'=8,'mlp'=4] {'req'}, dimensions={0} | all-to-all | bytes 49152 | tf_op jit(solution)/shard_map/all_to_all | solution.py:787
  419.9 1.5 collective-permute-start.53
  421.4 2.2 collective-permute-done.53
  (252 shorter events, 43.9 us)
Async XLA Ops:
  5.3 34.3 %collective-permute-start.4 = (bf16[2048,128]{1,0:T(8,128)(2,1)}, bf16[2048,128]{1,0:T(8,128)(2,1)}, u32[]{:S(2)}, u32[]{:S(2)}) collective-permute-start(bf16[2048,128]{1,0:T(8,128)(2,1)} %get-tuple-element.101.refs_2_), channel_id=1, source_target_pairs={{0,8},{4,12},{8,0},{12,4},{16,24},{20,28},{24,16},{28,20},{1,9},{5... | collective-permute-start | bytes 1572872 | tf_op jit(solution)/shard_map/ppermute | solution.py:31
  8.4 45.3 %collective-permute-start.2 = (bf16[2048,128]{1,0:T(8,128)(2,1)}, bf16[2048,128]{1,0:T(8,128)(2,1)}, u32[]{:S(2)}, u32[]{:S(2)}) collective-permute-start(bf16[2048,128]{1,0:T(8,128)(2,1)} %get-tuple-element.101.refs_2_), channel_id=1, source_target_pairs={{0,4},{4,0},{8,12},{12,8},{16,20},{20,16},{24,28},{28,24},{1,5},{5... | collective-permute-start | bytes 1572872 | tf_op jit(solution)/shard_map/ppermute | solution.py:31
  9.9 45.4 %collective-permute-start.5 = (bf16[128,2048]{1,0:T(8,128)(2,1)}, bf16[128,2048]{1,0:T(8,128)(2,1)}, u32[]{:S(2)}, u32[]{:S(2)}) collective-permute-start(bf16[128,2048]{1,0:T(8,128)(2,1)} %get-tuple-element.102.refs_3_), channel_id=1, source_target_pairs={{0,8},{4,12},{8,0},{12,4},{16,24},{20,28},{24,16},{28,20},{1,9},{5... | collective-permute-start | bytes 1572872 | tf_op jit(solution)/shard_map/ppermute | solution.py:31
  10.3 30.9 %collective-permute-start.3 = (bf16[128,2048]{1,0:T(8,128)(2,1)}, bf16[128,2048]{1,0:T(8,128)(2,1)}, u32[]{:S(2)}, u32[]{:S(2)}) collective-permute-start(bf16[128,2048]{1,0:T(8,128)(2,1)} %get-tuple-element.102.refs_3_), channel_id=1, source_target_pairs={{0,4},{4,0},{8,12},{12,8},{16,20},{20,16},{24,28},{28,24},{1,5},{5... | collective-permute-start | bytes 1572872 | tf_op jit(solution)/shard_map/ppermute | solution.py:31
  11.1 20.0 %collective-permute-start.15 = (s32[1,8]{1,0:T(1,128)S(1)}, s32[1,8]{1,0:T(1,128)S(1)}, u32[]{:S(2)}, u32[]{:S(2)}) collective-permute-start(s32[1,8]{1,0:T(1,128)S(1)} %pad_add_fusion.2), channel_id=1, source_target_pairs={{0,16},{4,20},{8,24},{12,28},{16,0},{20,4},{24,8},{28,12},{1,17},{... | collective-permute-start | bytes 104 | tf_op jit(solution)/shard_map/ppermute | solution.py:31
  31.1 7.2 %collective-permute-start = (bf16[256,512]{1,0:T(8,128)(2,1)S(1)}, bf16[256,512]{1,0:T(8,128)(2,1)S(1)}, u32[]{:S(2)}, u32[]{:S(2)}) collective-permute-start(bf16[256,512]{1,0:T(8,128)(2,1)S(1)} %copy-done.1), channel_id=1, source_target_pairs={{0,2},{1,3},{2,0},{3,1},{4,6},{5,7},{6,4},{7,5},{8,10},{9,11},{10,... | collective-permute-start | bytes 786440 | tf_op jit(solution)/shard_map/ppermute | solution.py:31
  39.1 5.1 %collective-permute-start.1 = (bf16[256,1024]{1,0:T(8,128)(2,1)}, bf16[256,1024]{1,0:T(8,128)(2,1)}, u32[]{:S(2)}, u32[]{:S(2)}) collective-permute-start(bf16[256,1024]{1,0:T(8,128)(2,1)} %pad_maximum_fusion.4), channel_id=1, source_target_pairs={{0,1},{1,0},{2,3},{3,2},{4,5},{5,4},{6,7},{7,6},{8,9},{9,8},{10,11... | collective-permute-start | bytes 1572872 | tf_op jit(solution)/shard_map/ppermute | solution.py:31
  39.6 16.5 %collective-permute-start.6 = (bf16[2048,128]{1,0:T(8,128)(2,1)}, bf16[2048,128]{1,0:T(8,128)(2,1)}, u32[]{:S(2)}, u32[]{:S(2)}) collective-permute-start(bf16[2048,128]{1,0:T(8,128)(2,1)} %collective-permute-done.4.refs_6_), channel_id=1, source_target_pairs={{0,4},{4,0},{8,12},{12,8},{16,20},{20,16},{24,28},{28,24},{1,5},{5... | collective-permute-start | bytes 1572872 | tf_op jit(solution)/shard_map/ppermute | solution.py:31
  41.2 20.3 %collective-permute-start.7 = (bf16[128,2048]{1,0:T(8,128)(2,1)}, bf16[128,2048]{1,0:T(8,128)(2,1)}, u32[]{:S(2)}, u32[]{:S(2)}) collective-permute-start(bf16[128,2048]{1,0:T(8,128)(2,1)} %collective-permute-done.3.refs_5_), channel_id=1, source_target_pairs={{0,8},{4,12},{8,0},{12,4},{16,24},{20,28},{24,16},{28,20},{1,9},{5... | collective-permute-start | bytes 1572872 | tf_op jit(solution)/shard_map/ppermute | solution.py:31
  50.0 15.3 %collective-permute-start.16 = (bf16[256,512]{1,0:T(8,128)(2,1)}, bf16[256,512]{1,0:T(8,128)(2,1)S(1)}, u32[]{:S(2)}, u32[]{:S(2)}) collective-permute-start(bf16[256,512]{1,0:T(8,128)(2,1)} %get-tuple-element.100.refs_0_), channel_id=1, source_target_pairs={{0,16},{4,20},{8,24},{12,28},{16,0},{20,4},{24,8},{28,12},{1,17},{... | collective-permute-start | bytes 786440 | tf_op jit(solution)/shard_map/ppermute | solution.py:31
  53.7 25.3 %collective-permute-start.8 = (bf16[272,512]{1,0:T(8,128)(2,1)}, bf16[272,512]{1,0:T(8,128)(2,1)S(1)}, u32[]{:S(2)}, u32[]{:S(2)}) collective-permute-start(bf16[272,512]{1,0:T(8,128)(2,1)} %get-tuple-element.114), channel_id=1, source_target_pairs={{0,4},{4,0},{8,12},{12,8},{16,20},{20,16},{24,28},{28,24},{1,5},{5... | collective-permute-start | bytes 835592 | tf_op jit(solution)/shard_map/ppermute | solution.py:31
  55.3 27.0 %collective-permute-start.9 = (bf16[272,512]{1,0:T(8,128)(2,1)}, bf16[272,512]{1,0:T(8,128)(2,1)S(1)}, u32[]{:S(2)}, u32[]{:S(2)}) collective-permute-start(bf16[272,512]{1,0:T(8,128)(2,1)} %get-tuple-element.115), channel_id=1, source_target_pairs={{0,8},{4,12},{8,0},{12,4},{16,24},{20,28},{24,16},{28,20},{1,9},{5... | collective-permute-start | bytes 835592 | tf_op jit(solution)/shard_map/ppermute | solution.py:31
  56.1 36.4 %collective-permute-start.10 = (bf16[272,512]{1,0:T(8,128)(2,1)}, bf16[272,512]{1,0:T(8,128)(2,1)S(1)}, u32[]{:S(2)}, u32[]{:S(2)}) collective-permute-start(bf16[272,512]{1,0:T(8,128)(2,1)} %get-tuple-element.116), channel_id=1, source_target_pairs={{0,12},{4,8},{8,4},{12,0},{16,28},{20,24},{24,20},{28,16},{1,13},{... | collective-permute-start | bytes 835592 | tf_op jit(solution)/shard_map/ppermute | solution.py:31
  61.6 47.8 %collective-permute-start.11 = (bf16[272,512]{1,0:T(8,128)(2,1)}, bf16[272,512]{1,0:T(8,128)(2,1)S(1)}, u32[]{:S(2)}, u32[]{:S(2)}) collective-permute-start(bf16[272,512]{1,0:T(8,128)(2,1)} %get-tuple-element.117), channel_id=1, source_target_pairs={{0,16},{4,20},{8,24},{12,28},{16,0},{20,4},{24,8},{28,12},{1,17},{... | collective-permute-start | bytes 835592 | tf_op jit(solution)/shard_map/ppermute | solution.py:31
  65.3 44.0 %collective-permute-start.12 = (bf16[272,512]{1,0:T(8,128)(2,1)}, bf16[272,512]{1,0:T(8,128)(2,1)S(1)}, u32[]{:S(2)}, u32[]{:S(2)}) collective-permute-start(bf16[272,512]{1,0:T(8,128)(2,1)} %get-tuple-element.118), channel_id=1, source_target_pairs={{0,20},{4,16},{8,28},{12,24},{16,4},{20,0},{24,12},{28,8},{1,21},{... | collective-permute-start | bytes 835592 | tf_op jit(solution)/shard_map/ppermute | solution.py:31
  79.0 221.5 %copy-start.9 = (bf16[272,512]{1,0:T(8,128)(2,1)}, bf16[272,512]{1,0:T(8,128)(2,1)S(1)}, u32[]{:S(2)}) copy-start(bf16[272,512]{1,0:T(8,128)(2,1)S(1)} %collective-permute-done.8.refs_7_) | copy-start | bytes 835588
  79.0 30.4 %collective-permute-start.13 = (bf16[272,512]{1,0:T(8,128)(2,1)S(1)}, bf16[272,512]{1,0:T(8,128)(2,1)S(1)}, u32[]{:S(2)}, u32[]{:S(2)}) collective-permute-start(bf16[272,512]{1,0:T(8,128)(2,1)S(1)} %copy-done.46), channel_id=1, source_target_pairs={{0,24},{4,28},{8,16},{12,20},{16,8},{20,12},{24,0},{28,4},{1,25},{... | collective-permute-start | bytes 835592 | tf_op jit(solution)/shard_map/ppermute | solution.py:31
  82.3 218.2 %copy-start.11 = (bf16[272,512]{1,0:T(8,128)(2,1)}, bf16[272,512]{1,0:T(8,128)(2,1)S(1)}, u32[]{:S(2)}) copy-start(bf16[272,512]{1,0:T(8,128)(2,1)S(1)} %collective-permute-done.9.refs_8_) | copy-start | bytes 835588
  82.3 27.1 %collective-permute-start.14 = (bf16[272,512]{1,0:T(8,128)(2,1)S(1)}, bf16[272,512]{1,0:T(8,128)(2,1)S(1)}, u32[]{:S(2)}, u32[]{:S(2)}) collective-permute-start(bf16[272,512]{1,0:T(8,128)(2,1)S(1)} %copy-done.45), channel_id=1, source_target_pairs={{0,28},{4,24},{8,20},{12,16},{16,12},{20,8},{24,4},{28,0},{1,29},{... | collective-permute-start | bytes 835592 | tf_op jit(solution)/shard_map/ppermute | solution.py:31
  92.5 208.0 %copy-start.13 = (bf16[272,512]{1,0:T(8,128)(2,1)}, bf16[272,512]{1,0:T(8,128)(2,1)S(1)}, u32[]{:S(2)}) copy-start(bf16[272,512]{1,0:T(8,128)(2,1)S(1)} %collective-permute-done.10.refs_9_) | copy-start | bytes 835588
  92.5 34.3 %collective-permute-start.17 = (bf16[4,80,512]{2,1,0:T(8,128)(2,1)S(1)}, bf16[4,80,512]{2,1,0:T(8,128)(2,1)S(1)}, u32[]{:S(2)}, u32[]{:S(2)}) collective-permute-start(bf16[4,80,512]{2,1,0:T(8,128)(2,1)S(1)} %get-tuple-element.123), channel_id=1, source_target_pairs={{0,16},{4,20},{8,24},{12,28},{16,0},{20,4},{24,8},{28,12},{1,17},{... | collective-permute-start | bytes 983048 | tf_op jit(solution)/shard_map/ppermute | solution.py:31
  109.4 55.1 %copy-start.19 = (bf16[272,512]{1,0:T(8,128)(2,1)}, bf16[272,512]{1,0:T(8,128)(2,1)S(1)}, u32[]{:S(2)}) copy-start(bf16[272,512]{1,0:T(8,128)(2,1)S(1)} %collective-permute-done.13.refs_12_) | copy-start | bytes 835588
  109.4 55.1 %copy-start.21 = (bf16[272,512]{1,0:T(8,128)(2,1)}, bf16[272,512]{1,0:T(8,128)(2,1)S(1)}, u32[]{:S(2)}) copy-start(bf16[272,512]{1,0:T(8,128)(2,1)S(1)} %collective-permute-done.14.refs_13_) | copy-start | bytes 835588
  128.5 2.0 collective-permute-start.18
  130.6 14.0 %collective-permute-start.19 = (bf16[2,256,512]{2,1,0:T(8,128)(2,1)S(1)}, bf16[2,256,512]{2,1,0:T(8,128)(2,1)S(1)}, u32[]{:S(2)}, u32[]{:S(2)}) collective-permute-start(bf16[2,256,512]{2,1,0:T(8,128)(2,1)S(1)} %add_convert_fusion.1), channel_id=1, source_target_pairs={{0,2},{1,3},{2,0},{3,1},{4,6},{5,7},{6,4},{7,5},{8,10},{9,11},{10,... | collective-permute-start | bytes 1572872 | tf_op jit(solution)/shard_map/ppermute | solution.py:31
  144.9 2.0 collective-permute-start.20
  164.5 2.0 collective-permute-start.21
  164.7 8.6 %collective-permute-start.23 = (bf16[256,512]{1,0:T(8,128)(2,1)S(1)}, bf16[256,512]{1,0:T(8,128)(2,1)S(1)}, u32[]{:S(2)}, u32[]{:S(2)}) collective-permute-start(bf16[256,512]{1,0:T(8,128)(2,1)S(1)} %copy-done.52), channel_id=1, source_target_pairs={{0,4},{4,0},{8,12},{12,8},{16,20},{20,16},{24,28},{28,24},{1,5},{5... | collective-permute-start | bytes 786440 | tf_op jit(solution)/shard_map/ppermute | solution.py:31
  165.3 16.0 %collective-permute-start.24 = (bf16[256,512]{1,0:T(8,128)(2,1)S(1)}, bf16[256,512]{1,0:T(8,128)(2,1)S(1)}, u32[]{:S(2)}, u32[]{:S(2)}) collective-permute-start(bf16[256,512]{1,0:T(8,128)(2,1)S(1)} %copy-done.50), channel_id=1, source_target_pairs={{0,8},{4,12},{8,0},{12,4},{16,24},{20,28},{24,16},{28,20},{1,9},{5... | collective-permute-start | bytes 786440 | tf_op jit(solution)/shard_map/ppermute | solution.py:31
  166.7 16.3 %collective-permute-start.22 = (bf16[1,256,512]{2,1,0:T(8,128)(2,1)S(1)}, bf16[1,256,512]{2,1,0:T(8,128)(2,1)S(1)}, u32[]{:S(2)}, u32[]{:S(2)}) collective-permute-start(bf16[1,256,512]{2,1,0:T(8,128)(2,1)S(1)} %slice.247), channel_id=1, source_target_pairs={{0,2},{1,3},{2,0},{3,1},{4,6},{5,7},{6,4},{7,5},{8,10},{9,11},{10,... | collective-permute-start | bytes 786440 | tf_op jit(solution)/shard_map/ppermute | solution.py:31
  168.2 19.7 %collective-permute-start.25 = (bf16[256,512]{1,0:T(8,128)(2,1)S(1)}, bf16[256,512]{1,0:T(8,128)(2,1)S(1)}, u32[]{:S(2)}, u32[]{:S(2)}) collective-permute-start(bf16[256,512]{1,0:T(8,128)(2,1)S(1)} %copy-done.56), channel_id=1, source_target_pairs={{0,12},{4,8},{8,4},{12,0},{16,28},{20,24},{24,20},{28,16},{1,13},{... | collective-permute-start | bytes 786440 | tf_op jit(solution)/shard_map/ppermute | solution.py:31
  170.0 32.6 %collective-permute-start.26 = (bf16[256,512]{1,0:T(8,128)(2,1)S(1)}, bf16[256,512]{1,0:T(8,128)(2,1)S(1)}, u32[]{:S(2)}, u32[]{:S(2)}) collective-permute-start(bf16[256,512]{1,0:T(8,128)(2,1)S(1)} %copy-done.55), channel_id=1, source_target_pairs={{0,16},{4,20},{8,24},{12,28},{16,0},{20,4},{24,8},{28,12},{1,17},{... | collective-permute-start | bytes 786440 | tf_op jit(solution)/shard_map/ppermute | solution.py:31
  173.3 69.9 %copy-start.23 = (bf16[256,512]{1,0:T(8,128)(2,1)}, bf16[256,512]{1,0:T(8,128)(2,1)S(1)}, u32[]{:S(2)}) copy-start(bf16[256,512]{1,0:T(8,128)(2,1)S(1)} %collective-permute-done.23.refs_15_) | copy-start | bytes 786436
  173.3 34.1 %collective-permute-start.27 = (bf16[256,512]{1,0:T(8,128)(2,1)S(1)}, bf16[256,512]{1,0:T(8,128)(2,1)S(1)}, u32[]{:S(2)}, u32[]{:S(2)}) collective-permute-start(bf16[256,512]{1,0:T(8,128)(2,1)S(1)} %copy-done.54), channel_id=1, source_target_pairs={{0,20},{4,16},{8,28},{12,24},{16,4},{20,0},{24,12},{28,8},{1,21},{... | collective-permute-start | bytes 786440 | tf_op jit(solution)/shard_map/ppermute | solution.py:31
  181.2 62.0 %copy-start.25 = (bf16[256,512]{1,0:T(8,128)(2,1)}, bf16[256,512]{1,0:T(8,128)(2,1)S(1)}, u32[]{:S(2)}) copy-start(bf16[256,512]{1,0:T(8,128)(2,1)S(1)} %collective-permute-done.24.refs_16_) | copy-start | bytes 786436
  181.2 26.2 %collective-permute-start.28 = (bf16[256,512]{1,0:T(8,128)(2,1)S(1)}, bf16[256,512]{1,0:T(8,128)(2,1)S(1)}, u32[]{:S(2)}, u32[]{:S(2)}) collective-permute-start(bf16[256,512]{1,0:T(8,128)(2,1)S(1)} %copy-done.53), channel_id=1, source_target_pairs={{0,24},{4,28},{8,16},{12,20},{16,8},{20,12},{24,0},{28,4},{1,25},{... | collective-permute-start | bytes 786440 | tf_op jit(solution)/shard_map/ppermute | solution.py:31
  183.0 24.5 %collective-permute-start.29 = (bf16[256,512]{1,0:T(8,128)(2,1)S(1)}, bf16[256,512]{1,0:T(8,128)(2,1)S(1)}, u32[]{:S(2)}, u32[]{:S(2)}) collective-permute-start(bf16[256,512]{1,0:T(8,128)(2,1)S(1)} %copy-done.51), channel_id=1, source_target_pairs={{0,28},{4,24},{8,20},{12,16},{16,12},{20,8},{24,4},{28,0},{1,29},{... | collective-permute-start | bytes 786440 | tf_op jit(solution)/shard_map/ppermute | solution.py:31
  187.1 90.9 %copy-start.44 = (bf16[256,512]{1,0:T(8,128)(2,1)}, bf16[256,512]{1,0:T(8,128)(2,1)S(1)}, u32[]{:S(2)}) copy-start(bf16[256,512]{1,0:T(8,128)(2,1)S(1)} %fusion.11) | copy-start | bytes 786436
  187.9 55.4 %copy-start.27 = (bf16[256,512]{1,0:T(8,128)(2,1)}, bf16[256,512]{1,0:T(8,128)(2,1)S(1)}, u32[]{:S(2)}) copy-start(bf16[256,512]{1,0:T(8,128)(2,1)S(1)} %collective-permute-done.25.refs_17_) | copy-start | bytes 786436
  202.6 40.8 %copy-start.29 = (bf16[256,512]{1,0:T(8,128)(2,1)}, bf16[256,512]{1,0:T(8,128)(2,1)S(1)}, u32[]{:S(2)}) copy-start(bf16[256,512]{1,0:T(8,128)(2,1)S(1)} %collective-permute-done.26.refs_18_) | copy-start | bytes 786436
  208.3 22.4 %collective-permute-start.30 = (bf16[1,256,512]{2,1,0:T(8,128)(2,1)S(1)}, bf16[1,256,512]{2,1,0:T(8,128)(2,1)S(1)}, u32[]{:S(2)}, u32[]{:S(2)}) collective-permute-start(bf16[1,256,512]{2,1,0:T(8,128)(2,1)S(1)} %bitcast.74), channel_id=1, source_target_pairs={{0,16},{4,20},{8,24},{12,28},{16,0},{20,4},{24,8},{28,12},{1,17},{... | collective-permute-start | bytes 786440 | tf_op jit(solution)/shard_map/ppermute | solution.py:31
  230.7 12.4 %collective-permute-start.31 = (bf16[2,256,512]{2,1,0:T(8,128)(2,1)S(1)}, bf16[2,256,512]{2,1,0:T(8,128)(2,1)S(1)}, u32[]{:S(2)}, u32[]{:S(2)}) collective-permute-start(bf16[2,256,512]{2,1,0:T(8,128)(2,1)S(1)} %maximum_bitcast_fusion.1), channel_id=1, source_target_pairs={{0,8},{4,12},{8,0},{12,4},{16,24},{20,28},{24,16},{28,20},{1,9},{5... | collective-permute-start | bytes 1572872 | tf_op jit(solution)/shard_map/ppermute | solution.py:31
  243.4 11.7 %collective-permute-start.32 = (bf16[4,128,512]{2,1,0:T(8,128)(2,1)S(1)}, bf16[4,128,512]{2,1,0:T(8,128)(2,1)S(1)}, u32[]{:S(2)}, u32[]{:S(2)}) collective-permute-start(bf16[4,128,512]{2,1,0:T(8,128)(2,1)S(1)} %get-tuple-element.234), channel_id=1, source_target_pairs={{0,4},{4,0},{8,12},{12,8},{16,20},{20,16},{24,28},{28,24},{1,5},{5... | collective-permute-start | bytes 1572872 | tf_op jit(solution)/shard_map/ppermute | solution.py:31
  244.3 12.2 %collective-permute-start.35 = (bf16[1,4,128,512]{3,2,1,0:T(8,128)(2,1)S(1)}, bf16[1,4,128,512]{3,2,1,0:T(8,128)(2,1)S(1)}, u32[]{:S(2)}, u32[]{:S(2)}) collective-permute-start(bf16[1,4,128,512]{3,2,1,0:T(8,128)(2,1)S(1)} %get-tuple-element.232), channel_id=1, source_target_pairs={{0,2},{1,3},{2,0},{3,1},{4,6},{5,7},{6,4},{7,5},{8,10},{9,11},{10,... | collective-permute-start | bytes 1572872 | tf_op jit(solution)/shard_map/ppermute | solution.py:31
  255.2 22.7 %collective-permute-start.33 = (bf16[1,2,4,128,512]{4,3,2,1,0:T(8,128)(2,1)S(1)}, bf16[1,2,4,128,512]{4,3,2,1,0:T(8,128)(2,1)S(1)}, u32[]{:S(2)}, u32[]{:S(2)}) collective-permute-start(bf16[1,2,4,128,512]{4,3,2,1,0:T(8,128)(2,1)S(1)} %maximum_bitcast_fusion), channel_id=1, source_target_pairs={{0,2},{1,3},{2,0},{3,1},{4,6},{5,7},{6,4},{7,5},{8,10},{9,11},{10,... | collective-permute-start | bytes 3145736 | tf_op jit(solution)/shard_map/ppermute | solution.py:31
  256.6 21.5 %collective-permute-start.36 = (bf16[2,4,128,512]{3,2,1,0:T(8,128)(2,1)S(1)}, bf16[2,4,128,512]{3,2,1,0:T(8,128)(2,1)S(1)}, u32[]{:S(2)}, u32[]{:S(2)}) collective-permute-start(bf16[2,4,128,512]{3,2,1,0:T(8,128)(2,1)S(1)} %get-tuple-element.231), channel_id=1, source_target_pairs={{0,4},{4,0},{8,12},{12,8},{16,20},{20,16},{24,28},{28,24},{1,5},{5... | collective-permute-start | bytes 3145736 | tf_op jit(solution)/shard_map/ppermute | solution.py:31
  278.0 64.2 %collective-permute-start.34 = (bf16[2,2,4,128,512]{4,3,2,1,0:T(8,128)(2,1)S(1)}, bf16[2,2,4,128,512]{4,3,2,1,0:T(8,128)(2,1)}, u32[]{:S(2)}, u32[]{:S(2)}) collective-permute-start(bf16[2,2,4,128,512]{4,3,2,1,0:T(8,128)(2,1)S(1)} %pad_maximum_fusion.refs_0_), channel_id=1, source_target_pairs={{0,1},{1,0},{2,3},{3,2},{4,5},{5,4},{6,7},{7,6},{8,9},{9,8},{10,11... | collective-permute-start | bytes 6291464 | tf_op jit(solution)/shard_map/ppermute | solution.py:31
  279.7 64.3 %collective-permute-start.37 = (bf16[2,2,4,128,512]{4,3,2,1,0:T(8,128)(2,1)}, bf16[2,2,4,128,512]{4,3,2,1,0:T(8,128)(2,1)}, u32[]{:S(2)}, u32[]{:S(2)}) collective-permute-start(bf16[2,2,4,128,512]{4,3,2,1,0:T(8,128)(2,1)} %pad_maximum_fusion.1.refs_2_), channel_id=1, source_target_pairs={{0,1},{1,0},{2,3},{3,2},{4,5},{5,4},{6,7},{7,6},{8,9},{9,8},{10,11... | collective-permute-start | bytes 6291464 | tf_op jit(solution)/shard_map/ppermute | solution.py:31
  280.2 8.3 %collective-permute-start.45 = (bf16[256,512]{1,0:T(8,128)(2,1)S(1)}, bf16[256,512]{1,0:T(8,128)(2,1)S(1)}, u32[]{:S(2)}, u32[]{:S(2)}) collective-permute-start(bf16[256,512]{1,0:T(8,128)(2,1)S(1)} %copy-done.49), channel_id=1, source_target_pairs={{0,4},{4,0},{8,12},{12,8},{16,20},{20,16},{24,28},{28,24},{1,5},{5... | collective-permute-start | bytes 786440 | tf_op jit(solution)/shard_map/ppermute | solution.py:31
  281.4 9.2 %collective-permute-start.46 = (bf16[256,512]{1,0:T(8,128)(2,1)S(1)}, bf16[256,512]{1,0:T(8,128)(2,1)S(1)}, u32[]{:S(2)}, u32[]{:S(2)}) collective-permute-start(bf16[256,512]{1,0:T(8,128)(2,1)S(1)} %copy-done.48), channel_id=1, source_target_pairs={{0,8},{4,12},{8,0},{12,4},{16,24},{20,28},{24,16},{28,20},{1,9},{5... | collective-permute-start | bytes 786440 | tf_op jit(solution)/shard_map/ppermute | solution.py:31
  282.0 15.7 %collective-permute-start.47 = (bf16[256,512]{1,0:T(8,128)(2,1)S(1)}, bf16[256,512]{1,0:T(8,128)(2,1)S(1)}, u32[]{:S(2)}, u32[]{:S(2)}) collective-permute-start(bf16[256,512]{1,0:T(8,128)(2,1)S(1)} %copy-done.47), channel_id=1, source_target_pairs={{0,12},{4,8},{8,4},{12,0},{16,28},{20,24},{24,20},{28,16},{1,13},{... | collective-permute-start | bytes 786440 | tf_op jit(solution)/shard_map/ppermute | solution.py:31
  289.2 27.3 %collective-permute-start.48 = (bf16[256,512]{1,0:T(8,128)(2,1)}, bf16[256,512]{1,0:T(8,128)(2,1)}, u32[]{:S(2)}, u32[]{:S(2)}) collective-permute-start(bf16[256,512]{1,0:T(8,128)(2,1)} %get-tuple-element.186), channel_id=1, source_target_pairs={{0,16},{4,20},{8,24},{12,28},{16,0},{20,4},{24,8},{28,12},{1,17},{... | collective-permute-start | bytes 786440 | tf_op jit(solution)/shard_map/ppermute | solution.py:31
  291.3 36.7 %collective-permute-start.49 = (bf16[256,512]{1,0:T(8,128)(2,1)}, bf16[256,512]{1,0:T(8,128)(2,1)}, u32[]{:S(2)}, u32[]{:S(2)}) collective-permute-start(bf16[256,512]{1,0:T(8,128)(2,1)} %get-tuple-element.187), channel_id=1, source_target_pairs={{0,20},{4,16},{8,28},{12,24},{16,4},{20,0},{24,12},{28,8},{1,21},{... | collective-permute-start | bytes 786440 | tf_op jit(solution)/shard_map/ppermute | solution.py:31
  298.4 30.8 %collective-permute-start.50 = (bf16[256,512]{1,0:T(8,128)(2,1)}, bf16[256,512]{1,0:T(8,128)(2,1)}, u32[]{:S(2)}, u32[]{:S(2)}) collective-permute-start(bf16[256,512]{1,0:T(8,128)(2,1)} %get-tuple-element.188), channel_id=1, source_target_pairs={{0,24},{4,28},{8,16},{12,20},{16,8},{20,12},{24,0},{28,4},{1,25},{... | collective-permute-start | bytes 786440 | tf_op jit(solution)/shard_map/ppermute | solution.py:31
  316.5 17.8 %collective-permute-start.51 = (bf16[256,512]{1,0:T(8,128)(2,1)}, bf16[256,512]{1,0:T(8,128)(2,1)}, u32[]{:S(2)}, u32[]{:S(2)}) collective-permute-start(bf16[256,512]{1,0:T(8,128)(2,1)} %get-tuple-element.189), channel_id=1, source_target_pairs={{0,28},{4,24},{8,20},{12,16},{16,12},{20,8},{24,4},{28,0},{1,29},{... | collective-permute-start | bytes 786440 | tf_op jit(solution)/shard_map/ppermute | solution.py:31
  328.0 10.7 %collective-permute-start.38 = (bf16[256,512]{1,0:T(8,128)(2,1)}, bf16[256,512]{1,0:T(8,128)(2,1)}, u32[]{:S(2)}, u32[]{:S(2)}) collective-permute-start(bf16[256,512]{1,0:T(8,128)(2,1)} %get-tuple-element.168), channel_id=1, source_target_pairs={{0,4},{4,0},{8,12},{12,8},{16,20},{20,16},{24,28},{28,24},{1,5},{5... | collective-permute-start | bytes 786440 | tf_op jit(solution)/shard_map/ppermute | solution.py:31
  329.2 10.4 %collective-permute-start.39 = (bf16[256,512]{1,0:T(8,128)(2,1)}, bf16[256,512]{1,0:T(8,128)(2,1)}, u32[]{:S(2)}, u32[]{:S(2)}) collective-permute-start(bf16[256,512]{1,0:T(8,128)(2,1)} %get-tuple-element.169), channel_id=1, source_target_pairs={{0,8},{4,12},{8,0},{12,4},{16,24},{20,28},{24,16},{28,20},{1,9},{5... | collective-permute-start | bytes 786440 | tf_op jit(solution)/shard_map/ppermute | solution.py:31
  334.3 30.8 %collective-permute-start.40 = (bf16[256,512]{1,0:T(8,128)(2,1)}, bf16[256,512]{1,0:T(8,128)(2,1)S(1)}, u32[]{:S(2)}, u32[]{:S(2)}) collective-permute-start(bf16[256,512]{1,0:T(8,128)(2,1)} %get-tuple-element.170), channel_id=1, source_target_pairs={{0,12},{4,8},{8,4},{12,0},{16,28},{20,24},{24,20},{28,16},{1,13},{... | collective-permute-start | bytes 786440 | tf_op jit(solution)/shard_map/ppermute | solution.py:31
  338.7 32.8 %collective-permute-start.41 = (bf16[256,512]{1,0:T(8,128)(2,1)}, bf16[256,512]{1,0:T(8,128)(2,1)S(1)}, u32[]{:S(2)}, u32[]{:S(2)}) collective-permute-start(bf16[256,512]{1,0:T(8,128)(2,1)} %get-tuple-element.171), channel_id=1, source_target_pairs={{0,16},{4,20},{8,24},{12,28},{16,0},{20,4},{24,8},{28,12},{1,17},{... | collective-permute-start | bytes 786440 | tf_op jit(solution)/shard_map/ppermute | solution.py:31
  339.6 38.2 %collective-permute-start.42 = (bf16[256,512]{1,0:T(8,128)(2,1)}, bf16[256,512]{1,0:T(8,128)(2,1)S(1)}, u32[]{:S(2)}, u32[]{:S(2)}) collective-permute-start(bf16[256,512]{1,0:T(8,128)(2,1)} %get-tuple-element.172), channel_id=1, source_target_pairs={{0,20},{4,16},{8,28},{12,24},{16,4},{20,0},{24,12},{28,8},{1,21},{... | collective-permute-start | bytes 786440 | tf_op jit(solution)/shard_map/ppermute | solution.py:31
  342.3 35.5 %collective-permute-start.43 = (bf16[256,512]{1,0:T(8,128)(2,1)}, bf16[256,512]{1,0:T(8,128)(2,1)S(1)}, u32[]{:S(2)}, u32[]{:S(2)}) collective-permute-start(bf16[256,512]{1,0:T(8,128)(2,1)} %get-tuple-element.173), channel_id=1, source_target_pairs={{0,24},{4,28},{8,16},{12,20},{16,8},{20,12},{24,0},{28,4},{1,25},{... | collective-permute-start | bytes 786440 | tf_op jit(solution)/shard_map/ppermute | solution.py:31
  344.0 33.7 %collective-permute-start.44 = (bf16[256,512]{1,0:T(8,128)(2,1)}, bf16[256,512]{1,0:T(8,128)(2,1)S(1)}, u32[]{:S(2)}, u32[]{:S(2)}) collective-permute-start(bf16[256,512]{1,0:T(8,128)(2,1)} %get-tuple-element.174), channel_id=1, source_target_pairs={{0,28},{4,24},{8,20},{12,16},{16,12},{20,8},{24,4},{28,0},{1,29},{... | collective-permute-start | bytes 786440 | tf_op jit(solution)/shard_map/ppermute | solution.py:31
  418.6 1.2 collective-permute-start.52
  419.9 3.7 collective-permute-start.53
  (50 other events, 825.9 us)

commit v2 on v1

--- a/solution.py
+++ b/solution.py
@@ -201,7 +201,8 @@
     )(kv)
 
 
-def attention_kernel(flags, owners, *refs, pieces, heads, group, own, slab):
+def attention_kernel(flags, owners, *refs, places, heads, group, own, slab):
+    pieces = len(places)
     q_ref, tenant_ref, kv_refs, rest = refs[0], refs[1], refs[2 : 2 + 2 * pieces], refs[2 + 2 * pieces :]
     if own:
         own_key, own_value, begin_ref = rest[:3]
@@ -263,10 +264,10 @@
 
     for j in range(pieces):
 
-        @pl.when(flags[block, j] > 0)
+        @pl.when(flags[block, places[j]] > 0)
         def _(j=j):
             top, summed, value = attend(kv_refs[2 * j], kv_refs[2 * j + 1], slab)
-            ok = tenants == owners[j]
+            ok = tenants == owners[places[j]]
             old = best[...]
             new = jnp.where(ok, jnp.maximum(old, top), old)
             keep = jnp.where(ok, jnp.exp(old - new), 1.0)
@@ -301,8 +302,9 @@
         lse_out[0] = lse
 
 
-def attention_call(query, tenant, flags, owners, pieces, own_part):
+def attention_call(query, tenant, flags, owners, pieces, places, own_part, name):
     rows, width = query.shape
+    pieces = [pieces[place] for place in places]
     slab, wide = pieces[0][0].shape
     own = own_part is not None
     heads = wide // 64
@@ -320,7 +322,7 @@
         in_specs += [full(own_key), full(own_value), lanes]
     depth = 64 if own else 80
     kernel = functools.partial(
-        attention_kernel, pieces=len(pieces), heads=heads, group=group, own=own, slab=slab
+        attention_kernel, places=places, heads=heads, group=group, own=own, slab=slab
     )
     return pl.pallas_call(
         kernel,
@@ -340,27 +342,33 @@
                 pltpu.VMEM((wide, stack), F32),
             ],
         ),
-        compiler_params=params(40),
+        compiler_params=params(60),
         cost_estimate=pl.CostEstimate(
             flops=4 * rows * group * slab * wide * 4,
             bytes_accessed=4 * slab * wide * len(pieces),
             transcendentals=rows * group * heads * slab,
         ),
-        name="attention_own" if own else "attention_partner",
+        name=name,
     )(flags, owners, *operands)
 
 
 def project_kernel(
-    place, one, lse_one, two, w_out, kept, sent, attended, *, count, width, pieces
+    place, one, lse_one, two, three, w_out, kept, sent, attended, *, count, width, pieces
 ):
     me = place[0]
     for b in range(one.shape[0]):
-        first = lse_one[b]
-        extra = two[b, 64:, :].astype(F32)
-        second = extra[0:1] + extra[1:2] + extra[2:3]
-        share_one = 1.0 / (1.0 + jnp.exp(second - first))
-        share_two = 1.0 / (1.0 + jnp.exp(first - second))
-        merged = one[b] * share_one + two[b, :64, :].astype(F32) * share_two
+        logs = [lse_one[b]]
+        for other in (two, three):
+            extra = other[b, 64:, :].astype(F32)
+            logs.append(extra[0:1] + extra[1:2] + extra[2:3])
+        top = functools.reduce(jnp.maximum, logs)
+        shares = [jnp.exp(value - top) for value in logs]
+        inverse = 1.0 / sum(shares)
+        merged = (
+            one[b] * (shares[0] * inverse)
+            + two[b, :64, :].astype(F32) * (shares[1] * inverse)
+            + three[b, :64, :].astype(F32) * (shares[2] * inverse)
+        )
         rows = jnp.transpose(jnp.concatenate([merged, jnp.zeros_like(merged)], axis=0))
         for t in range(count // 2):
             left = rows[2 * t * BLOCK : (2 * t + 1) * BLOCK]
@@ -374,7 +382,7 @@
         (sent if j % 2 else kept)[j // 2] = part.astype(BF)
 
 
-def project_call(place, one, lse_one, two, w_out, pieces):
+def project_call(place, one, lse_one, two, three, w_out, pieces):
     rows = one.shape[0] * BLOCK
     model = w_out.shape[1]
     width = model // pieces
@@ -386,7 +394,7 @@
     return pl.pallas_call(
         kernel,
         out_shape=(half, half),
-        in_specs=[pl.BlockSpec(memory_space=pltpu.SMEM)] + [whole] * 4,
+        in_specs=[pl.BlockSpec(memory_space=pltpu.SMEM)] + [whole] * 5,
         out_specs=(whole, whole),
         scratch_shapes=[pltpu.VMEM((rows, w_out.shape[0]), BF)],
         compiler_params=params(24),
@@ -394,7 +402,7 @@
             flops=2 * rows * w_out.size, bytes_accessed=2 * w_out.size, transcendentals=0
         ),
         name="project",
-    )(place, one, lse_one, two, w_out)
+    )(place, one, lse_one, two, three, w_out)
 
 
 def swiglu_kernel(
@@ -456,7 +464,7 @@
                 pltpu.VMEM((rows, model), F32),
             ],
         ),
-        compiler_params=params(40),
+        compiler_params=params(60),
         cost_estimate=pl.CostEstimate(
             flops=6 * rows * model * units,
             bytes_accessed=6 * model * units,
@@ -466,137 +474,193 @@
     )(place, ours, theirs, gain.reshape(pieces, width), w_gate, w_up, w_down)
 
 
-def head_kernel(place, *refs, depth, offset, span, width, pieces, blocks, cuts, step_cols):
-    quads = refs[:4]
-    gain, targets = refs[4:6]
-    count = blocks * cuts
-    w_refs = refs[6 : 6 + count]
-    out, w_full, normed, sems = refs[6 + count :]
+def head_kernel(
+    place, *refs, count, locate, depth, offset, span, width, pieces, blocks, widths, code_widths
+):
+    hidden = refs[:count]
+    w_refs = refs[count : count + blocks * len(widths)]
+    code_refs = refs[count + blocks * len(widths) : count + blocks * (len(widths) + 1)]
+    out, w_full, tile, codes, raw, factors, tops, w_sems, tile_sems, code_sems = refs[
+        count + blocks * (len(widths) + 1) :
+    ]
     me_req, me_mlp = place[1], place[0]
-    step = pl.program_id(0)
+    rows = tile.shape[1]
+    half_rows = rows // 2
+    model = tile.shape[2]
     columns_here = w_full.shape[1]
-    cut = columns_here // cuts
-
-    @pl.when(step == 0)
-    def _():
-        copies = [
-            pltpu.make_async_copy(
-                w_refs[n].at[:depth, :],
-                w_full.at[
-                    pl.ds(pl.multiple_of((me_req ^ (n % blocks)) * depth, depth), depth),
-                    pl.ds(n // blocks * cut, cut),
-                ],
-                sems.at[n],
-            )
-            for n in range(count)
-        ]
-        for copy in copies:
-            copy.start()
-        for copy in copies:
-            copy.wait()
-
-    rows_half = quads[0].shape[-2]
-    for part in range(2):
-        own_ref, other_ref = quads[2 * part], quads[2 * part + 1]
-        loaded = []
-        for j in range(pieces):
-            source = (other_ref if j % 2 else own_ref)[...].reshape(
-                pieces // 2, rows_half, width
-            )
-            loaded.append(source[j // 2].astype(F32))
-        squares = sum(jnp.sum(value * value, axis=-1, keepdims=True) for value in loaded)
-        factor = lax.rsqrt(squares / (pieces * width) + EPS)
-        for j in range(pieces):
-            quarter = me_mlp ^ j
-            where = pl.ds(pl.multiple_of(quarter * width, width), width)
-            normed[part * rows_half : (part + 1) * rows_half, where] = (
-                loaded[j] * factor * gain[pl.ds(quarter, 1), :]
-            ).astype(BF)
-
-    rows = 2 * rows_half
+
+    def fetch(z, y):
+        copies = []
+        for part in range(2):
+            for j in range(pieces):
+                index, where = locate(part, j // 2, y, j % 2)
+                source = hidden[index]
+                for position in where:
+                    source = source.at[position if position is not None else z]
+                copies.append(
+                    pltpu.make_async_copy(
+                        source,
+                        tile.at[
+                            y,
+                            pl.ds(part * half_rows, half_rows),
+                            pl.ds(pl.multiple_of((me_mlp ^ j) * width, width), width),
+                        ],
+                        tile_sems.at[y, part * pieces + j],
+                    )
+                )
+        return copies
+
+    w_copies = [
+        pltpu.make_async_copy(
+            w_refs[n].at[:depth, :],
+            w_full.at[
+                pl.ds(pl.multiple_of((me_req ^ (n % blocks)) * depth, depth), depth),
+                pl.ds(sum(widths[: n // blocks]), widths[n // blocks]),
+            ],
+            w_sems.at[n],
+        )
+        for n in range(blocks * len(widths))
+    ]
+    code_copies = [
+        pltpu.make_async_copy(code_refs[k].at[depth:, :], codes.at[k], code_sems.at[k])
+        for k in range(blocks)
+    ]
+    for copy in fetch(0, 0) + code_copies + w_copies:
+        copy.start()
+    for copy in code_copies + w_copies:
+        copy.wait()
+
     lane = lane_ids((rows, LANES))
     base = me_mlp * (span * blocks) + me_req * span + offset
-    wanted = targets[...] - base
-    best = jnp.full((rows, LANES), NEG, F32)
-    total = jnp.zeros((rows, LANES), F32)
-    picked = jnp.zeros((rows, LANES), F32)
-    for c in range(columns_here // step_cols):
-        logits = jnp.dot(
-            normed[...],
-            w_full[:, c * step_cols : (c + 1) * step_cols],
-            preferred_element_type=F32,
+    step_cols = math.gcd(columns_here, 256)
+    lanes_of = lambda values, c: values[:, c * LANES : (c + 1) * LANES]
+
+    def wanted_of(here):
+        lines = codes[here].astype(F32)
+        flat = jnp.concatenate(
+            [lines[l : l + 1] for l in range(-(-2 * rows // code_widths))], axis=1
         )
-        tiles = [logits[:, t * LANES : (t + 1) * LANES] for t in range(step_cols // LANES)]
-        new = functools.reduce(jnp.maximum, tiles, best)
-        total = total * jnp.exp(best - new)
-        for t, tile in enumerate(tiles):
-            total = total + jnp.exp(tile - new)
-            hit = lane == wanted - (c * step_cols + t * LANES)
-            picked = picked + jnp.where(hit, tile, 0.0)
-        best = new
-    top = jnp.max(best, axis=-1, keepdims=True)
-    summed = jnp.sum(total * jnp.exp(best - top), axis=-1, keepdims=True)
-    chosen = jnp.sum(picked, axis=-1, keepdims=True)
-    joined = jnp.where(lane == 0, top, jnp.where(lane == 1, summed, chosen))
-    out[...] = jnp.transpose(joined)[:8][None]
-
-
-def head_call(place, quads, gain, targets, w_parts, depth, offset, span):
-    blocks = len(w_parts[0])
-    cut = w_parts[0][0].shape[1]
-    columns = cut * len(w_parts)
-    half_rows, width = quads[0][0].shape[-2:]
+        wanted = (flat[:, :rows] * 256.0 + flat[:, rows : 2 * rows]).astype(jnp.int32)
+        return jnp.transpose(jnp.broadcast_to(wanted, (LANES, rows))) - base - lane
+
+    def stage(new, old, place_old):
+        if old is not None:
+            factor = factors[old]
+            best = tops[old] * factor
+            total = jnp.zeros((rows, LANES), F32)
+            picked = jnp.zeros((rows, LANES), F32)
+            wanted = wanted_of(place_old)
+        if new is not None:
+            squares = jnp.zeros((rows, LANES), F32)
+            top = jnp.full((rows, LANES), NEG, F32)
+        steps = columns_here // step_cols
+        per_step = -(-(model // LANES) // steps)
+        for c in range(steps):
+            part = slice(c * step_cols, (c + 1) * step_cols)
+            if new is not None:
+                logits = jnp.dot(tile[new], w_full[:, part], preferred_element_type=F32)
+                raw[new, :, part] = logits
+                for t in range(step_cols // LANES):
+                    top = jnp.maximum(top, lanes_of(logits, t))
+                for t in range(c * per_step, min((c + 1) * per_step, model // LANES)):
+                    value = tile[new, :, t * LANES : (t + 1) * LANES].astype(F32)
+                    squares = squares + value * value
+            if old is not None:
+                for t in range(c * step_cols // LANES, (c + 1) * step_cols // LANES):
+                    value = raw[old, :, t * LANES : (t + 1) * LANES] * factor
+                    total = total + jnp.exp(value - best)
+                    picked = jnp.where(wanted == t * LANES, value, picked)
+        if new is not None:
+            tops[new] = top
+            scale = lax.rsqrt(jnp.sum(squares, axis=-1, keepdims=True) / model + EPS)
+            factors[new] = jnp.broadcast_to(scale, (rows, LANES))
+        if old is not None:
+            best = jnp.transpose(best)
+            highest = jnp.max(best, axis=0, keepdims=True)
+            summed = jnp.sum(jnp.transpose(total) * jnp.exp(best - highest), axis=0, keepdims=True)
+            chosen = jnp.sum(jnp.transpose(picked), axis=0, keepdims=True)
+            line = lax.broadcasted_iota(jnp.int32, (8, rows), 0)
+            joined = jnp.where(line == 0, highest, jnp.where(line == 1, summed, chosen))
+            out[pl.ds(place_old ^ me_req, 1)] = joined[None]
+
+    depth_z = blocks // 2
+
+    def begin(z, y):
+        for copy in fetch(z, y):
+            copy.start()
+
+    def finish(z, y):
+        for copy in fetch(z, y):
+            copy.wait()
+
+    begin(0, 1)
+    finish(0, 0)
+    stage(0, None, None)
+
+    def pair(z, carry):
+        begin(z + 1, 0)
+        finish(z, 1)
+        stage(1, 0, 2 * z)
+        begin(z + 1, 1)
+        finish(z + 1, 0)
+        stage(0, 1, 2 * z + 1)
+        return carry
+
+    lax.fori_loop(0, depth_z - 1, pair, 0)
+    last = depth_z - 1
+    finish(last, 1)
+    stage(1, 0, 2 * last)
+    stage(None, 1, 2 * last + 1)
+
+
+def head_call(place, hidden, locate, w_parts, codes, depth, offset, span):
+    blocks = len(codes)
+    widths = [part[0].shape[1] for part in w_parts]
+    columns = sum(widths)
+    half_rows, width = hidden[0].shape[-2:]
     model = depth * blocks
     pieces = model // width
     rows = 2 * half_rows
-
-    def spec(order):
-        def index(s, place_ref):
-            where = {"y": s % 2, "z": s // 2, "x": 0}
-            return tuple(where[name] for name in order) + (0, 0)
-
-        shape = tuple(pieces // 2 if name == "x" else 1 for name in order)
-        return pl.BlockSpec(shape + (half_rows, width), index)
-
-    step_cols = min(512, columns)
+    code_widths = codes[0].shape[1]
     kernel = functools.partial(
         head_kernel,
+        count=len(hidden),
+        locate=locate,
         depth=depth,
         offset=offset,
         span=span,
         width=width,
         pieces=pieces,
         blocks=blocks,
-        cuts=len(w_parts),
-        step_cols=step_cols,
-    )
+        widths=widths,
+        code_widths=code_widths,
+    )
+    operands = list(hidden) + sum(w_parts, []) + list(codes)
     return pl.pallas_call(
         kernel,
         out_shape=jax.ShapeDtypeStruct((blocks, 8, rows), F32),
-        grid_spec=pltpu.PrefetchScalarGridSpec(
-            num_scalar_prefetch=1,
-            grid=(blocks,),
-            in_specs=[spec(order) for _, order in quads]
-            + [
-                pl.BlockSpec((pieces, width), lambda s, place_ref: (0, 0)),
-                pl.BlockSpec((rows, 1), lambda s, place_ref: (s, 0)),
-            ]
-            + [pl.BlockSpec(memory_space=pl.ANY)] * (blocks * len(w_parts)),
-            out_specs=pl.BlockSpec((1, 8, rows), lambda s, place_ref: (s ^ place_ref[1], 0, 0)),
-            scratch_shapes=[
-                pltpu.VMEM((model, columns), BF),
-                pltpu.VMEM((rows, model), BF),
-                pltpu.SemaphoreType.DMA((blocks * len(w_parts),)),
-            ],
-        ),
-        compiler_params=params(40),
+        in_specs=[pl.BlockSpec(memory_space=pltpu.SMEM)]
+        + [pl.BlockSpec(memory_space=pl.ANY)] * len(operands),
+        out_specs=pl.BlockSpec(memory_space=pltpu.VMEM),
+        scratch_shapes=[
+            pltpu.VMEM((model, columns), BF),
+            pltpu.VMEM((2, rows, model), BF),
+            pltpu.VMEM((blocks, 16, code_widths), BF),
+            pltpu.VMEM((2, rows, columns), F32),
+            pltpu.VMEM((2, rows, LANES), F32),
+            pltpu.VMEM((2, rows, LANES), F32),
+            pltpu.SemaphoreType.DMA((blocks * len(widths),)),
+            pltpu.SemaphoreType.DMA((2, 2 * pieces)),
+            pltpu.SemaphoreType.DMA((blocks,)),
+        ],
+        compiler_params=params(60),
         cost_estimate=pl.CostEstimate(
             flops=2 * rows * blocks * model * columns,
             bytes_accessed=2 * model * columns + 2 * rows * blocks * model,
             transcendentals=rows * blocks * columns,
         ),
         name="head",
-    )(place, *[array for array, _ in quads], gain.reshape(pieces, width), targets, *sum(w_parts, []))
+    )(place, *operands)
 
 
 def merge_stats(one, two):
@@ -637,34 +701,21 @@
     split_count = groups // TENANTS
     head_size = q_gain.shape[0]
 
-    meta = jnp.concatenate([req_lengths, req_tenant], axis=1)
-    meta_far = swap(meta, "req", half)
+    meta_far = swap(jnp.concatenate([req_lengths, req_tenant], axis=1), "req", half)
     per = req_lengths.shape[1]
 
-    span = w_head.shape[1] // groups
-    parts_of_span = 4
-    cut = span // parts_of_span
-    coded = jnp.concatenate([targets >> 8, targets & 255]).astype(F32).astype(BF)
-    coded = coded.reshape(-1, cut)
-    extra = jnp.pad(coded, ((0, 16 - coded.shape[0]), (0, 0)))
-
-    def head_part(part, k):
-        block = lax.dynamic_slice_in_dim(w_head, (me_req ^ k) * span + part * cut, cut, 1)
-        return jnp.concatenate([block, extra], axis=0) if part == 0 else block
-
-    own_parts = [head_part(part, 0) for part in range(parts_of_span)]
-    out_parts = [[head_part(part, k) for k in range(1, groups)] for part in range(parts_of_span)]
-
-    def send_part(part, event):
-        blocks = after(tuple(out_parts[part]), event)
-        return [own_parts[part]] + [
-            swap(block, "req", k) for k, block in zip(range(1, groups), blocks)
-        ]
+    pieces = [split_call(prefix_kv[0])]
 
     stream = [tokens]
     for bit in [b for b in bits_of(parts) if b > 1][::-1]:
         got = swap(jnp.concatenate(stream, axis=1), "mlp", bit)
         stream = stream + [got[:, i * width : (i + 1) * width] for i in range(len(stream))]
+    stream, req_lengths, req_tenant, meta_far, prefix_piece = lax.optimization_barrier(
+        (stream, req_lengths, req_tenant, meta_far, prefix_piece)
+    )
+    pieces, w_head, final_gain, targets = lax.optimization_barrier(
+        (pieces, w_head, final_gain, targets)
+    )
     got = swap(jnp.concatenate(stream, axis=1), "mlp", 1)
     stream = [
         part
@@ -672,14 +723,63 @@
         for part in (mine, got[:, i * width : (i + 1) * width])
     ]
 
-    stream, own_parts, out_parts = lax.optimization_barrier((stream, own_parts, out_parts))
-
-    pieces = [split_call(prefix_kv[0])]
-    for k in range(1, half):
-        least, most = k & -k, 1 << (k.bit_length() - 1)
-        pieces.append(
-            (swap(pieces[k ^ least][0], "req", least), swap(pieces[k ^ most][1], "req", most))
+    span = w_head.shape[1] // groups
+    quarter = span // 4
+    cuts = [(0, 2 * quarter), (2 * quarter, quarter), (3 * quarter, quarter)]
+    coded = jnp.concatenate([targets >> 8, targets & 255]).astype(F32).astype(BF)
+    coded = coded.reshape(-1, cuts[0][1]) if 2 * rows >= cuts[0][1] else jnp.pad(
+        coded, (0, cuts[0][1] - 2 * rows)
+    ).reshape(1, -1)
+    extra = jnp.pad(coded, ((0, 16 - coded.shape[0]), (0, 0)))
+
+    row_gain = lax.dynamic_slice_in_dim(final_gain, me_req * w_head.shape[0], w_head.shape[0], 0)
+    row_gain = row_gain[:, None]
+
+    def head_part(part, k, matrix):
+        start, size = cuts[part]
+        block = lax.dynamic_slice_in_dim(matrix, (me_req ^ k) * span + start, size, 1)
+        block = (block.astype(F32) * row_gain).astype(BF)
+        return jnp.concatenate([block, extra], axis=0) if part == 0 else block
+
+    across = groups // 4
+    inner = (me_req // across == 1) | (me_req // across == 2)
+    head_in = {}
+    head_out = {}
+
+    def far(part, place):
+        first = half + place * (half // 4)
+        return [(part, k) for k in range(first, first + half // 4)]
+
+    def near(part, place):
+        return [(part, k) for k in range(1, half) if (k - 1) % 3 == place]
+
+    def send(units, event, where=None):
+        blocks = after([head_out[unit] for unit in units], event)
+        sent = {}
+        for unit, block in zip(units, blocks):
+            pairs = [
+                (i, i ^ unit[1])
+                for i in range(groups)
+                if where is None or (i // across in (1, 2)) == (where == "inner")
+            ]
+            sent[unit] = (where, lax.ppermute(block, "req", pairs))
+        return sent
+
+    def arrive(sent, event):
+        event, blocks = lax.optimization_barrier(
+            (event, {unit: block for unit, (_, block) in sent.items()})
         )
+        got = {unit: (sent[unit][0], blocks[unit]) for unit in sent}
+        for unit, (where, block) in got.items():
+            if unit in head_in:
+                block = jnp.where(inner == (where == "inner"), block, head_in[unit])
+            head_in[unit] = block
+        return event
+
+    far_rest = [k for _, k in far(0, 2) if k != half + half // 2]
+    early = [(part, half + half // 2) for part in range(3)]
+    head_out.update({unit: head_part(*unit, w_head) for unit in early})
+    sent_start = send(early, tokens, "inner")
 
     request, offset, tenant = row_layout(req_lengths[0], req_tenant[0], rows)
     _, _, tenant_far = row_layout(meta_far[0, :per], meta_far[0, per:], rows)
@@ -702,30 +802,68 @@
     row_ids = jnp.arange(rows, dtype=jnp.int32)
     cosine, sine = rope_tables((PLEN + offset).astype(jnp.float32), head_size)
 
+    near_rows = (flags_of(tenant), by_block(tenant), by_block(row_ids - offset))
+    far_rows = (flags_of(tenant_far), by_block(tenant_far))
+    stream, owners, near_rows, far_rows, cosine, sine = lax.optimization_barrier(
+        (stream, owners, near_rows, far_rows, cosine, sine)
+    )
     query, own_key, own_value = qkv_call(
         place, stream, attn_gain, w_query, w_keyval, cosine, sine, q_gain, k_gain
     )
+    for k in range(1, half):
+        if k & (k - 1) == 0:
+            pieces.append(tuple(swap(array, "req", k) for array in pieces[0]))
+        else:
+            pieces.append(None)
+    direct = [k for k in range(half) if pieces[k] is not None]
+    passed = [k for k in range(half) if pieces[k] is None]
+    arrived = [pieces[k] for k in direct]
+    arrived, query = lax.optimization_barrier((arrived, query))
+    for k, piece in zip(direct, arrived):
+        pieces[k] = piece
+    for k in passed:
+        least, most = k & -k, 1 << (k.bit_length() - 1)
+        pieces[k] = (
+            swap(pieces[k ^ least][0], "req", least), swap(pieces[k ^ most][1], "req", most)
+        )
     query_far = swap(query, "req", half)
-    part_0 = send_part(0, query)
-    out_far, _ = attention_call(
-        query_far, by_block(tenant_far), flags_of(tenant_far), owners, pieces, None
-    )
-    back = swap(out_far, "req", half)
     out_near, lse_near = attention_call(
         query,
-        by_block(tenant),
-        flags_of(tenant),
+        near_rows[1],
+        near_rows[0],
         owners,
         pieces,
-        (own_key, own_value, by_block(row_ids - offset)),
-    )
-    out_near, part_0 = lax.optimization_barrier((out_near, part_0))
-    kept, sent = project_call(place, out_near, lse_near, back, w_out, parts)
+        direct,
+        (own_key, own_value, near_rows[2]),
+        "attention_near",
+    )
+    query_far, out_near = lax.optimization_barrier((query_far, out_near))
+    query_far = arrive(sent_start, query_far)
+    w_rest = after(w_head, query_far)
+    for part in range(len(cuts)):
+        head_in[part, 0] = head_part(part, 0, w_rest)
+        for k in range(1, groups):
+            if (part, k) not in head_out:
+                head_out[part, k] = head_part(part, k, w_rest)
+
+    sent_one = send(far(0, 1) + near(0, 0), query_far)
+    out_far, _ = attention_call(
+        query_far, far_rows[1], far_rows[0], owners, pieces, range(half), None, "attention_far"
+    )
+    out_far = arrive(sent_one, out_far)
+    back = swap(out_far, "req", half)
+    sent_one = send(far(1, 0) + near(0, 1), out_far)
+    query = after(query, out_far)
+    out_rest, _ = attention_call(
+        query, near_rows[1], near_rows[0], owners, pieces, passed, None, "attention_rest"
+    )
+    back, out_rest = arrive(sent_one, (back, out_rest))
+    kept, sent = project_call(place, out_near, lse_near, back, out_rest, w_out, parts)
 
     def over_cores(kept, sent):
         return kept.astype(F32) + swap(sent, "mlp", 1).astype(F32)
 
-    part_1 = send_part(1, kept)
+    sent_one = send(far(0, 0) + near(0, 2), kept)
     summed = over_cores(kept, sent)
     x_bits = [b // 2 for b in bits_of(parts) if b > 1]
     for bit in x_bits:
@@ -734,55 +872,83 @@
         summed = summed.astype(BF).astype(F32) + jnp.stack([got[i] for i in order]).astype(F32)
     residual = jnp.stack(stream[0::2]).astype(F32)
     mid = (residual + summed).astype(BF)
+    mid = arrive(sent_one, mid)
     mid_other = swap(mid, "mlp", 1)
 
-    kept, sent = swiglu_call(place, mid, mid_other, mlp_gain, w_gate, w_up, w_down)
+    sent_one = {**send(far(1, 1) + near(1, 0), mid), **send(far(0, 3), mid, "outer")}
+    kept, sent = arrive(
+        sent_one, swiglu_call(place, mid, mid_other, mlp_gain, w_gate, w_up, w_down)
+    )
+    sent_one = {**send(near(1, 1), kept), **send(far(1, 3) + far(2, 3), kept, "inner")}
     summed = over_cores(kept, sent)
     for bit in x_bits:
         got = swap(summed[bit:].astype(BF), "mlp", 2 * bit)
         summed = summed[:bit] + got.astype(F32)
     out_share = (mid[0].astype(F32) + summed[0]).astype(BF)
 
-    out_share, part_1 = lax.optimization_barrier((out_share, part_1))
+    out_share = arrive(sent_one, out_share)
 
     spread = out_share[None]
     for bit in [b for b in bits_of(groups) if b > 1]:
+        last = bit == 2
+        if last:
+            sent_one = send(far(0, 3), spread, "inner")
         got = swap(spread, "req", bit)
         count = spread.shape[0]
         spread = (
             jnp.stack([spread, got], axis=0) if count == 1 else jnp.stack([spread, got], axis=1)
         ).reshape(2 * count, rows, width)
-    part_2 = send_part(2, spread)
-    part_3 = send_part(3, spread)
+        if last:
+            spread = arrive(sent_one, spread)
+    middle = half + half // 2
+    sent_one = send([(1, middle), (2, middle)] + far(1, 3), spread, "outer")
     top_rows, low_rows = spread[:, : rows // 2], spread[:, rows // 2 :]
 
-    def add_y(values, axis):
-        return jnp.stack([values, swap(values, "req", 1)], axis=axis)
-
-    def add_x(values, axis):
-        values = jnp.expand_dims(values, axis)
-        for bit in x_bits[::-1]:
-            values = jnp.concatenate([values, swap(values, "mlp", 2 * bit)], axis=axis)
+    x_count = parts // 2
+
+    def add_x(values, bits):
+        for bit in bits:
+            values = jnp.concatenate([values, swap(values, "mlp", 2 * bit)], axis=0)
         return values
 
-    top_rows = add_x(add_y(top_rows, 0), 0)
-    low_rows = add_y(add_x(low_rows, 0), 0)
-    quads = [
-        (top_rows, "xyz"),
-        (swap(top_rows, "mlp", 1), "xyz"),
-        (low_rows, "yxz"),
-        (swap(low_rows, "mlp", 1), "yxz"),
-    ]
-
-    codes = jnp.stack([block[w_head.shape[0] :].reshape(-1)[: 2 * rows] for block in part_0])
-    codes = codes.astype(F32).astype(jnp.int32)
-    wanted = (codes[:, :rows] * 256 + codes[:, rows:]).reshape(groups * rows, 1)
-    stats = None
-    for first, group_of in ((0, [part_0, part_1, part_2]), (3, [part_3])):
-        found = head_call(
-            place, quads, final_gain, wanted, group_of, w_head.shape[0], first * cut, span
+    top_rows = jnp.stack([top_rows, swap(top_rows, "req", 1)])[None]
+    low_rows = add_x(low_rows[None], x_bits[::-1])
+    top_rows, low_rows = arrive(sent_one, (top_rows, low_rows))
+    sent_one = {
+        **send(near(1, 2) + far(2, 0), top_rows),
+        **send([(0, half + half // 2)], top_rows, "outer"),
+    }
+    top_rows = add_x(top_rows, x_bits[::-1][:-1])
+    top_more = swap(top_rows, "mlp", 2 * x_bits[0])
+    low_more = swap(low_rows, "req", 1)
+    others = [(part, k) for part in (0, 1, 2) for k in far_rest]
+    sent_one.update(send(others, top_rows))
+    top_more, low_more = arrive(sent_one, (top_more, low_more))
+    sent_last = {
+        **send(far(2, 1), top_more),
+        **send(far(2, 3), top_more, "outer"),
+        **send(near(2, 0) + near(2, 1) + near(2, 2), top_more),
+    }
+    hidden = [top_rows, top_more, low_rows, low_more]
+    hidden = hidden + [swap(values, "mlp", 1) for values in hidden]
+    split_at = x_count // 2
+
+    def locate(part, x, y, core):
+        if part == 0:
+            return (4 * core + x // split_at, (x % split_at, y, None))
+        return (4 * core + 2 + y, (x, None))
+
+    depth = w_head.shape[0]
+    codes = [head_in[0, k] for k in range(groups)]
+
+    def head_of(parts_of):
+        blocks = [[head_in[part, k] for k in range(groups)] for part in parts_of]
+        return head_call(
+            place, hidden, locate, blocks, codes, depth, cuts[parts_of[0]][0], span
         )[:, :3]
-        stats = found if stats is None else merge_stats(stats, found)
+
+    stats = arrive(sent_last, head_of([0, 1]))
+    stats = merge_stats(stats, head_of([2]))
 
     spread_stats = lax.all_to_all(stats, "req", 0, 0, tiled=True)
     top = jnp.max(spread_stats[:, 0], axis=0)

time: 425 us -> 377 us (0.89); the launches traced: 424 us -> 370 us
  waiting for transfers between devices: 182 us -> 126 us
  other arithmetic: 12.3 us -> 29.7 us
  local copies, waits for them, and re-layouts: 28.3 us -> 15.7 us
  blocking collectives: 16.8 us -> 9.29 us
  Pallas kernels: 91.3 us -> 96.1 us
    ppermute x54 -> x28, waiting for transfers between devices: 182 us -> 56.3 us  [swap(): return lax.ppermute(values, axis, [(i, i ^ bit) for i in range(size)])]
    ppermute x0 -> x27, waiting for transfers between devices: none -> 70.2 us  [send(): sent[unit] = (where, lax.ppermute(block, 'req', pairs))]
    ppermute x54 -> x28, starting transfers between devices: 91.6 us -> 43.3 us  [swap(): return lax.ppermute(values, axis, [(i, i ^ bit) for i in range(size)])]
    ppermute x0 -> x27, starting transfers between devices: none -> 47.9 us  [send(): sent[unit] = (where, lax.ppermute(block, 'req', pairs))]
    convert_element_type x1 -> x4, other arithmetic: 0.01 us -> 10.9 us  [head_part(): block = (block.astype(F32) * row_gain).astype(BF)]
    all_to_all x1, blocking collectives: 16.8 us -> 9.29 us  [body(): spread_stats = lax.all_to_all(stats, 'req', 0, 0, tiled=True)]
    pallas_call x2 -> x3, Pallas kernels: 30 us -> 36.7 us  [attention_call(): pl.pallas_call(kernel, out_shape=(jax.ShapeDtypeStruct((blocks, depth, st...]
    unnamed x122 -> x140, local copies, waits for them, and re-layouts: 14.1 us -> 8.07 us
  transfers between devices with their start and end apart: 54 -> 55, of which waited for: 28 -> 19; matrix products, arithmetic and copies ran while one was open for 6% -> 9% of each run, Pallas kernels for 11% -> 21%
where the time goes in v2:
time: 377 us; the launch traced here: 370 us
  waiting for transfers between devices  126 us (33%)
  Pallas kernels  96.1 us (25%)
  starting transfers between devices  91.2 us (24%)
  other arithmetic  29.7 us (8%)
  local copies, waits for them, and re-layouts  15.7 us (4%)
  blocking collectives  9.29 us (2%)
    ppermute x27, waiting for transfers between devices, send(): sent[unit] = (where, lax.ppermute(block, 'req', pairs))  70.2 us
    ppermute x28, waiting for transfers between devices, swap(): return lax.ppermute(values, axis, [(i, i ^ bit) for i in range(size)])  56.3 us
    ppermute x27, starting transfers between devices, send(): sent[unit] = (where, lax.ppermute(block, 'req', pairs))  47.9 us
    ppermute x28, starting transfers between devices, swap(): return lax.ppermute(values, axis, [(i, i ^ bit) for i in range(size)])  43.3 us
    pallas_call x3, Pallas kernels, attention_call(): pl.pallas_call(kernel, out_shape=(jax.ShapeDtypeStruct((blocks, depth, st...  36.7 us
    pallas_call x2, Pallas kernels, head_call(): pl.pallas_call(kernel, out_shape=jax.ShapeDtypeStruct((blocks, 8, rows),...  34.5 us
    pallas_call x1, Pallas kernels, swiglu_call(): pl.pallas_call(kernel, out_shape=(half, half), grid_spec=pltpu.PrefetchSc...  16.9 us
    convert_element_type x4, other arithmetic, head_part(): block = (block.astype(F32) * row_gain).astype(BF)  10.9 us
  transfers between devices with their start and end apart: 55, of which 19 were waited for; matrix products, arithmetic and copies ran while one was open for 9% of the time, Pallas kernels for 21%

profile of v2, /device:TPU:0, one launch (start us, length us, event | category | flops | bytes accessed | tf_op | source)
XLA Modules:
  0.0 370.4 jit_solution(12721611213746094542)
XLA Ops:
  0.6 1.2 copy-done.3
  1.9 3.5 split.1
  5.3 3.0 collective-permute-start.5
  8.3 1.5 collective-permute-start.3
  10.6 2.6 collective-permute-start.1
  13.2 1.5 collective-permute-start
  16.6 1.2 multiply_convert_fusion.7
  17.9 2.0 multiply_convert_fusion.22
  21.2 1.3 collective-permute-start.4
  27.2 2.6 and_select_fusion.owners
  31.5 1.5 collective-permute-start.8
  35.8 1.2 copy-done.4
  37.0 2.9 qkv.1
  41.8 1.2 collective-permute-start.10
  43.1 9.8 %collective-permute-start.7 = (bf16[256,512]{1,0:T(8,128)(2,1)S(1)}, bf16[256,512]{1,0:T(8,128)(2,1)S(1)}, u32[]{:S(2)}, u32[]{:S(2)}) collective-permute-start(bf16[256,512]{1,0:T(8,128)(2,1)S(1)} %get-tuple-element.165.refs_0_), channel_id=1, source_target_pairs={{0,16},{4,20},{8,24},{12,28},{16,0},{20,4},{24,8},{28,12},{1,17},{... | collective-permute-start | bytes 786440 | tf_op jit(solution)/shard_map/ppermute | solution.py:31
  52.9 11.6 %attention_near.1 = (f32[4,64,512]{2,1,0:T(8,128)}, f32[4,1,512]{2,1,0:T(1,128)}) custom-call(s32[4,4]{1,0:T(4,128)} %get-tuple-element.135.flags, s32[4]{0:T(128)} %copy-done.49, bf16[256,512]{1,0:T(8,128)(2,1)} %copy-done.9, s32[4,1,512]{2,1,0:T(1,128)} %tile.27.refs_1_, bf16[2048,128]{1,0:T(8,128)(2,1)} %get-tuple-element.138.refs_2_, ...), custom_call_target="tpu_custom_call" | custom-call | flops 4294967296 | bytes 3145728 | tf_op jit(solution)/shard_map/attention_near/pallas_call | solution.py:327
  64.5 9.3 %collective-permute-done.7.refs_0_ = bf16[256,512]{1,0:T(8,128)(2,1)S(1)} collective-permute-done((bf16[256,512]{1,0:T(8,128)(2,1)S(1)}, bf16[256,512]{1,0:T(8,128)(2,1)S(1)}, u32[]{:S(2)}, u32[]{:S(2)}) %collective-permute-start.7) | collective-permute-done | bytes 262176 | tf_op jit(solution)/shard_map/ppermute | solution.py:31
  74.4 3.5 multiply_convert_fusion
  78.0 1.7 fusion.8
  79.7 1.5 collective-permute-start.13
  81.2 4.2 %multiply_convert_fusion.9 = (bf16[256,512]{1,0:T(8,128)(2,1)}, bf16[256,512]{1,0:T(8,128)(2,1)}, bf16[256,512]{1,0:T(8,128)(2,1)}, bf16[256,512]{1,0:T(8,128)(2...) fusion(bf16[256,16384]{1,0:T(8,128)(2,1)} %param.30, ...), kind=kLoop, calls=%fused_computation.33 | loop fusion | flops 5505024 | bytes 7341112 | tf_op jit(solution)/shard_map/convert_element_type | solution.py:741
  85.4 3.7 %collective-permute-done.11.refs_8_.refs_2_ = bf16[2048,128]{1,0:T(8,128)(2,1)} collective-permute-done((bf16[2048,128]{1,0:T(8,128)(2,1)}, bf16[2048,128]{1,0:T(8,128)(2,1)}, u32[]{:S(2)}, u32[]{:S(2)}) %collective-permute-start.11) | collective-permute-done | bytes 524320 | tf_op jit(solution)/shard_map/ppermute | solution.py:31
  89.1 17.3 %attention_far.1 = (bf16[4,80,512]{2,1,0:T(8,128)(2,1)}, f32[4,1,512]{2,1,0:T(1,128)}) custom-call(s32[4,4]{1,0:T(4,128)} %get-tuple-element.150.flags, s32[4]{0:T(128)} %copy-done.49, bf16[256,512]{1,0:T(8,128)(2,1)} %copy-done.63, s32[4,1,512]{2,1,0:T(1,128)} %tile.62.refs_1_, bf16[2048,128]{1,0:T(8,128)(2,1)} %get-tuple-element.138.refs_2_, ...), custom_call_target="tpu_custom_call" | custom-call | flops 4294967296 | bytes 4194304 | tf_op jit(solution)/shard_map/attention_far/pallas_call | solution.py:327
  106.4 5.1 %collective-permute-done.13.refs_9_.refs_25_.refs_17_ = bf16[272,1024]{1,0:T(8,128)(2,1)S(1)} collective-permute-done((bf16[272,1024]{1,0:T(8,128)(2,1)S(1)}, bf16[272,1024]{1,0:T(8,128)(2,1)S(1)}, u32[]{:S(2)}, u32[]{:S(2)}) %collective-permute-start.13) | collective-permute-done | bytes 557088 | tf_op jit(solution)/shard_map/ppermute | solution.py:765
  111.6 3.3 collective-permute-start.15
  115.7 7.7 %attention_rest.1 = (bf16[4,80,512]{2,1,0:T(8,128)(2,1)}, f32[4,1,512]{2,1,0:T(1,128)}) custom-call(s32[4,4]{1,0:T(4,128)} %get-tuple-element.135.flags, s32[4]{0:T(128)} %copy-done.49, bf16[256,512]{1,0:T(8,128)(2,1)} %copy-done.9, s32[4,1,512]{2,1,0:T(1,128)} %tile.27.refs_1_, bf16[2048,128]{1,0:T(8,128)(2,1)} %collective-permute-done.11.refs_8_.refs_2_, ...), custom_call_target="tpu_custom_call" | custom-call | flops 4294967296 | bytes 1048576 | tf_op jit(solution)/shard_map/attention_rest/pallas_call | solution.py:327
  123.4 16.2 %collective-permute-done.17.refs_20_ = bf16[256,512]{1,0:T(8,128)(2,1)} collective-permute-done((bf16[256,512]{1,0:T(8,128)(2,1)}, bf16[256,512]{1,0:T(8,128)(2,1)}, u32[]{:S(2)}, u32[]{:S(2)}) %collective-permute-start.17) | collective-permute-done | bytes 262176 | tf_op jit(solution)/shard_map/ppermute | solution.py:765
  140.7 1.7 project.1
  142.5 1.9 collective-permute-done.18
  144.5 1.6 collective-permute-start.19
  146.0 1.5 collective-permute-start.20
  147.6 3.3 collective-permute-start.21
  150.9 7.6 %collective-permute-done.19 = bf16[2,256,512]{2,1,0:T(8,128)(2,1)S(1)} collective-permute-done((bf16[2,256,512]{2,1,0:T(8,128)(2,1)S(1)}, bf16[2,256,512]{2,1,0:T(8,128)(2,1)S(1)}, u32[]{:S(2)}, u32[]{:S(2)}) %collective-permute-start.19) | collective-permute-done | bytes 524320 | tf_op jit(solution)/shard_map/ppermute | solution.py:31
  158.8 14.3 %collective-permute-done.20.refs_11_.refs_27_.refs_19_ = bf16[272,1024]{1,0:T(8,128)(2,1)S(1)} collective-permute-done((bf16[272,1024]{1,0:T(8,128)(2,1)S(1)}, bf16[272,1024]{1,0:T(8,128)(2,1)S(1)}, u32[]{:S(2)}, u32[]{:S(2)}) %collective-permute-start.20) | collective-permute-done | bytes 557088 | tf_op jit(solution)/shard_map/ppermute | solution.py:765
  173.1 2.2 collective-permute-done.21.refs_12_.refs_28_.refs_20_
  177.9 4.9 %collective-permute-start.23 = (bf16[272,1024]{1,0:T(8,128)(2,1)S(1)}, bf16[272,1024]{1,0:T(8,128)(2,1)S(1)}, u32[]{:S(2)}, u32[]{:S(2)}) collective-permute-start(bf16[272,1024]{1,0:T(8,128)(2,1)S(1)} %get-tuple-element.187), channel_id=1, source_target_pairs={{0,28},{4,24},{24,4},{28,0},{1,29},{5,25},{25,5},{29,1},{2,30},{6,... | collective-permute-start | bytes 1671176 | tf_op jit(solution)/shard_map/ppermute | solution.py:765
  183.7 16.9 %swiglu.1 = (bf16[2,256,512]{2,1,0:T(8,128)(2,1)}, bf16[2,256,512]{2,1,0:T(8,128)(2,1)}) custom-call(s32[2]{0:T(128)} %copy-done.8, bf16[2,256,512]{2,1,0:T(8,128)(2,1)} %copy-done.12, bf16[2,256,512]{2,1,0:T(8,128)(2,1)} %copy-done.21, f32[4,512]{1,0:T(4,128)} %reshape.233.gain, bf16[2048,2048]{1,0:T(8,128)(2,1)} %w_gate.1, bf16[2048,2048]{1,0:T(8,128)(2,1)} %w_up.1, ...), custom_call_target="tpu_custom_call" | custom-call | flops 6442450944 | bytes 25165824 | tf_op jit(solution)/shard_map/swiglu/pallas_call | solution.py:447
  200.6 4.3 %collective-permute-done.25.refs_21_ = bf16[256,512]{1,0:T(8,128)(2,1)S(1)} collective-permute-done((bf16[256,512]{1,0:T(8,128)(2,1)S(1)}, bf16[256,512]{1,0:T(8,128)(2,1)S(1)}, u32[]{:S(2)}, u32[]{:S(2)}) %collective-permute-start.25) | collective-permute-done | bytes 262176 | tf_op jit(solution)/shard_map/ppermute | solution.py:765
  205.0 2.1 collective-permute-done.26
  207.1 1.2 convert_add_fusion
  210.3 6.4 %collective-permute-done.27 = bf16[1,256,512]{2,1,0:T(8,128)(2,1)S(1)} collective-permute-done((bf16[1,256,512]{2,1,0:T(8,128)(2,1)S(1)}, bf16[1,256,512]{2,1,0:T(8,128)(2,1)S(1)}, u32[]{:S(2)}, u32[]{:S(2)}) %collective-permute-start.27) | collective-permute-done | bytes 262176 | tf_op jit(solution)/shard_map/ppermute | solution.py:31
  217.0 10.1 %collective-permute-start.31 = (bf16[1,256,512]{2,1,0:T(8,128)(2,1)S(1)}, bf16[1,256,512]{2,1,0:T(8,128)(2,1)S(1)}, u32[]{:S(2)}, u32[]{:S(2)}) collective-permute-start(bf16[1,256,512]{2,1,0:T(8,128)(2,1)S(1)} %bitcast.62), channel_id=1, source_target_pairs={{0,16},{4,20},{8,24},{12,28},{16,0},{20,4},{24,8},{28,12},{1,17},{... | collective-permute-start | bytes 786440 | tf_op jit(solution)/shard_map/ppermute | solution.py:31
  227.1 10.7 %collective-permute-done.31 = bf16[1,256,512]{2,1,0:T(8,128)(2,1)S(1)} collective-permute-done((bf16[1,256,512]{2,1,0:T(8,128)(2,1)S(1)}, bf16[1,256,512]{2,1,0:T(8,128)(2,1)S(1)}, u32[]{:S(2)}, u32[]{:S(2)}) %collective-permute-start.31) | collective-permute-done | bytes 262176 | tf_op jit(solution)/shard_map/ppermute | solution.py:31
  238.7 11.1 %collective-permute-done.32 = bf16[2,256,512]{2,1,0:T(8,128)(2,1)S(1)} collective-permute-done((bf16[2,256,512]{2,1,0:T(8,128)(2,1)S(1)}, bf16[2,256,512]{2,1,0:T(8,128)(2,1)S(1)}, u32[]{:S(2)}, u32[]{:S(2)}) %collective-permute-start.32) | collective-permute-done | bytes 524320 | tf_op jit(solution)/shard_map/ppermute | solution.py:31
  251.6 1.5 collective-permute-start.35
  253.1 4.6 %collective-permute-start.36 = (bf16[256,512]{1,0:T(8,128)(2,1)}, bf16[256,512]{1,0:T(8,128)(2,1)S(1)}, u32[]{:S(2)}, u32[]{:S(2)}) collective-permute-start(bf16[256,512]{1,0:T(8,128)(2,1)} %get-tuple-element.189), channel_id=1, source_target_pairs={{0,24},{4,28},{24,0},{28,4},{1,25},{5,29},{25,1},{29,5},{2,26},{6,... | collective-permute-start | bytes 786440 | tf_op jit(solution)/shard_map/ppermute | solution.py:765
  257.8 3.6 collective-permute-start.37
  261.4 5.0 %collective-permute-start.38 = (bf16[256,512]{1,0:T(8,128)(2,1)}, bf16[256,512]{1,0:T(8,128)(2,1)S(1)}, u32[]{:S(2)}, u32[]{:S(2)}) collective-permute-start(bf16[256,512]{1,0:T(8,128)(2,1)} %get-tuple-element.191), channel_id=1, source_target_pairs={{0,24},{4,28},{24,0},{28,4},{1,25},{5,29},{25,1},{29,5},{2,26},{6,... | collective-permute-start | bytes 786440 | tf_op jit(solution)/shard_map/ppermute | solution.py:765
  266.7 5.2 %collective-permute-done.37 = bf16[256,512]{1,0:T(8,128)(2,1)S(1)} collective-permute-done((bf16[256,512]{1,0:T(8,128)(2,1)S(1)}, bf16[256,512]{1,0:T(8,128)(2,1)S(1)}, u32[]{:S(2)}, u32[]{:S(2)}) %collective-permute-start.37) | collective-permute-done | bytes 262176 | tf_op jit(solution)/shard_map/ppermute | solution.py:765
  271.9 2.7 collective-permute-done.38
  274.7 1.2 collective-permute-start.40
  276.4 4.2 %collective-permute-start.41 = (bf16[272,1024]{1,0:T(8,128)(2,1)}, bf16[272,1024]{1,0:T(8,128)(2,1)}, u32[]{:S(2)}, u32[]{:S(2)}) collective-permute-start(bf16[272,1024]{1,0:T(8,128)(2,1)} %fusion.7), channel_id=1, source_target_pairs={{0,24},{4,28},{24,0},{28,4},{1,25},{5,29},{25,1},{29,5},{2,26},{6,... | collective-permute-start | bytes 1671176 | tf_op jit(solution)/shard_map/ppermute | solution.py:765
  280.6 2.4 collective-permute-start.43
  283.0 20.1 %collective-permute-done.42.refs_19_ = bf16[256,512]{1,0:T(8,128)(2,1)} collective-permute-done((bf16[256,512]{1,0:T(8,128)(2,1)}, bf16[256,512]{1,0:T(8,128)(2,1)}, u32[]{:S(2)}, u32[]{:S(2)}) %collective-permute-start.42) | collective-permute-done | bytes 262176 | tf_op jit(solution)/shard_map/ppermute | solution.py:765
  307.3 1.2 collective-permute-start.48
  308.6 1.9 broadcast_select_fusion.1.refs_14_.refs_30_.refs_22_
  310.6 2.3 collective-permute-start.50
  313.5 5.1 %collective-permute-start.52 = (bf16[256,512]{1,0:T(8,128)(2,1)S(1)}, bf16[256,512]{1,0:T(8,128)(2,1)S(1)}, u32[]{:S(2)}, u32[]{:S(2)}) collective-permute-start(bf16[256,512]{1,0:T(8,128)(2,1)S(1)} %copy-done.23), channel_id=1, source_target_pairs={{0,28},{4,24},{24,4},{28,0},{1,29},{5,25},{25,5},{29,1},{2,30},{6,... | collective-permute-start | bytes 786440 | tf_op jit(solution)/shard_map/ppermute | solution.py:765
  318.7 22.8 %head.2 = f32[8,8,256]{2,1,0:T(8,128)} custom-call(s32[2]{0:T(128)} %copy-done.8, bf16[1,2,4,128,512]{4,3,2,1,0:T(8,128)(2,1)} %copy-done.15, bf16[1,2,4,128,512]{4,3,2,1,0:T(8,128)(2,1)} %collective-permute-done.39.refs_1_, bf16[2,4,128,512]{3,2,1,0:T(8,128)(2,1)} %copy-done.16, bf16[2,4,128,512]{3,2,1,0:T(8,128)(2,1)} %collective-permute-done.40.refs_3_, ...), custom_call_target="tpu_custom_call" | custom-call | flops 12884901888 | bytes 14680064 | tf_op jit(solution)/shard_map/head/pallas_call | solution.py:639
  342.5 11.8 %head.3 = f32[8,8,256]{2,1,0:T(8,128)} custom-call(s32[2]{0:T(128)} %copy-done.8, bf16[1,2,4,128,512]{4,3,2,1,0:T(8,128)(2,1)} %copy-done.15, bf16[1,2,4,128,512]{4,3,2,1,0:T(8,128)(2,1)} %collective-permute-done.39.refs_1_, bf16[2,4,128,512]{3,2,1,0:T(8,128)(2,1)} %copy-done.16, bf16[2,4,128,512]{3,2,1,0:T(8,128)(2,1)} %collective-permute-done.40.refs_3_, ...), custom_call_target="tpu_custom_call" | custom-call | flops 4294967296 | bytes 10485760 | tf_op jit(solution)/shard_map/head/pallas_call | solution.py:639
  355.3 9.3 %all_to_all.5 = f32[8,3,256]{2,1,0:T(4,128)S(1)} all-to-all(f32[8,3,256]{2,1,0:T(4,128)S(1)} %pad_maximum_fusion.5), channel_id=1, replica_groups=mesh['req'=8,'mlp'=4] {'req'}, dimensions={0} | all-to-all | bytes 49152 | tf_op jit(solution)/shard_map/all_to_all | solution.py:953
  364.7 1.2 collective-permute-done.53
  365.9 1.6 collective-permute-start.54
  367.5 2.1 collective-permute-done.54
  (273 shorter events, 34.6 us)
Async XLA Ops:
  5.3 35.8 %collective-permute-start.5 = (bf16[2048,128]{1,0:T(8,128)(2,1)}, bf16[2048,128]{1,0:T(8,128)(2,1)}, u32[]{:S(2)}, u32[]{:S(2)}) collective-permute-start(bf16[2048,128]{1,0:T(8,128)(2,1)} %get-tuple-element.138.refs_2_), channel_id=1, source_target_pairs={{0,8},{4,12},{8,0},{12,4},{16,24},{20,28},{24,16},{28,20},{1,9},{5... | collective-permute-start | bytes 1572872 | tf_op jit(solution)/shard_map/ppermute | solution.py:31
  8.3 33.5 %collective-permute-start.3 = (bf16[2048,128]{1,0:T(8,128)(2,1)}, bf16[2048,128]{1,0:T(8,128)(2,1)}, u32[]{:S(2)}, u32[]{:S(2)}) collective-permute-start(bf16[2048,128]{1,0:T(8,128)(2,1)} %get-tuple-element.138.refs_2_), channel_id=1, source_target_pairs={{0,4},{4,0},{8,12},{12,8},{16,20},{20,16},{24,28},{28,24},{1,5},{5... | collective-permute-start | bytes 1572872 | tf_op jit(solution)/shard_map/ppermute | solution.py:31
  10.6 10.6 %collective-permute-start.1 = (s32[1,8]{1,0:T(1,128)S(1)}, s32[1,8]{1,0:T(1,128)S(1)}, u32[]{:S(2)}, u32[]{:S(2)}) collective-permute-start(s32[1,8]{1,0:T(1,128)S(1)} %pad_add_fusion), channel_id=1, source_target_pairs={{0,16},{4,20},{8,24},{12,28},{16,0},{20,4},{24,8},{28,12},{1,17},{... | collective-permute-start | bytes 104 | tf_op jit(solution)/shard_map/ppermute | solution.py:31
  13.2 9.3 %collective-permute-start = (bf16[256,512]{1,0:T(8,128)(2,1)}, bf16[256,512]{1,0:T(8,128)(2,1)S(1)}, u32[]{:S(2)}, u32[]{:S(2)}) collective-permute-start(bf16[256,512]{1,0:T(8,128)(2,1)} %refs_0_), channel_id=1, source_target_pairs={{0,2},{1,3},{2,0},{3,1},{4,6},{5,7},{6,4},{7,5},{8,10},{9,11},{10,... | collective-permute-start | bytes 786440 | tf_op jit(solution)/shard_map/ppermute | solution.py:31
  14.7 28.4 %collective-permute-start.6 = (bf16[128,2048]{1,0:T(8,128)(2,1)}, bf16[128,2048]{1,0:T(8,128)(2,1)}, u32[]{:S(2)}, u32[]{:S(2)}) collective-permute-start(bf16[128,2048]{1,0:T(8,128)(2,1)} %get-tuple-element.139.refs_3_), channel_id=1, source_target_pairs={{0,8},{4,12},{8,0},{12,4},{16,24},{20,28},{24,16},{28,20},{1,9},{5... | collective-permute-start | bytes 1572872 | tf_op jit(solution)/shard_map/ppermute | solution.py:31
  21.2 118.5 %copy-start.8 = (s32[2]{0:T(128)}, s32[2]{0:T(128)S(1)}, u32[]{:S(2)}) copy-start(s32[2]{0:T(128)S(1)} %pad_add_fusion.2.place) | copy-start | bytes 28
  21.2 21.9 %collective-permute-start.4 = (bf16[128,2048]{1,0:T(8,128)(2,1)}, bf16[128,2048]{1,0:T(8,128)(2,1)}, u32[]{:S(2)}, u32[]{:S(2)}) collective-permute-start(bf16[128,2048]{1,0:T(8,128)(2,1)} %get-tuple-element.139.refs_3_), channel_id=1, source_target_pairs={{0,4},{4,0},{8,12},{12,8},{16,20},{20,16},{24,28},{28,24},{1,5},{5... | collective-permute-start | bytes 1572872 | tf_op jit(solution)/shard_map/ppermute | solution.py:31
  24.1 6.6 %collective-permute-start.2 = (bf16[256,1024]{1,0:T(8,128)(2,1)}, bf16[256,1024]{1,0:T(8,128)(2,1)S(1)}, u32[]{:S(2)}, u32[]{:S(2)}) collective-permute-start(bf16[256,1024]{1,0:T(8,128)(2,1)} %pad_maximum_fusion.2), channel_id=1, source_target_pairs={{0,1},{1,0},{2,3},{3,2},{4,5},{5,4},{6,7},{7,6},{8,9},{9,8},{10,11... | collective-permute-start | bytes 1572872 | tf_op jit(solution)/shard_map/ppermute | solution.py:31
  31.5 42.9 %collective-permute-start.8 = (bf16[272,1024]{1,0:T(8,128)(2,1)}, bf16[272,1024]{1,0:T(8,128)(2,1)}, u32[]{:S(2)}, u32[]{:S(2)}) collective-permute-start(bf16[272,1024]{1,0:T(8,128)(2,1)} %fusion.7), channel_id=1, source_target_pairs={{8,16},{12,20},{16,8},{20,12},{9,17},{13,21},{17,9},{21,13},{10,18... | collective-permute-start | bytes 1671176 | tf_op jit(solution)/shard_map/ppermute | solution.py:765
  41.2 33.2 %collective-permute-start.9 = (bf16[256,512]{1,0:T(8,128)(2,1)}, bf16[256,512]{1,0:T(8,128)(2,1)S(1)}, u32[]{:S(2)}, u32[]{:S(2)}) collective-permute-start(bf16[256,512]{1,0:T(8,128)(2,1)} %get-tuple-element.189), channel_id=1, source_target_pairs={{8,16},{12,20},{16,8},{20,12},{9,17},{13,21},{17,9},{21,13},{10,18... | collective-permute-start | bytes 786440 | tf_op jit(solution)/shard_map/ppermute | solution.py:765
  41.8 32.6 %collective-permute-start.10 = (bf16[256,512]{1,0:T(8,128)(2,1)}, bf16[256,512]{1,0:T(8,128)(2,1)S(1)}, u32[]{:S(2)}, u32[]{:S(2)}) collective-permute-start(bf16[256,512]{1,0:T(8,128)(2,1)} %get-tuple-element.191), channel_id=1, source_target_pairs={{8,16},{12,20},{16,8},{20,12},{9,17},{13,21},{17,9},{21,13},{10,18... | collective-permute-start | bytes 786440 | tf_op jit(solution)/shard_map/ppermute | solution.py:765
  43.1 30.8 %collective-permute-start.7 = (bf16[256,512]{1,0:T(8,128)(2,1)S(1)}, bf16[256,512]{1,0:T(8,128)(2,1)S(1)}, u32[]{:S(2)}, u32[]{:S(2)}) collective-permute-start(bf16[256,512]{1,0:T(8,128)(2,1)S(1)} %get-tuple-element.165.refs_0_), channel_id=1, source_target_pairs={{0,16},{4,20},{8,24},{12,28},{16,0},{20,4},{24,8},{28,12},{1,17},{... | collective-permute-start | bytes 786440 | tf_op jit(solution)/shard_map/ppermute | solution.py:31
  52.9 32.5 %collective-permute-start.12 = (bf16[128,2048]{1,0:T(8,128)(2,1)}, bf16[128,2048]{1,0:T(8,128)(2,1)S(1)}, u32[]{:S(2)}, u32[]{:S(2)}) collective-permute-start(bf16[128,2048]{1,0:T(8,128)(2,1)} %collective-permute-done.4.refs_5_), channel_id=1, source_target_pairs={{0,8},{4,12},{8,0},{12,4},{16,24},{20,28},{24,16},{28,20},{1,9},{5... | collective-permute-start | bytes 1572872 | tf_op jit(solution)/shard_map/ppermute | solution.py:31
  73.9 15.2 %collective-permute-start.11 = (bf16[2048,128]{1,0:T(8,128)(2,1)}, bf16[2048,128]{1,0:T(8,128)(2,1)}, u32[]{:S(2)}, u32[]{:S(2)}) collective-permute-start(bf16[2048,128]{1,0:T(8,128)(2,1)} %collective-permute-done.5.refs_6_), channel_id=1, source_target_pairs={{0,4},{4,0},{8,12},{12,8},{16,20},{20,16},{24,28},{28,24},{1,5},{5... | collective-permute-start | bytes 1572872 | tf_op jit(solution)/shard_map/ppermute | solution.py:31
  79.7 31.9 %collective-permute-start.13 = (bf16[272,1024]{1,0:T(8,128)(2,1)S(1)}, bf16[272,1024]{1,0:T(8,128)(2,1)S(1)}, u32[]{:S(2)}, u32[]{:S(2)}) collective-permute-start(bf16[272,1024]{1,0:T(8,128)(2,1)S(1)} %get-tuple-element.162), channel_id=1, source_target_pairs={{0,4},{4,0},{8,12},{12,8},{16,20},{20,16},{24,28},{28,24},{1,5},{5... | collective-permute-start | bytes 1671176 | tf_op jit(solution)/shard_map/ppermute | solution.py:765
  81.2 30.4 %collective-permute-start.14 = (bf16[272,1024]{1,0:T(8,128)(2,1)S(1)}, bf16[272,1024]{1,0:T(8,128)(2,1)S(1)}, u32[]{:S(2)}, u32[]{:S(2)}) collective-permute-start(bf16[272,1024]{1,0:T(8,128)(2,1)S(1)} %get-tuple-element.163), channel_id=1, source_target_pairs={{0,20},{4,16},{8,28},{12,24},{16,4},{20,0},{24,12},{28,8},{1,21},{... | collective-permute-start | bytes 1671176 | tf_op jit(solution)/shard_map/ppermute | solution.py:765
  111.5 28.2 %copy-start.7 = (f32[4,1,512]{2,1,0:T(1,128)S(1)}, f32[4,1,512]{2,1,0:T(1,128)}, u32[]{:S(2)}) copy-start(f32[4,1,512]{2,1,0:T(1,128)} %get-tuple-element.149.lse_one) | copy-start | bytes 24580
  111.5 28.1 %collective-permute-start.16 = (bf16[272,1024]{1,0:T(8,128)(2,1)}, bf16[272,1024]{1,0:T(8,128)(2,1)}, u32[]{:S(2)}, u32[]{:S(2)}) collective-permute-start(bf16[272,1024]{1,0:T(8,128)(2,1)} %get-tuple-element.167), channel_id=1, source_target_pairs={{0,8},{4,12},{8,0},{12,4},{16,24},{20,28},{24,16},{28,20},{1,9},{5... | collective-permute-start | bytes 1671176 | tf_op jit(solution)/shard_map/ppermute | solution.py:765
  111.6 28.0 %collective-permute-start.15 = (bf16[4,80,512]{2,1,0:T(8,128)(2,1)}, bf16[4,80,512]{2,1,0:T(8,128)(2,1)S(1)}, u32[]{:S(2)}, u32[]{:S(2)}) collective-permute-start(bf16[4,80,512]{2,1,0:T(8,128)(2,1)} %get-tuple-element.164), channel_id=1, source_target_pairs={{0,16},{4,20},{8,24},{12,28},{16,0},{20,4},{24,8},{28,12},{1,17},{... | collective-permute-start | bytes 983048 | tf_op jit(solution)/shard_map/ppermute | solution.py:31
  114.9 24.8 %collective-permute-start.17 = (bf16[256,512]{1,0:T(8,128)(2,1)}, bf16[256,512]{1,0:T(8,128)(2,1)}, u32[]{:S(2)}, u32[]{:S(2)}) collective-permute-start(bf16[256,512]{1,0:T(8,128)(2,1)} %get-tuple-element.168), channel_id=1, source_target_pairs={{0,16},{4,20},{8,24},{12,28},{16,0},{20,4},{24,8},{28,12},{1,17},{... | collective-permute-start | bytes 786440 | tf_op jit(solution)/shard_map/ppermute | solution.py:765
  142.4 2.0 collective-permute-start.18
  144.5 14.0 %collective-permute-start.19 = (bf16[2,256,512]{2,1,0:T(8,128)(2,1)S(1)}, bf16[2,256,512]{2,1,0:T(8,128)(2,1)S(1)}, u32[]{:S(2)}, u32[]{:S(2)}) collective-permute-start(bf16[2,256,512]{2,1,0:T(8,128)(2,1)S(1)} %add_convert_fusion.1), channel_id=1, source_target_pairs={{0,2},{1,3},{2,0},{3,1},{4,6},{5,7},{6,4},{7,5},{8,10},{9,11},{10,... | collective-permute-start | bytes 1572872 | tf_op jit(solution)/shard_map/ppermute | solution.py:31
  146.0 27.0 %collective-permute-start.20 = (bf16[272,1024]{1,0:T(8,128)(2,1)S(1)}, bf16[272,1024]{1,0:T(8,128)(2,1)S(1)}, u32[]{:S(2)}, u32[]{:S(2)}) collective-permute-start(bf16[272,1024]{1,0:T(8,128)(2,1)S(1)} %copy-done.18), channel_id=1, source_target_pairs={{0,12},{4,8},{8,4},{12,0},{16,28},{20,24},{24,20},{28,16},{1,13},{... | collective-permute-start | bytes 1671176 | tf_op jit(solution)/shard_map/ppermute | solution.py:765
  147.6 27.6 %collective-permute-start.21 = (bf16[272,1024]{1,0:T(8,128)(2,1)S(1)}, bf16[272,1024]{1,0:T(8,128)(2,1)S(1)}, u32[]{:S(2)}, u32[]{:S(2)}) collective-permute-start(bf16[272,1024]{1,0:T(8,128)(2,1)S(1)} %copy-done.17), channel_id=1, source_target_pairs={{0,16},{4,20},{8,24},{12,28},{16,0},{20,4},{24,8},{28,12},{1,17},{... | collective-permute-start | bytes 1671176 | tf_op jit(solution)/shard_map/ppermute | solution.py:765
  176.1 6.7 %collective-permute-start.22 = (bf16[2,256,512]{2,1,0:T(8,128)(2,1)S(1)}, bf16[2,256,512]{2,1,0:T(8,128)(2,1)S(1)}, u32[]{:S(2)}, u32[]{:S(2)}) collective-permute-start(bf16[2,256,512]{2,1,0:T(8,128)(2,1)S(1)} %add_convert_fusion.ours), channel_id=1, source_target_pairs={{0,1},{1,0},{2,3},{3,2},{4,5},{5,4},{6,7},{7,6},{8,9},{9,8},{10,11... | collective-permute-start | bytes 1572872 | tf_op jit(solution)/shard_map/ppermute | solution.py:31
  176.7 23.8 %collective-permute-start.24 = (bf16[256,512]{1,0:T(8,128)(2,1)S(1)}, bf16[256,512]{1,0:T(8,128)(2,1)S(1)}, u32[]{:S(2)}, u32[]{:S(2)}) collective-permute-start(bf16[256,512]{1,0:T(8,128)(2,1)S(1)} %copy-done.31), channel_id=1, source_target_pairs={{0,4},{4,0},{8,12},{12,8},{16,20},{20,16},{24,28},{28,24},{1,5},{5... | collective-permute-start | bytes 786440 | tf_op jit(solution)/shard_map/ppermute | solution.py:765
  177.3 27.6 %collective-permute-start.25 = (bf16[256,512]{1,0:T(8,128)(2,1)S(1)}, bf16[256,512]{1,0:T(8,128)(2,1)S(1)}, u32[]{:S(2)}, u32[]{:S(2)}) collective-permute-start(bf16[256,512]{1,0:T(8,128)(2,1)S(1)} %copy-done.30), channel_id=1, source_target_pairs={{0,20},{4,16},{8,28},{12,24},{16,4},{20,0},{24,12},{28,8},{1,21},{... | collective-permute-start | bytes 786440 | tf_op jit(solution)/shard_map/ppermute | solution.py:765
  177.9 27.0 %collective-permute-start.23 = (bf16[272,1024]{1,0:T(8,128)(2,1)S(1)}, bf16[272,1024]{1,0:T(8,128)(2,1)S(1)}, u32[]{:S(2)}, u32[]{:S(2)}) collective-permute-start(bf16[272,1024]{1,0:T(8,128)(2,1)S(1)} %get-tuple-element.187), channel_id=1, source_target_pairs={{0,28},{4,24},{24,4},{28,0},{1,29},{5,25},{25,5},{29,1},{2,30},{6,... | collective-permute-start | bytes 1671176 | tf_op jit(solution)/shard_map/ppermute | solution.py:765
  204.9 2.2 collective-permute-start.26
  208.3 8.4 %collective-permute-start.27 = (bf16[1,256,512]{2,1,0:T(8,128)(2,1)S(1)}, bf16[1,256,512]{2,1,0:T(8,128)(2,1)S(1)}, u32[]{:S(2)}, u32[]{:S(2)}) collective-permute-start(bf16[1,256,512]{2,1,0:T(8,128)(2,1)S(1)} %slice.168), channel_id=1, source_target_pairs={{0,2},{1,3},{2,0},{3,1},{4,6},{5,7},{6,4},{7,5},{8,10},{9,11},{10,... | collective-permute-start | bytes 786440 | tf_op jit(solution)/shard_map/ppermute | solution.py:31
  208.9 8.1 %collective-permute-start.28 = (bf16[256,512]{1,0:T(8,128)(2,1)S(1)}, bf16[256,512]{1,0:T(8,128)(2,1)S(1)}, u32[]{:S(2)}, u32[]{:S(2)}) collective-permute-start(bf16[256,512]{1,0:T(8,128)(2,1)S(1)} %copy-done.29), channel_id=1, source_target_pairs={{0,8},{4,12},{8,0},{12,4},{16,24},{20,28},{24,16},{28,20},{1,9},{5... | collective-permute-start | bytes 786440 | tf_op jit(solution)/shard_map/ppermute | solution.py:765
  208.9 8.1 %collective-permute-start.29 = (bf16[256,512]{1,0:T(8,128)(2,1)S(1)}, bf16[256,512]{1,0:T(8,128)(2,1)S(1)}, u32[]{:S(2)}, u32[]{:S(2)}) collective-permute-start(bf16[256,512]{1,0:T(8,128)(2,1)S(1)} %copy-done.28), channel_id=1, source_target_pairs={{8,20},{12,16},{16,12},{20,8},{9,21},{13,17},{17,13},{21,9},{10,22... | collective-permute-start | bytes 786440 | tf_op jit(solution)/shard_map/ppermute | solution.py:765
  209.6 7.4 %collective-permute-start.30 = (bf16[256,512]{1,0:T(8,128)(2,1)S(1)}, bf16[256,512]{1,0:T(8,128)(2,1)S(1)}, u32[]{:S(2)}, u32[]{:S(2)}) collective-permute-start(bf16[256,512]{1,0:T(8,128)(2,1)S(1)} %copy-done.23), channel_id=1, source_target_pairs={{8,20},{12,16},{16,12},{20,8},{9,21},{13,17},{17,13},{21,9},{10,22... | collective-permute-start | bytes 786440 | tf_op jit(solution)/shard_map/ppermute | solution.py:765
  216.9 33.1 %copy-start.14 = (bf16[256,512]{1,0:T(8,128)(2,1)}, bf16[256,512]{1,0:T(8,128)(2,1)S(1)}, u32[]{:S(2)}) copy-start(bf16[256,512]{1,0:T(8,128)(2,1)S(1)} %fusion.11) | copy-start | bytes 786436
  217.0 32.9 %copy-start.62 = (bf16[256,512]{1,0:T(8,128)(2,1)}, bf16[256,512]{1,0:T(8,128)(2,1)S(1)}, u32[]{:S(2)}) copy-start(bf16[256,512]{1,0:T(8,128)(2,1)S(1)} %collective-permute-done.28.refs_18_) | copy-start | bytes 786436
  217.0 32.9 %copy-start.38 = (bf16[256,512]{1,0:T(8,128)(2,1)}, bf16[256,512]{1,0:T(8,128)(2,1)S(1)}, u32[]{:S(2)}) copy-start(bf16[256,512]{1,0:T(8,128)(2,1)S(1)} %collective-permute-done.29) | copy-start | bytes 786436
  217.0 32.9 %copy-start.36 = (bf16[256,512]{1,0:T(8,128)(2,1)}, bf16[256,512]{1,0:T(8,128)(2,1)S(1)}, u32[]{:S(2)}) copy-start(bf16[256,512]{1,0:T(8,128)(2,1)S(1)} %collective-permute-done.30) | copy-start | bytes 786436
  217.0 20.9 %collective-permute-start.31 = (bf16[1,256,512]{2,1,0:T(8,128)(2,1)S(1)}, bf16[1,256,512]{2,1,0:T(8,128)(2,1)S(1)}, u32[]{:S(2)}, u32[]{:S(2)}) collective-permute-start(bf16[1,256,512]{2,1,0:T(8,128)(2,1)S(1)} %bitcast.62), channel_id=1, source_target_pairs={{0,16},{4,20},{8,24},{12,28},{16,0},{20,4},{24,8},{28,12},{1,17},{... | collective-permute-start | bytes 786440 | tf_op jit(solution)/shard_map/ppermute | solution.py:31
  237.9 11.9 %collective-permute-start.32 = (bf16[2,256,512]{2,1,0:T(8,128)(2,1)S(1)}, bf16[2,256,512]{2,1,0:T(8,128)(2,1)S(1)}, u32[]{:S(2)}, u32[]{:S(2)}) collective-permute-start(bf16[2,256,512]{2,1,0:T(8,128)(2,1)S(1)} %maximum_bitcast_fusion.1), channel_id=1, source_target_pairs={{0,8},{4,12},{8,0},{12,4},{16,24},{20,28},{24,16},{28,20},{1,9},{5... | collective-permute-start | bytes 1572872 | tf_op jit(solution)/shard_map/ppermute | solution.py:31
  238.0 12.0 %collective-permute-start.33 = (bf16[272,1024]{1,0:T(8,128)(2,1)S(1)}, bf16[272,1024]{1,0:T(8,128)(2,1)S(1)}, u32[]{:S(2)}, u32[]{:S(2)}) collective-permute-start(bf16[272,1024]{1,0:T(8,128)(2,1)S(1)} %get-tuple-element.187), channel_id=1, source_target_pairs={{8,20},{12,16},{16,12},{20,8},{9,21},{13,17},{17,13},{21,9},{10,22... | collective-permute-start | bytes 1671176 | tf_op jit(solution)/shard_map/ppermute | solution.py:765
  250.8 15.7 %collective-permute-start.34 = (bf16[4,128,512]{2,1,0:T(8,128)(2,1)S(1)}, bf16[4,128,512]{2,1,0:T(8,128)(2,1)S(1)}, u32[]{:S(2)}, u32[]{:S(2)}) collective-permute-start(bf16[4,128,512]{2,1,0:T(8,128)(2,1)S(1)} %get-tuple-element.265), channel_id=1, source_target_pairs={{0,4},{4,0},{8,12},{12,8},{16,20},{20,16},{24,28},{28,24},{1,5},{5... | collective-permute-start | bytes 1572872 | tf_op jit(solution)/shard_map/ppermute | solution.py:31
  251.6 14.9 %collective-permute-start.35 = (bf16[1,4,128,512]{3,2,1,0:T(8,128)(2,1)S(1)}, bf16[1,4,128,512]{3,2,1,0:T(8,128)(2,1)S(1)}, u32[]{:S(2)}, u32[]{:S(2)}) collective-permute-start(bf16[1,4,128,512]{3,2,1,0:T(8,128)(2,1)S(1)} %get-tuple-element.263), channel_id=1, source_target_pairs={{0,2},{1,3},{2,0},{3,1},{4,6},{5,7},{6,4},{7,5},{8,10},{9,11},{10,... | collective-permute-start | bytes 1572872 | tf_op jit(solution)/shard_map/ppermute | solution.py:31
  253.1 13.6 %collective-permute-start.36 = (bf16[256,512]{1,0:T(8,128)(2,1)}, bf16[256,512]{1,0:T(8,128)(2,1)S(1)}, u32[]{:S(2)}, u32[]{:S(2)}) collective-permute-start(bf16[256,512]{1,0:T(8,128)(2,1)} %get-tuple-element.189), channel_id=1, source_target_pairs={{0,24},{4,28},{24,0},{28,4},{1,25},{5,29},{25,1},{29,5},{2,26},{6,... | collective-permute-start | bytes 786440 | tf_op jit(solution)/shard_map/ppermute | solution.py:765
  257.8 14.1 %collective-permute-start.37 = (bf16[256,512]{1,0:T(8,128)(2,1)S(1)}, bf16[256,512]{1,0:T(8,128)(2,1)S(1)}, u32[]{:S(2)}, u32[]{:S(2)}) collective-permute-start(bf16[256,512]{1,0:T(8,128)(2,1)S(1)} %copy-done.28), channel_id=1, source_target_pairs={{0,28},{4,24},{24,4},{28,0},{1,29},{5,25},{25,5},{29,1},{2,30},{6,... | collective-permute-start | bytes 786440 | tf_op jit(solution)/shard_map/ppermute | solution.py:765
  261.4 13.2 %collective-permute-start.38 = (bf16[256,512]{1,0:T(8,128)(2,1)}, bf16[256,512]{1,0:T(8,128)(2,1)S(1)}, u32[]{:S(2)}, u32[]{:S(2)}) collective-permute-start(bf16[256,512]{1,0:T(8,128)(2,1)} %get-tuple-element.191), channel_id=1, source_target_pairs={{0,24},{4,28},{24,0},{28,4},{1,25},{5,29},{25,1},{29,5},{2,26},{6,... | collective-permute-start | bytes 786440 | tf_op jit(solution)/shard_map/ppermute | solution.py:765
  266.6 38.5 %copy-start.15 = (bf16[1,2,4,128,512]{4,3,2,1,0:T(8,128)(2,1)}, bf16[1,2,4,128,512]{4,3,2,1,0:T(8,128)(2,1)S(1)}, u32[]{:S(2)}) copy-start(bf16[1,2,4,128,512]{4,3,2,1,0:T(8,128)(2,1)S(1)} %maximum_bitcast_fusion.refs_0_) | copy-start | bytes 3145732
  266.6 37.6 %copy-start.20 = (bf16[272,1024]{1,0:T(8,128)(2,1)S(1)}, bf16[272,1024]{1,0:T(8,128)(2,1)}, u32[]{:S(2)}) copy-start(bf16[272,1024]{1,0:T(8,128)(2,1)} %copy-done.19) | copy-start | bytes 1671172
  266.7 39.1 %copy-start.16 = (bf16[2,4,128,512]{3,2,1,0:T(8,128)(2,1)}, bf16[2,4,128,512]{3,2,1,0:T(8,128)(2,1)S(1)}, u32[]{:S(2)}) copy-start(bf16[2,4,128,512]{3,2,1,0:T(8,128)(2,1)S(1)} %pad_maximum_fusion.1.refs_2_) | copy-start | bytes 3145732
  274.7 29.0 %collective-permute-start.40 = (bf16[2,4,128,512]{3,2,1,0:T(8,128)(2,1)S(1)}, bf16[2,4,128,512]{3,2,1,0:T(8,128)(2,1)}, u32[]{:S(2)}, u32[]{:S(2)}) collective-permute-start(bf16[2,4,128,512]{3,2,1,0:T(8,128)(2,1)S(1)} %pad_maximum_fusion.1.refs_2_), channel_id=1, source_target_pairs={{0,4},{4,0},{8,12},{12,8},{16,20},{20,16},{24,28},{28,24},{1,5},{5... | collective-permute-start | bytes 3145736 | tf_op jit(solution)/shard_map/ppermute | solution.py:31
  275.8 27.8 %collective-permute-start.39 = (bf16[1,2,4,128,512]{4,3,2,1,0:T(8,128)(2,1)S(1)}, bf16[1,2,4,128,512]{4,3,2,1,0:T(8,128)(2,1)}, u32[]{:S(2)}, u32[]{:S(2)}) collective-permute-start(bf16[1,2,4,128,512]{4,3,2,1,0:T(8,128)(2,1)S(1)} %maximum_bitcast_fusion.refs_0_), channel_id=1, source_target_pairs={{0,2},{1,3},{2,0},{3,1},{4,6},{5,7},{6,4},{7,5},{8,10},{9,11},{10,... | collective-permute-start | bytes 3145736 | tf_op jit(solution)/shard_map/ppermute | solution.py:31
  276.4 27.3 %collective-permute-start.41 = (bf16[272,1024]{1,0:T(8,128)(2,1)}, bf16[272,1024]{1,0:T(8,128)(2,1)}, u32[]{:S(2)}, u32[]{:S(2)}) collective-permute-start(bf16[272,1024]{1,0:T(8,128)(2,1)} %fusion.7), channel_id=1, source_target_pairs={{0,24},{4,28},{24,0},{28,4},{1,25},{5,29},{25,1},{29,5},{2,26},{6,... | collective-permute-start | bytes 1671176 | tf_op jit(solution)/shard_map/ppermute | solution.py:765
  280.5 22.6 %collective-permute-start.42 = (bf16[256,512]{1,0:T(8,128)(2,1)}, bf16[256,512]{1,0:T(8,128)(2,1)}, u32[]{:S(2)}, u32[]{:S(2)}) collective-permute-start(bf16[256,512]{1,0:T(8,128)(2,1)} %get-tuple-element.195), channel_id=1, source_target_pairs={{0,12},{4,8},{8,4},{12,0},{16,28},{20,24},{24,20},{28,16},{1,13},{... | collective-permute-start | bytes 786440 | tf_op jit(solution)/shard_map/ppermute | solution.py:765
  280.6 22.5 %collective-permute-start.43 = (bf16[256,512]{1,0:T(8,128)(2,1)}, bf16[256,512]{1,0:T(8,128)(2,1)}, u32[]{:S(2)}, u32[]{:S(2)}) collective-permute-start(bf16[256,512]{1,0:T(8,128)(2,1)} %get-tuple-element.196), channel_id=1, source_target_pairs={{0,16},{4,20},{8,24},{12,28},{16,0},{20,4},{24,8},{28,12},{1,17},{... | collective-permute-start | bytes 786440 | tf_op jit(solution)/shard_map/ppermute | solution.py:765
  303.1 7.4 %collective-permute-start.46 = (bf16[2,4,128,512]{3,2,1,0:T(8,128)(2,1)S(1)}, bf16[2,4,128,512]{3,2,1,0:T(8,128)(2,1)S(1)}, u32[]{:S(2)}, u32[]{:S(2)}) collective-permute-start(bf16[2,4,128,512]{3,2,1,0:T(8,128)(2,1)S(1)} %pad_maximum_fusion.1.refs_2_), channel_id=1, source_target_pairs={{0,1},{1,0},{2,3},{3,2},{4,5},{5,4},{6,7},{7,6},{8,9},{9,8},{10,11... | collective-permute-start | bytes 3145736 | tf_op jit(solution)/shard_map/ppermute | solution.py:31
  303.1 7.5 %collective-permute-start.44 = (bf16[1,2,4,128,512]{4,3,2,1,0:T(8,128)(2,1)S(1)}, bf16[1,2,4,128,512]{4,3,2,1,0:T(8,128)(2,1)S(1)}, u32[]{:S(2)}, u32[]{:S(2)}) collective-permute-start(bf16[1,2,4,128,512]{4,3,2,1,0:T(8,128)(2,1)S(1)} %maximum_bitcast_fusion.refs_0_), channel_id=1, source_target_pairs={{0,1},{1,0},{2,3},{3,2},{4,5},{5,4},{6,7},{7,6},{8,9},{9,8},{10,11... | collective-permute-start | bytes 3145736 | tf_op jit(solution)/shard_map/ppermute | solution.py:31
  303.6 9.3 %collective-permute-start.47 = (bf16[2,4,128,512]{3,2,1,0:T(8,128)(2,1)}, bf16[2,4,128,512]{3,2,1,0:T(8,128)(2,1)S(1)}, u32[]{:S(2)}, u32[]{:S(2)}) collective-permute-start(bf16[2,4,128,512]{3,2,1,0:T(8,128)(2,1)} %collective-permute-done.40.refs_3_), channel_id=1, source_target_pairs={{0,1},{1,0},{2,3},{3,2},{4,5},{5,4},{6,7},{7,6},{8,9},{9,8},{10,11... | collective-permute-start | bytes 3145736 | tf_op jit(solution)/shard_map/ppermute | solution.py:31
  303.7 9.8 %collective-permute-start.45 = (bf16[1,2,4,128,512]{4,3,2,1,0:T(8,128)(2,1)}, bf16[1,2,4,128,512]{4,3,2,1,0:T(8,128)(2,1)S(1)}, u32[]{:S(2)}, u32[]{:S(2)}) collective-permute-start(bf16[1,2,4,128,512]{4,3,2,1,0:T(8,128)(2,1)} %collective-permute-done.39.refs_1_), channel_id=1, source_target_pairs={{0,1},{1,0},{2,3},{3,2},{4,5},{5,4},{6,7},{7,6},{8,9},{9,8},{10,11... | collective-permute-start | bytes 3145736 | tf_op jit(solution)/shard_map/ppermute | solution.py:31
  307.3 34.1 %collective-permute-start.48 = (bf16[256,512]{1,0:T(8,128)(2,1)S(1)}, bf16[256,512]{1,0:T(8,128)(2,1)}, u32[]{:S(2)}, u32[]{:S(2)}) collective-permute-start(bf16[256,512]{1,0:T(8,128)(2,1)S(1)} %copy-done.27), channel_id=1, source_target_pairs={{0,4},{4,0},{8,12},{12,8},{16,20},{20,16},{24,28},{28,24},{1,5},{5... | collective-permute-start | bytes 786440 | tf_op jit(solution)/shard_map/ppermute | solution.py:765
  310.5 31.0 %collective-permute-start.49 = (bf16[256,512]{1,0:T(8,128)(2,1)S(1)}, bf16[256,512]{1,0:T(8,128)(2,1)S(1)}, u32[]{:S(2)}, u32[]{:S(2)}) collective-permute-start(bf16[256,512]{1,0:T(8,128)(2,1)S(1)} %copy-done.26), channel_id=1, source_target_pairs={{0,8},{4,12},{8,0},{12,4},{16,24},{20,28},{24,16},{28,20},{1,9},{5... | collective-permute-start | bytes 786440 | tf_op jit(solution)/shard_map/ppermute | solution.py:765
  310.6 30.9 %collective-permute-start.50 = (bf16[256,512]{1,0:T(8,128)(2,1)S(1)}, bf16[256,512]{1,0:T(8,128)(2,1)S(1)}, u32[]{:S(2)}, u32[]{:S(2)}) collective-permute-start(bf16[256,512]{1,0:T(8,128)(2,1)S(1)} %copy-done.25), channel_id=1, source_target_pairs={{0,12},{4,8},{8,4},{12,0},{16,28},{20,24},{24,20},{28,16},{1,13},{... | collective-permute-start | bytes 786440 | tf_op jit(solution)/shard_map/ppermute | solution.py:765
  312.9 28.6 %collective-permute-start.51 = (bf16[256,512]{1,0:T(8,128)(2,1)S(1)}, bf16[256,512]{1,0:T(8,128)(2,1)S(1)}, u32[]{:S(2)}, u32[]{:S(2)}) collective-permute-start(bf16[256,512]{1,0:T(8,128)(2,1)S(1)} %copy-done.24), channel_id=1, source_target_pairs={{0,20},{4,16},{8,28},{12,24},{16,4},{20,0},{24,12},{28,8},{1,21},{... | collective-permute-start | bytes 786440 | tf_op jit(solution)/shard_map/ppermute | solution.py:765
  313.5 28.0 %collective-permute-start.52 = (bf16[256,512]{1,0:T(8,128)(2,1)S(1)}, bf16[256,512]{1,0:T(8,128)(2,1)S(1)}, u32[]{:S(2)}, u32[]{:S(2)}) collective-permute-start(bf16[256,512]{1,0:T(8,128)(2,1)S(1)} %copy-done.23), channel_id=1, source_target_pairs={{0,28},{4,24},{24,4},{28,0},{1,29},{5,25},{25,5},{29,1},{2,30},{6,... | collective-permute-start | bytes 786440 | tf_op jit(solution)/shard_map/ppermute | solution.py:765
  364.6 1.2 collective-permute-start.53
  365.9 3.7 collective-permute-start.54
  (62 other events, 455.9 us)

commit v3 on v2

--- a/solution.py
+++ b/solution.py
@@ -777,7 +777,7 @@
         return event
 
     far_rest = [k for _, k in far(0, 2) if k != half + half // 2]
-    early = [(part, half + half // 2) for part in range(3)]
+    early = [(part, half + half // 2) for part in range(2)]
     head_out.update({unit: head_part(*unit, w_head) for unit in early})
     sent_start = send(early, tokens, "inner")
 
@@ -863,7 +863,7 @@
     def over_cores(kept, sent):
         return kept.astype(F32) + swap(sent, "mlp", 1).astype(F32)
 
-    sent_one = send(far(0, 0) + near(0, 2), kept)
+    sent_one = send(far(0, 0) + near(0, 2) + near(2, 0), kept)
     summed = over_cores(kept, sent)
     x_bits = [b // 2 for b in bits_of(parts) if b > 1]
     for bit in x_bits:
@@ -879,7 +879,7 @@
     kept, sent = arrive(
         sent_one, swiglu_call(place, mid, mid_other, mlp_gain, w_gate, w_up, w_down)
     )
-    sent_one = {**send(near(1, 1), kept), **send(far(1, 3) + far(2, 3), kept, "inner")}
+    sent_one = {**send(near(1, 1) + near(2, 1), kept), **send(far(1, 3) + far(2, 3), kept, "inner")}
     summed = over_cores(kept, sent)
     for bit in x_bits:
         got = swap(summed[bit:].astype(BF), "mlp", 2 * bit)
@@ -901,7 +901,7 @@
         if last:
             spread = arrive(sent_one, spread)
     middle = half + half // 2
-    sent_one = send([(1, middle), (2, middle)] + far(1, 3), spread, "outer")
+    sent_one = send([(1, middle)] + far(1, 3), spread, "outer")
     top_rows, low_rows = spread[:, : rows // 2], spread[:, rows // 2 :]
 
     x_count = parts // 2
@@ -925,9 +925,9 @@
     sent_one.update(send(others, top_rows))
     top_more, low_more = arrive(sent_one, (top_more, low_more))
     sent_last = {
-        **send(far(2, 1), top_more),
+        **send(far(2, 1) + [(2, middle)], top_more),
         **send(far(2, 3), top_more, "outer"),
-        **send(near(2, 0) + near(2, 1) + near(2, 2), top_more),
+        **send(near(2, 2), top_more),
     }
     hidden = [top_rows, top_more, low_rows, low_more]
     hidden = hidden + [swap(values, "mlp", 1) for values in hidden]

time: 377 us -> 360 us (0.955)
  starting transfers between devices: 91.2 us -> 80.8 us
  waiting for transfers between devices: 126 us -> 119 us
    ppermute x28, starting transfers between devices: 43.3 us -> 34.3 us  [swap(): return lax.ppermute(values, axis, [(i, i ^ bit) for i in range(size)])]
    ppermute x28, waiting for transfers between devices: 56.3 us -> 51.6 us  [swap(): return lax.ppermute(values, axis, [(i, i ^ bit) for i in range(size)])]
    ppermute x27 -> x26, waiting for transfers between devices: 70.2 us -> 67.2 us  [send(): sent[unit] = (where, lax.ppermute(block, 'req', pairs))]
    ppermute x27 -> x26, starting transfers between devices: 47.9 us -> 46.5 us  [send(): sent[unit] = (where, lax.ppermute(block, 'req', pairs))]
  transfers between devices with their start and end apart: 55 -> 54, of which waited for: 19 -> 21; matrix products, arithmetic and copies ran while one was open for 9% -> 9% of each run, Pallas kernels for 21% -> 23%
where the time goes in v3:
time: 360 us; the launch traced here: 355 us
  waiting for transfers between devices  119 us (33%)
  Pallas kernels  98.1 us (27%)
  starting transfers between devices  80.8 us (22%)
  other arithmetic  28.1 us (8%)
  local copies, waits for them, and re-layouts  17.3 us (5%)
  blocking collectives  9.89 us (3%)
    ppermute x26, waiting for transfers between devices, send(): sent[unit] = (where, lax.ppermute(block, 'req', pairs))  67.2 us
    ppermute x28, waiting for transfers between devices, swap(): return lax.ppermute(values, axis, [(i, i ^ bit) for i in range(size)])  51.6 us
    ppermute x26, starting transfers between devices, send(): sent[unit] = (where, lax.ppermute(block, 'req', pairs))  46.5 us
    pallas_call x3, Pallas kernels, attention_call(): pl.pallas_call(kernel, out_shape=(jax.ShapeDtypeStruct((blocks, depth, st...  38.7 us
    pallas_call x2, Pallas kernels, head_call(): pl.pallas_call(kernel, out_shape=jax.ShapeDtypeStruct((blocks, 8, rows),...  34.6 us
    ppermute x28, starting transfers between devices, swap(): return lax.ppermute(values, axis, [(i, i ^ bit) for i in range(size)])  34.3 us
    pallas_call x1, Pallas kernels, swiglu_call(): pl.pallas_call(kernel, out_shape=(half, half), grid_spec=pltpu.PrefetchSc...  16.8 us
    convert_element_type x4, other arithmetic, head_part(): block = (block.astype(F32) * row_gain).astype(BF)  10.9 us
  transfers between devices with their start and end apart: 54, of which 21 were waited for; matrix products, arithmetic and copies ran while one was open for 9% of the time, Pallas kernels for 23%

profile of v3, /device:TPU:0, one launch (start us, length us, event | category | flops | bytes accessed | tf_op | source)
XLA Modules:
  0.0 355.0 jit_solution(3857415743456967444)
XLA Ops:
  0.6 1.2 copy-done.3
  1.9 3.5 split.1
  5.3 3.0 collective-permute-start.5
  8.4 1.5 collective-permute-start.3
  10.6 2.6 collective-permute-start.1
  13.2 1.5 collective-permute-start
  16.6 1.7 multiply_convert_fusion.23
  18.4 1.3 multiply_convert_fusion.7
  21.0 1.5 collective-permute-start.4
  27.3 2.7 and_select_fusion.owners
  31.8 1.5 collective-permute-start.8
  36.1 1.2 copy-done.4
  37.3 2.9 qkv.1
  41.4 1.2 collective-permute-start.9
  42.7 7.0 %collective-permute-start.7 = (bf16[256,512]{1,0:T(8,128)(2,1)S(1)}, bf16[256,512]{1,0:T(8,128)(2,1)S(1)}, u32[]{:S(2)}, u32[]{:S(2)}) collective-permute-start(bf16[256,512]{1,0:T(8,128)(2,1)S(1)} %get-tuple-element.162.refs_0_), channel_id=1, source_target_pairs={{0,16},{4,20},{8,24},{12,28},{16,0},{20,4},{24,8},{28,12},{1,17},{... | collective-permute-start | bytes 786440 | tf_op jit(solution)/shard_map/ppermute | solution.py:31
  50.4 13.6 %attention_near.1 = (f32[4,64,512]{2,1,0:T(8,128)}, f32[4,1,512]{2,1,0:T(1,128)}) custom-call(s32[4,4]{1,0:T(4,128)} %get-tuple-element.133.flags, s32[4]{0:T(128)} %copy-done.50, bf16[256,512]{1,0:T(8,128)(2,1)} %copy-done.9, s32[4,1,512]{2,1,0:T(1,128)} %tile.27.refs_1_, bf16[2048,128]{1,0:T(8,128)(2,1)} %get-tuple-element.136.refs_2_, ...), custom_call_target="tpu_custom_call" | custom-call | flops 4294967296 | bytes 3145728 | tf_op jit(solution)/shard_map/attention_near/pallas_call | solution.py:327
  64.0 4.6 %collective-permute-done.7.refs_0_ = bf16[256,512]{1,0:T(8,128)(2,1)S(1)} collective-permute-done((bf16[256,512]{1,0:T(8,128)(2,1)S(1)}, bf16[256,512]{1,0:T(8,128)(2,1)S(1)}, u32[]{:S(2)}, u32[]{:S(2)}) %collective-permute-start.7) | collective-permute-done | bytes 262176 | tf_op jit(solution)/shard_map/ppermute | solution.py:31
  68.7 3.5 multiply_convert_fusion
  72.2 1.7 fusion.8
  75.3 4.3 %multiply_convert_fusion.9 = (bf16[256,512]{1,0:T(8,128)(2,1)}, bf16[256,512]{1,0:T(8,128)(2,1)}, bf16[256,512]{1,0:T(8,128)(2,1)}, bf16[256,512]{1,0:T(8,128)(2...) fusion(bf16[256,16384]{1,0:T(8,128)(2,1)} %param.30, ...), kind=kLoop, calls=%fused_computation.33 | loop fusion | flops 5898240 | bytes 7865404 | tf_op jit(solution)/shard_map/convert_element_type | solution.py:741
  80.4 17.3 %attention_far.1 = (bf16[4,80,512]{2,1,0:T(8,128)(2,1)}, f32[4,1,512]{2,1,0:T(1,128)}) custom-call(s32[4,4]{1,0:T(4,128)} %get-tuple-element.148.flags, s32[4]{0:T(128)} %copy-done.50, bf16[256,512]{1,0:T(8,128)(2,1)} %copy-done.64, s32[4,1,512]{2,1,0:T(1,128)} %tile.62.refs_1_, bf16[2048,128]{1,0:T(8,128)(2,1)} %get-tuple-element.136.refs_2_, ...), custom_call_target="tpu_custom_call" | custom-call | flops 4294967296 | bytes 4194304 | tf_op jit(solution)/shard_map/attention_far/pallas_call | solution.py:327
  97.8 4.3 %collective-permute-done.13.refs_13_.refs_29_.refs_21_ = bf16[272,1024]{1,0:T(8,128)(2,1)S(1)} collective-permute-done((bf16[272,1024]{1,0:T(8,128)(2,1)S(1)}, bf16[272,1024]{1,0:T(8,128)(2,1)S(1)}, u32[]{:S(2)}, u32[]{:S(2)}) %collective-permute-start.13) | collective-permute-done | bytes 557088 | tf_op jit(solution)/shard_map/ppermute | solution.py:765
  102.1 2.0 collective-permute-start.15
  104.1 2.9 collective-permute-start.16
  107.0 7.7 %attention_rest.1 = (bf16[4,80,512]{2,1,0:T(8,128)(2,1)}, f32[4,1,512]{2,1,0:T(1,128)}) custom-call(s32[4,4]{1,0:T(4,128)} %get-tuple-element.133.flags, s32[4]{0:T(128)} %copy-done.50, bf16[256,512]{1,0:T(8,128)(2,1)} %copy-done.9, s32[4,1,512]{2,1,0:T(1,128)} %tile.27.refs_1_, bf16[2048,128]{1,0:T(8,128)(2,1)} %collective-permute-done.10.refs_8_.refs_2_, ...), custom_call_target="tpu_custom_call" | custom-call | flops 4294967296 | bytes 1048576 | tf_op jit(solution)/shard_map/attention_rest/pallas_call | solution.py:327
  114.8 16.4 %collective-permute-done.16.refs_20_ = bf16[256,512]{1,0:T(8,128)(2,1)} collective-permute-done((bf16[256,512]{1,0:T(8,128)(2,1)}, bf16[256,512]{1,0:T(8,128)(2,1)}, u32[]{:S(2)}, u32[]{:S(2)}) %collective-permute-start.16) | collective-permute-done | bytes 262176 | tf_op jit(solution)/shard_map/ppermute | solution.py:765
  132.2 1.7 project.1
  134.0 1.9 collective-permute-done.17
  136.0 1.5 collective-permute-start.18
  137.5 2.2 collective-permute-start.20
  139.8 1.3 collective-permute-start.21
  141.1 8.9 %collective-permute-done.18 = bf16[2,256,512]{2,1,0:T(8,128)(2,1)S(1)} collective-permute-done((bf16[2,256,512]{2,1,0:T(8,128)(2,1)S(1)}, bf16[2,256,512]{2,1,0:T(8,128)(2,1)S(1)}, u32[]{:S(2)}, u32[]{:S(2)}) %collective-permute-start.18) | collective-permute-done | bytes 524320 | tf_op jit(solution)/shard_map/ppermute | solution.py:31
  150.3 13.5 %collective-permute-done.19.refs_11_.refs_27_.refs_19_ = bf16[272,1024]{1,0:T(8,128)(2,1)S(1)} collective-permute-done((bf16[272,1024]{1,0:T(8,128)(2,1)S(1)}, bf16[272,1024]{1,0:T(8,128)(2,1)S(1)}, u32[]{:S(2)}, u32[]{:S(2)}) %collective-permute-start.19) | collective-permute-done | bytes 557088 | tf_op jit(solution)/shard_map/ppermute | solution.py:765
  166.9 1.2 collective-permute-start.25
  168.1 3.6 %collective-permute-start.23 = (bf16[272,1024]{1,0:T(8,128)(2,1)S(1)}, bf16[272,1024]{1,0:T(8,128)(2,1)S(1)}, u32[]{:S(2)}, u32[]{:S(2)}) collective-permute-start(bf16[272,1024]{1,0:T(8,128)(2,1)S(1)} %get-tuple-element.186), channel_id=1, source_target_pairs={{0,28},{4,24},{24,4},{28,0},{1,29},{5,25},{25,5},{29,1},{2,30},{6,... | collective-permute-start | bytes 1671176 | tf_op jit(solution)/shard_map/ppermute | solution.py:765
  172.5 16.8 %swiglu.1 = (bf16[2,256,512]{2,1,0:T(8,128)(2,1)}, bf16[2,256,512]{2,1,0:T(8,128)(2,1)}) custom-call(s32[2]{0:T(128)} %copy-done.8, bf16[2,256,512]{2,1,0:T(8,128)(2,1)} %copy-done.12, bf16[2,256,512]{2,1,0:T(8,128)(2,1)} %copy-done.23, f32[4,512]{1,0:T(4,128)} %reshape.233.gain, bf16[2048,2048]{1,0:T(8,128)(2,1)} %w_gate.1, bf16[2048,2048]{1,0:T(8,128)(2,1)} %w_up.1, ...), custom_call_target="tpu_custom_call" | custom-call | flops 6442450944 | bytes 25165824 | tf_op jit(solution)/shard_map/swiglu/pallas_call | solution.py:447
  189.4 4.4 %collective-permute-done.25.refs_21_ = bf16[256,512]{1,0:T(8,128)(2,1)S(1)} collective-permute-done((bf16[256,512]{1,0:T(8,128)(2,1)S(1)}, bf16[256,512]{1,0:T(8,128)(2,1)S(1)}, u32[]{:S(2)}, u32[]{:S(2)}) %collective-permute-start.25) | collective-permute-done | bytes 262176 | tf_op jit(solution)/shard_map/ppermute | solution.py:765
  193.9 2.1 collective-permute-done.26
  196.0 1.2 convert_add_fusion
  197.9 2.0 collective-permute-start.30
  201.3 4.4 %collective-permute-done.27 = bf16[1,256,512]{2,1,0:T(8,128)(2,1)S(1)} collective-permute-done((bf16[1,256,512]{2,1,0:T(8,128)(2,1)S(1)}, bf16[1,256,512]{2,1,0:T(8,128)(2,1)S(1)}, u32[]{:S(2)}, u32[]{:S(2)}) %collective-permute-start.27) | collective-permute-done | bytes 262176 | tf_op jit(solution)/shard_map/ppermute | solution.py:31
  205.8 1.3 collective-permute-done.28.refs_18_
  207.0 4.5 %collective-permute-done.30.refs_10_ = bf16[256,512]{1,0:T(8,128)(2,1)S(1)} collective-permute-done((bf16[256,512]{1,0:T(8,128)(2,1)S(1)}, bf16[256,512]{1,0:T(8,128)(2,1)S(1)}, u32[]{:S(2)}, u32[]{:S(2)}) %collective-permute-start.30) | collective-permute-done | bytes 262176 | tf_op jit(solution)/shard_map/ppermute | solution.py:765
  211.6 5.3 %collective-permute-start.32 = (bf16[1,256,512]{2,1,0:T(8,128)(2,1)S(1)}, bf16[1,256,512]{2,1,0:T(8,128)(2,1)S(1)}, u32[]{:S(2)}, u32[]{:S(2)}) collective-permute-start(bf16[1,256,512]{2,1,0:T(8,128)(2,1)S(1)} %bitcast.62), channel_id=1, source_target_pairs={{0,16},{4,20},{8,24},{12,28},{16,0},{20,4},{24,8},{28,12},{1,17},{... | collective-permute-start | bytes 786440 | tf_op jit(solution)/shard_map/ppermute | solution.py:31
  216.8 10.7 %collective-permute-done.32 = bf16[1,256,512]{2,1,0:T(8,128)(2,1)S(1)} collective-permute-done((bf16[1,256,512]{2,1,0:T(8,128)(2,1)S(1)}, bf16[1,256,512]{2,1,0:T(8,128)(2,1)S(1)}, u32[]{:S(2)}, u32[]{:S(2)}) %collective-permute-start.32) | collective-permute-done | bytes 262176 | tf_op jit(solution)/shard_map/ppermute | solution.py:31
  228.4 11.7 %collective-permute-done.33 = bf16[2,256,512]{2,1,0:T(8,128)(2,1)S(1)} collective-permute-done((bf16[2,256,512]{2,1,0:T(8,128)(2,1)S(1)}, bf16[2,256,512]{2,1,0:T(8,128)(2,1)S(1)}, u32[]{:S(2)}, u32[]{:S(2)}) %collective-permute-start.33) | collective-permute-done | bytes 524320 | tf_op jit(solution)/shard_map/ppermute | solution.py:31
  241.0 1.5 collective-permute-start.35
  242.6 1.5 collective-permute-start.36
  244.0 2.9 collective-permute-start.37
  246.9 4.7 %collective-permute-start.38 = (bf16[256,512]{1,0:T(8,128)(2,1)S(1)}, bf16[256,512]{1,0:T(8,128)(2,1)S(1)}, u32[]{:S(2)}, u32[]{:S(2)}) collective-permute-start(bf16[256,512]{1,0:T(8,128)(2,1)S(1)} %copy-done.31), channel_id=1, source_target_pairs={{0,28},{4,24},{24,4},{28,0},{1,29},{5,25},{25,5},{29,1},{2,30},{6,... | collective-permute-start | bytes 786440 | tf_op jit(solution)/shard_map/ppermute | solution.py:765
  251.6 3.7 %collective-permute-done.35 = bf16[4,128,512]{2,1,0:T(8,128)(2,1)S(1)} collective-permute-done((bf16[4,128,512]{2,1,0:T(8,128)(2,1)S(1)}, bf16[4,128,512]{2,1,0:T(8,128)(2,1)S(1)}, u32[]{:S(2)}, u32[]{:S(2)}) %collective-permute-start.35) | collective-permute-done | bytes 524320 | tf_op jit(solution)/shard_map/ppermute | solution.py:31
  256.2 2.8 collective-permute-done.38
  258.9 1.6 collective-permute-start.40
  261.6 3.1 collective-permute-start.41
  264.9 2.9 collective-permute-start.43
  267.8 18.5 %collective-permute-done.42.refs_19_ = bf16[256,512]{1,0:T(8,128)(2,1)S(1)} collective-permute-done((bf16[256,512]{1,0:T(8,128)(2,1)S(1)}, bf16[256,512]{1,0:T(8,128)(2,1)S(1)}, u32[]{:S(2)}, u32[]{:S(2)}) %collective-permute-start.42) | collective-permute-done | bytes 262176 | tf_op jit(solution)/shard_map/ppermute | solution.py:765
  291.9 4.9 %collective-permute-start.49 = (bf16[256,512]{1,0:T(8,128)(2,1)S(1)}, bf16[256,512]{1,0:T(8,128)(2,1)S(1)}, u32[]{:S(2)}, u32[]{:S(2)}) collective-permute-start(bf16[256,512]{1,0:T(8,128)(2,1)S(1)} %copy-done.27), channel_id=1, source_target_pairs={{0,20},{4,16},{8,28},{12,24},{16,4},{20,0},{24,12},{28,8},{1,21},{... | collective-permute-start | bytes 786440 | tf_op jit(solution)/shard_map/ppermute | solution.py:765
  296.8 1.4 collective-permute-start.50
  298.2 4.5 %collective-permute-start.51 = (bf16[256,512]{1,0:T(8,128)(2,1)S(1)}, bf16[256,512]{1,0:T(8,128)(2,1)S(1)}, u32[]{:S(2)}, u32[]{:S(2)}) collective-permute-start(bf16[256,512]{1,0:T(8,128)(2,1)S(1)} %copy-done.25), channel_id=1, source_target_pairs={{0,28},{4,24},{24,4},{28,0},{1,29},{5,25},{25,5},{29,1},{2,30},{6,... | collective-permute-start | bytes 786440 | tf_op jit(solution)/shard_map/ppermute | solution.py:765
  302.7 22.8 %head.2 = f32[8,8,256]{2,1,0:T(8,128)} custom-call(s32[2]{0:T(128)} %copy-done.8, bf16[1,2,4,128,512]{4,3,2,1,0:T(8,128)(2,1)} %copy-done.15, bf16[1,2,4,128,512]{4,3,2,1,0:T(8,128)(2,1)} %collective-permute-done.39.refs_1_, bf16[2,4,128,512]{3,2,1,0:T(8,128)(2,1)} %copy-done.16, bf16[2,4,128,512]{3,2,1,0:T(8,128)(2,1)} %collective-permute-done.40.refs_3_, ...), custom_call_target="tpu_custom_call" | custom-call | flops 12884901888 | bytes 14680064 | tf_op jit(solution)/shard_map/head/pallas_call | solution.py:639
  326.4 11.8 %head.3 = f32[8,8,256]{2,1,0:T(8,128)} custom-call(s32[2]{0:T(128)} %copy-done.8, bf16[1,2,4,128,512]{4,3,2,1,0:T(8,128)(2,1)} %copy-done.15, bf16[1,2,4,128,512]{4,3,2,1,0:T(8,128)(2,1)} %collective-permute-done.39.refs_1_, bf16[2,4,128,512]{3,2,1,0:T(8,128)(2,1)} %copy-done.16, bf16[2,4,128,512]{3,2,1,0:T(8,128)(2,1)} %collective-permute-done.40.refs_3_, ...), custom_call_target="tpu_custom_call" | custom-call | flops 4294967296 | bytes 10485760 | tf_op jit(solution)/shard_map/head/pallas_call | solution.py:639
  339.2 9.9 %all_to_all.5 = f32[8,3,256]{2,1,0:T(4,128)S(1)} all-to-all(f32[8,3,256]{2,1,0:T(4,128)S(1)} %pad_maximum_fusion.5), channel_id=1, replica_groups=mesh['req'=8,'mlp'=4] {'req'}, dimensions={0} | all-to-all | bytes 49152 | tf_op jit(solution)/shard_map/all_to_all | solution.py:953
  350.5 1.5 collective-permute-start.53
  352.0 2.2 collective-permute-done.53
  (270 shorter events, 37.9 us)
Async XLA Ops:
  5.3 36.1 %collective-permute-start.5 = (bf16[2048,128]{1,0:T(8,128)(2,1)}, bf16[2048,128]{1,0:T(8,128)(2,1)}, u32[]{:S(2)}, u32[]{:S(2)}) collective-permute-start(bf16[2048,128]{1,0:T(8,128)(2,1)} %get-tuple-element.136.refs_2_), channel_id=1, source_target_pairs={{0,8},{4,12},{8,0},{12,4},{16,24},{20,28},{24,16},{28,20},{1,9},{5... | collective-permute-start | bytes 1572872 | tf_op jit(solution)/shard_map/ppermute | solution.py:31
  8.4 34.3 %collective-permute-start.3 = (bf16[2048,128]{1,0:T(8,128)(2,1)}, bf16[2048,128]{1,0:T(8,128)(2,1)}, u32[]{:S(2)}, u32[]{:S(2)}) collective-permute-start(bf16[2048,128]{1,0:T(8,128)(2,1)} %get-tuple-element.136.refs_2_), channel_id=1, source_target_pairs={{0,4},{4,0},{8,12},{12,8},{16,20},{20,16},{24,28},{28,24},{1,5},{5... | collective-permute-start | bytes 1572872 | tf_op jit(solution)/shard_map/ppermute | solution.py:31
  10.6 10.4 %collective-permute-start.1 = (s32[1,8]{1,0:T(1,128)S(1)}, s32[1,8]{1,0:T(1,128)S(1)}, u32[]{:S(2)}, u32[]{:S(2)}) collective-permute-start(s32[1,8]{1,0:T(1,128)S(1)} %pad_add_fusion), channel_id=1, source_target_pairs={{0,16},{4,20},{8,24},{12,28},{16,0},{20,4},{24,8},{28,12},{1,17},{... | collective-permute-start | bytes 104 | tf_op jit(solution)/shard_map/ppermute | solution.py:31
  13.2 9.3 %collective-permute-start = (bf16[256,512]{1,0:T(8,128)(2,1)}, bf16[256,512]{1,0:T(8,128)(2,1)S(1)}, u32[]{:S(2)}, u32[]{:S(2)}) collective-permute-start(bf16[256,512]{1,0:T(8,128)(2,1)} %refs_0_), channel_id=1, source_target_pairs={{0,2},{1,3},{2,0},{3,1},{4,6},{5,7},{6,4},{7,5},{8,10},{9,11},{10,... | collective-permute-start | bytes 786440 | tf_op jit(solution)/shard_map/ppermute | solution.py:31
  14.7 27.9 %collective-permute-start.6 = (bf16[128,2048]{1,0:T(8,128)(2,1)}, bf16[128,2048]{1,0:T(8,128)(2,1)}, u32[]{:S(2)}, u32[]{:S(2)}) collective-permute-start(bf16[128,2048]{1,0:T(8,128)(2,1)} %get-tuple-element.137.refs_3_), channel_id=1, source_target_pairs={{0,8},{4,12},{8,0},{12,4},{16,24},{20,28},{24,16},{28,20},{1,9},{5... | collective-permute-start | bytes 1572872 | tf_op jit(solution)/shard_map/ppermute | solution.py:31
  21.0 110.2 %copy-start.8 = (s32[2]{0:T(128)}, s32[2]{0:T(128)S(1)}, u32[]{:S(2)}) copy-start(s32[2]{0:T(128)S(1)} %pad_add_fusion.2.place) | copy-start | bytes 28
  21.0 21.7 %collective-permute-start.4 = (bf16[128,2048]{1,0:T(8,128)(2,1)}, bf16[128,2048]{1,0:T(8,128)(2,1)}, u32[]{:S(2)}, u32[]{:S(2)}) collective-permute-start(bf16[128,2048]{1,0:T(8,128)(2,1)} %get-tuple-element.137.refs_3_), channel_id=1, source_target_pairs={{0,4},{4,0},{8,12},{12,8},{16,20},{20,16},{24,28},{28,24},{1,5},{5... | collective-permute-start | bytes 1572872 | tf_op jit(solution)/shard_map/ppermute | solution.py:31
  24.1 6.8 %collective-permute-start.2 = (bf16[256,1024]{1,0:T(8,128)(2,1)}, bf16[256,1024]{1,0:T(8,128)(2,1)S(1)}, u32[]{:S(2)}, u32[]{:S(2)}) collective-permute-start(bf16[256,1024]{1,0:T(8,128)(2,1)} %pad_maximum_fusion.2), channel_id=1, source_target_pairs={{0,1},{1,0},{2,3},{3,2},{4,5},{5,4},{6,7},{7,6},{8,9},{9,8},{10,11... | collective-permute-start | bytes 1572872 | tf_op jit(solution)/shard_map/ppermute | solution.py:31
  31.8 36.9 %collective-permute-start.8 = (bf16[272,1024]{1,0:T(8,128)(2,1)}, bf16[272,1024]{1,0:T(8,128)(2,1)}, u32[]{:S(2)}, u32[]{:S(2)}) collective-permute-start(bf16[272,1024]{1,0:T(8,128)(2,1)} %fusion.7), channel_id=1, source_target_pairs={{8,16},{12,20},{16,8},{20,12},{9,17},{13,21},{17,9},{21,13},{10,18... | collective-permute-start | bytes 1671176 | tf_op jit(solution)/shard_map/ppermute | solution.py:765
  41.4 27.2 %collective-permute-start.9 = (bf16[256,512]{1,0:T(8,128)(2,1)}, bf16[256,512]{1,0:T(8,128)(2,1)S(1)}, u32[]{:S(2)}, u32[]{:S(2)}) collective-permute-start(bf16[256,512]{1,0:T(8,128)(2,1)} %multiply_convert_fusion.23), channel_id=1, source_target_pairs={{8,16},{12,20},{16,8},{20,12},{9,17},{13,21},{17,9},{21,13},{10,18... | collective-permute-start | bytes 786440 | tf_op jit(solution)/shard_map/ppermute | solution.py:765
  42.7 26.0 %collective-permute-start.7 = (bf16[256,512]{1,0:T(8,128)(2,1)S(1)}, bf16[256,512]{1,0:T(8,128)(2,1)S(1)}, u32[]{:S(2)}, u32[]{:S(2)}) collective-permute-start(bf16[256,512]{1,0:T(8,128)(2,1)S(1)} %get-tuple-element.162.refs_0_), channel_id=1, source_target_pairs={{0,16},{4,20},{8,24},{12,28},{16,0},{20,4},{24,8},{28,12},{1,17},{... | collective-permute-start | bytes 786440 | tf_op jit(solution)/shard_map/ppermute | solution.py:31
  49.7 30.0 %collective-permute-start.11 = (bf16[128,2048]{1,0:T(8,128)(2,1)}, bf16[128,2048]{1,0:T(8,128)(2,1)S(1)}, u32[]{:S(2)}, u32[]{:S(2)}) collective-permute-start(bf16[128,2048]{1,0:T(8,128)(2,1)} %collective-permute-done.4.refs_5_), channel_id=1, source_target_pairs={{0,8},{4,12},{8,0},{12,4},{16,24},{20,28},{24,16},{28,20},{1,9},{5... | collective-permute-start | bytes 1572872 | tf_op jit(solution)/shard_map/ppermute | solution.py:31
  49.9 29.8 %collective-permute-start.10 = (bf16[2048,128]{1,0:T(8,128)(2,1)}, bf16[2048,128]{1,0:T(8,128)(2,1)}, u32[]{:S(2)}, u32[]{:S(2)}) collective-permute-start(bf16[2048,128]{1,0:T(8,128)(2,1)} %collective-permute-done.5.refs_6_), channel_id=1, source_target_pairs={{0,4},{4,0},{8,12},{12,8},{16,20},{20,16},{24,28},{28,24},{1,5},{5... | collective-permute-start | bytes 1572872 | tf_op jit(solution)/shard_map/ppermute | solution.py:31
  73.9 23.8 %collective-permute-start.12 = (bf16[272,1024]{1,0:T(8,128)(2,1)S(1)}, bf16[272,1024]{1,0:T(8,128)(2,1)S(1)}, u32[]{:S(2)}, u32[]{:S(2)}) collective-permute-start(bf16[272,1024]{1,0:T(8,128)(2,1)S(1)} %get-tuple-element.159), channel_id=1, source_target_pairs={{0,4},{4,0},{8,12},{12,8},{16,20},{20,16},{24,28},{28,24},{1,5},{5... | collective-permute-start | bytes 1671176 | tf_op jit(solution)/shard_map/ppermute | solution.py:765
  74.4 27.7 %collective-permute-start.13 = (bf16[272,1024]{1,0:T(8,128)(2,1)S(1)}, bf16[272,1024]{1,0:T(8,128)(2,1)S(1)}, u32[]{:S(2)}, u32[]{:S(2)}) collective-permute-start(bf16[272,1024]{1,0:T(8,128)(2,1)S(1)} %get-tuple-element.160), channel_id=1, source_target_pairs={{0,20},{4,16},{8,28},{12,24},{16,4},{20,0},{24,12},{28,8},{1,21},{... | collective-permute-start | bytes 1671176 | tf_op jit(solution)/shard_map/ppermute | solution.py:765
  102.1 29.1 %copy-start.5 = (f32[4,64,512]{2,1,0:T(8,128)S(1)}, f32[4,64,512]{2,1,0:T(8,128)}, u32[]{:S(2)}) copy-start(f32[4,64,512]{2,1,0:T(8,128)} %get-tuple-element.146.one) | copy-start | bytes 1572868
  102.1 29.1 %copy-start.7 = (f32[4,1,512]{2,1,0:T(1,128)S(1)}, f32[4,1,512]{2,1,0:T(1,128)}, u32[]{:S(2)}) copy-start(f32[4,1,512]{2,1,0:T(1,128)} %get-tuple-element.147.lse_one) | copy-start | bytes 24580
  102.1 29.0 %collective-permute-start.15 = (bf16[272,1024]{1,0:T(8,128)(2,1)}, bf16[272,1024]{1,0:T(8,128)(2,1)}, u32[]{:S(2)}, u32[]{:S(2)}) collective-permute-start(bf16[272,1024]{1,0:T(8,128)(2,1)} %get-tuple-element.164), channel_id=1, source_target_pairs={{0,8},{4,12},{8,0},{12,4},{16,24},{20,28},{24,16},{28,20},{1,9},{5... | collective-permute-start | bytes 1671176 | tf_op jit(solution)/shard_map/ppermute | solution.py:765
  104.1 27.1 %collective-permute-start.14 = (bf16[4,80,512]{2,1,0:T(8,128)(2,1)}, bf16[4,80,512]{2,1,0:T(8,128)(2,1)S(1)}, u32[]{:S(2)}, u32[]{:S(2)}) collective-permute-start(bf16[4,80,512]{2,1,0:T(8,128)(2,1)} %get-tuple-element.161), channel_id=1, source_target_pairs={{0,16},{4,20},{8,24},{12,28},{16,0},{20,4},{24,8},{28,12},{1,17},{... | collective-permute-start | bytes 983048 | tf_op jit(solution)/shard_map/ppermute | solution.py:31
  104.1 27.1 %collective-permute-start.16 = (bf16[256,512]{1,0:T(8,128)(2,1)}, bf16[256,512]{1,0:T(8,128)(2,1)}, u32[]{:S(2)}, u32[]{:S(2)}) collective-permute-start(bf16[256,512]{1,0:T(8,128)(2,1)} %get-tuple-element.165), channel_id=1, source_target_pairs={{0,16},{4,20},{8,24},{12,28},{16,0},{20,4},{24,8},{28,12},{1,17},{... | collective-permute-start | bytes 786440 | tf_op jit(solution)/shard_map/ppermute | solution.py:765
  133.9 2.0 collective-permute-start.17
  136.0 14.0 %collective-permute-start.18 = (bf16[2,256,512]{2,1,0:T(8,128)(2,1)S(1)}, bf16[2,256,512]{2,1,0:T(8,128)(2,1)S(1)}, u32[]{:S(2)}, u32[]{:S(2)}) collective-permute-start(bf16[2,256,512]{2,1,0:T(8,128)(2,1)S(1)} %add_convert_fusion.1), channel_id=1, source_target_pairs={{0,2},{1,3},{2,0},{3,1},{4,6},{5,7},{6,4},{7,5},{8,10},{9,11},{10,... | collective-permute-start | bytes 1572872 | tf_op jit(solution)/shard_map/ppermute | solution.py:31
  137.5 26.3 %collective-permute-start.19 = (bf16[272,1024]{1,0:T(8,128)(2,1)S(1)}, bf16[272,1024]{1,0:T(8,128)(2,1)S(1)}, u32[]{:S(2)}, u32[]{:S(2)}) collective-permute-start(bf16[272,1024]{1,0:T(8,128)(2,1)S(1)} %copy-done.18), channel_id=1, source_target_pairs={{0,12},{4,8},{8,4},{12,0},{16,28},{20,24},{24,20},{28,16},{1,13},{... | collective-permute-start | bytes 1671176 | tf_op jit(solution)/shard_map/ppermute | solution.py:765
  137.5 27.3 %collective-permute-start.20 = (bf16[272,1024]{1,0:T(8,128)(2,1)S(1)}, bf16[272,1024]{1,0:T(8,128)(2,1)S(1)}, u32[]{:S(2)}, u32[]{:S(2)}) collective-permute-start(bf16[272,1024]{1,0:T(8,128)(2,1)S(1)} %copy-done.17), channel_id=1, source_target_pairs={{0,16},{4,20},{8,24},{12,28},{16,0},{20,4},{24,8},{28,12},{1,17},{... | collective-permute-start | bytes 1671176 | tf_op jit(solution)/shard_map/ppermute | solution.py:765
  139.8 10.6 %collective-permute-start.21 = (bf16[256,512]{1,0:T(8,128)(2,1)S(1)}, bf16[256,512]{1,0:T(8,128)(2,1)S(1)}, u32[]{:S(2)}, u32[]{:S(2)}) collective-permute-start(bf16[256,512]{1,0:T(8,128)(2,1)S(1)} %copy-done.36), channel_id=1, source_target_pairs={{0,4},{4,0},{8,12},{12,8},{16,20},{20,16},{24,28},{28,24},{1,5},{5... | collective-permute-start | bytes 786440 | tf_op jit(solution)/shard_map/ppermute | solution.py:765
  165.7 6.0 %collective-permute-start.22 = (bf16[2,256,512]{2,1,0:T(8,128)(2,1)S(1)}, bf16[2,256,512]{2,1,0:T(8,128)(2,1)S(1)}, u32[]{:S(2)}, u32[]{:S(2)}) collective-permute-start(bf16[2,256,512]{2,1,0:T(8,128)(2,1)S(1)} %add_convert_fusion.ours), channel_id=1, source_target_pairs={{0,1},{1,0},{2,3},{3,2},{4,5},{5,4},{6,7},{7,6},{8,9},{9,8},{10,11... | collective-permute-start | bytes 1572872 | tf_op jit(solution)/shard_map/ppermute | solution.py:31
  166.3 23.1 %collective-permute-start.24 = (bf16[256,512]{1,0:T(8,128)(2,1)S(1)}, bf16[256,512]{1,0:T(8,128)(2,1)S(1)}, u32[]{:S(2)}, u32[]{:S(2)}) collective-permute-start(bf16[256,512]{1,0:T(8,128)(2,1)S(1)} %copy-done.35), channel_id=1, source_target_pairs={{0,4},{4,0},{8,12},{12,8},{16,20},{20,16},{24,28},{28,24},{1,5},{5... | collective-permute-start | bytes 786440 | tf_op jit(solution)/shard_map/ppermute | solution.py:765
  166.9 26.9 %collective-permute-start.25 = (bf16[256,512]{1,0:T(8,128)(2,1)S(1)}, bf16[256,512]{1,0:T(8,128)(2,1)S(1)}, u32[]{:S(2)}, u32[]{:S(2)}) collective-permute-start(bf16[256,512]{1,0:T(8,128)(2,1)S(1)} %copy-done.34), channel_id=1, source_target_pairs={{0,20},{4,16},{8,28},{12,24},{16,4},{20,0},{24,12},{28,8},{1,21},{... | collective-permute-start | bytes 786440 | tf_op jit(solution)/shard_map/ppermute | solution.py:765
  168.1 25.7 %collective-permute-start.23 = (bf16[272,1024]{1,0:T(8,128)(2,1)S(1)}, bf16[272,1024]{1,0:T(8,128)(2,1)S(1)}, u32[]{:S(2)}, u32[]{:S(2)}) collective-permute-start(bf16[272,1024]{1,0:T(8,128)(2,1)S(1)} %get-tuple-element.186), channel_id=1, source_target_pairs={{0,28},{4,24},{24,4},{28,0},{1,29},{5,25},{25,5},{29,1},{2,30},{6,... | collective-permute-start | bytes 1671176 | tf_op jit(solution)/shard_map/ppermute | solution.py:765
  193.8 2.2 collective-permute-start.26
  197.2 8.4 %collective-permute-start.27 = (bf16[1,256,512]{2,1,0:T(8,128)(2,1)S(1)}, bf16[1,256,512]{2,1,0:T(8,128)(2,1)S(1)}, u32[]{:S(2)}, u32[]{:S(2)}) collective-permute-start(bf16[1,256,512]{2,1,0:T(8,128)(2,1)S(1)} %slice.168), channel_id=1, source_target_pairs={{0,2},{1,3},{2,0},{3,1},{4,6},{5,7},{6,4},{7,5},{8,10},{9,11},{10,... | collective-permute-start | bytes 786440 | tf_op jit(solution)/shard_map/ppermute | solution.py:31
  197.9 9.2 %collective-permute-start.28 = (bf16[256,512]{1,0:T(8,128)(2,1)S(1)}, bf16[256,512]{1,0:T(8,128)(2,1)S(1)}, u32[]{:S(2)}, u32[]{:S(2)}) collective-permute-start(bf16[256,512]{1,0:T(8,128)(2,1)S(1)} %copy-done.33), channel_id=1, source_target_pairs={{0,8},{4,12},{8,0},{12,4},{16,24},{20,28},{24,16},{28,20},{1,9},{5... | collective-permute-start | bytes 786440 | tf_op jit(solution)/shard_map/ppermute | solution.py:765
  197.9 13.7 %collective-permute-start.30 = (bf16[256,512]{1,0:T(8,128)(2,1)S(1)}, bf16[256,512]{1,0:T(8,128)(2,1)S(1)}, u32[]{:S(2)}, u32[]{:S(2)}) collective-permute-start(bf16[256,512]{1,0:T(8,128)(2,1)S(1)} %copy-done.32), channel_id=1, source_target_pairs={{0,8},{4,12},{8,0},{12,4},{16,24},{20,28},{24,16},{28,20},{1,9},{5... | collective-permute-start | bytes 786440 | tf_op jit(solution)/shard_map/ppermute | solution.py:765
  199.9 11.7 %collective-permute-start.29 = (bf16[256,512]{1,0:T(8,128)(2,1)S(1)}, bf16[256,512]{1,0:T(8,128)(2,1)S(1)}, u32[]{:S(2)}, u32[]{:S(2)}) collective-permute-start(bf16[256,512]{1,0:T(8,128)(2,1)S(1)} %copy-done.31), channel_id=1, source_target_pairs={{8,20},{12,16},{16,12},{20,8},{9,21},{13,17},{17,13},{21,9},{10,22... | collective-permute-start | bytes 786440 | tf_op jit(solution)/shard_map/ppermute | solution.py:765
  200.6 11.0 %collective-permute-start.31 = (bf16[256,512]{1,0:T(8,128)(2,1)S(1)}, bf16[256,512]{1,0:T(8,128)(2,1)S(1)}, u32[]{:S(2)}, u32[]{:S(2)}) collective-permute-start(bf16[256,512]{1,0:T(8,128)(2,1)S(1)} %copy-done.25), channel_id=1, source_target_pairs={{8,20},{12,16},{16,12},{20,8},{9,21},{13,17},{17,13},{21,9},{10,22... | collective-permute-start | bytes 786440 | tf_op jit(solution)/shard_map/ppermute | solution.py:765
  205.8 34.4 %copy-start.14 = (bf16[256,512]{1,0:T(8,128)(2,1)}, bf16[256,512]{1,0:T(8,128)(2,1)S(1)}, u32[]{:S(2)}) copy-start(bf16[256,512]{1,0:T(8,128)(2,1)S(1)} %fusion.11) | copy-start | bytes 786436
  207.0 33.0 %copy-start.61 = (bf16[256,512]{1,0:T(8,128)(2,1)}, bf16[256,512]{1,0:T(8,128)(2,1)S(1)}, u32[]{:S(2)}) copy-start(bf16[256,512]{1,0:T(8,128)(2,1)S(1)} %collective-permute-done.28.refs_18_) | copy-start | bytes 786436
  211.6 16.0 %collective-permute-start.32 = (bf16[1,256,512]{2,1,0:T(8,128)(2,1)S(1)}, bf16[1,256,512]{2,1,0:T(8,128)(2,1)S(1)}, u32[]{:S(2)}, u32[]{:S(2)}) collective-permute-start(bf16[1,256,512]{2,1,0:T(8,128)(2,1)S(1)} %bitcast.62), channel_id=1, source_target_pairs={{0,16},{4,20},{8,24},{12,28},{16,0},{20,4},{24,8},{28,12},{1,17},{... | collective-permute-start | bytes 786440 | tf_op jit(solution)/shard_map/ppermute | solution.py:31
  227.6 12.5 %collective-permute-start.33 = (bf16[2,256,512]{2,1,0:T(8,128)(2,1)S(1)}, bf16[2,256,512]{2,1,0:T(8,128)(2,1)S(1)}, u32[]{:S(2)}, u32[]{:S(2)}) collective-permute-start(bf16[2,256,512]{2,1,0:T(8,128)(2,1)S(1)} %maximum_bitcast_fusion.1), channel_id=1, source_target_pairs={{0,8},{4,12},{8,0},{12,4},{16,24},{20,28},{24,16},{28,20},{1,9},{5... | collective-permute-start | bytes 1572872 | tf_op jit(solution)/shard_map/ppermute | solution.py:31
  227.7 12.5 %collective-permute-start.34 = (bf16[272,1024]{1,0:T(8,128)(2,1)S(1)}, bf16[272,1024]{1,0:T(8,128)(2,1)S(1)}, u32[]{:S(2)}, u32[]{:S(2)}) collective-permute-start(bf16[272,1024]{1,0:T(8,128)(2,1)S(1)} %get-tuple-element.186), channel_id=1, source_target_pairs={{8,20},{12,16},{16,12},{20,8},{9,21},{13,17},{17,13},{21,9},{10,22... | collective-permute-start | bytes 1671176 | tf_op jit(solution)/shard_map/ppermute | solution.py:765
  241.0 14.3 %collective-permute-start.35 = (bf16[4,128,512]{2,1,0:T(8,128)(2,1)S(1)}, bf16[4,128,512]{2,1,0:T(8,128)(2,1)S(1)}, u32[]{:S(2)}, u32[]{:S(2)}) collective-permute-start(bf16[4,128,512]{2,1,0:T(8,128)(2,1)S(1)} %get-tuple-element.260), channel_id=1, source_target_pairs={{0,4},{4,0},{8,12},{12,8},{16,20},{20,16},{24,28},{28,24},{1,5},{5... | collective-permute-start | bytes 1572872 | tf_op jit(solution)/shard_map/ppermute | solution.py:31
  242.6 12.9 %collective-permute-start.36 = (bf16[1,4,128,512]{3,2,1,0:T(8,128)(2,1)S(1)}, bf16[1,4,128,512]{3,2,1,0:T(8,128)(2,1)S(1)}, u32[]{:S(2)}, u32[]{:S(2)}) collective-permute-start(bf16[1,4,128,512]{3,2,1,0:T(8,128)(2,1)S(1)} %get-tuple-element.258), channel_id=1, source_target_pairs={{0,2},{1,3},{2,0},{3,1},{4,6},{5,7},{6,4},{7,5},{8,10},{9,11},{10,... | collective-permute-start | bytes 1572872 | tf_op jit(solution)/shard_map/ppermute | solution.py:31
  244.0 12.1 %collective-permute-start.37 = (bf16[256,512]{1,0:T(8,128)(2,1)}, bf16[256,512]{1,0:T(8,128)(2,1)S(1)}, u32[]{:S(2)}, u32[]{:S(2)}) collective-permute-start(bf16[256,512]{1,0:T(8,128)(2,1)} %multiply_convert_fusion.23), channel_id=1, source_target_pairs={{0,24},{4,28},{24,0},{28,4},{1,25},{5,29},{25,1},{29,5},{2,26},{6,... | collective-permute-start | bytes 786440 | tf_op jit(solution)/shard_map/ppermute | solution.py:765
  246.9 12.0 %collective-permute-start.38 = (bf16[256,512]{1,0:T(8,128)(2,1)S(1)}, bf16[256,512]{1,0:T(8,128)(2,1)S(1)}, u32[]{:S(2)}, u32[]{:S(2)}) collective-permute-start(bf16[256,512]{1,0:T(8,128)(2,1)S(1)} %copy-done.31), channel_id=1, source_target_pairs={{0,28},{4,24},{24,4},{28,0},{1,29},{5,25},{25,5},{29,1},{2,30},{6,... | collective-permute-start | bytes 786440 | tf_op jit(solution)/shard_map/ppermute | solution.py:765
  255.4 33.7 %copy-start.15 = (bf16[1,2,4,128,512]{4,3,2,1,0:T(8,128)(2,1)}, bf16[1,2,4,128,512]{4,3,2,1,0:T(8,128)(2,1)S(1)}, u32[]{:S(2)}) copy-start(bf16[1,2,4,128,512]{4,3,2,1,0:T(8,128)(2,1)S(1)} %maximum_bitcast_fusion.refs_0_) | copy-start | bytes 3145732
  255.4 32.8 %copy-start.20 = (bf16[272,1024]{1,0:T(8,128)(2,1)S(1)}, bf16[272,1024]{1,0:T(8,128)(2,1)}, u32[]{:S(2)}) copy-start(bf16[272,1024]{1,0:T(8,128)(2,1)} %copy-done.19) | copy-start | bytes 1671172
  255.6 34.6 %copy-start.16 = (bf16[2,4,128,512]{3,2,1,0:T(8,128)(2,1)}, bf16[2,4,128,512]{3,2,1,0:T(8,128)(2,1)S(1)}, u32[]{:S(2)}) copy-start(bf16[2,4,128,512]{3,2,1,0:T(8,128)(2,1)S(1)} %pad_maximum_fusion.1.refs_2_) | copy-start | bytes 3145732
  256.2 31.6 %copy-start.43 = (bf16[256,512]{1,0:T(8,128)(2,1)}, bf16[256,512]{1,0:T(8,128)(2,1)S(1)}, u32[]{:S(2)}) copy-start(bf16[256,512]{1,0:T(8,128)(2,1)S(1)} %collective-permute-done.37) | copy-start | bytes 786436
  258.9 28.8 %copy-start.45 = (bf16[256,512]{1,0:T(8,128)(2,1)}, bf16[256,512]{1,0:T(8,128)(2,1)S(1)}, u32[]{:S(2)}) copy-start(bf16[256,512]{1,0:T(8,128)(2,1)S(1)} %collective-permute-done.38) | copy-start | bytes 786436
  258.9 28.1 %collective-permute-start.40 = (bf16[2,4,128,512]{3,2,1,0:T(8,128)(2,1)S(1)}, bf16[2,4,128,512]{3,2,1,0:T(8,128)(2,1)}, u32[]{:S(2)}, u32[]{:S(2)}) collective-permute-start(bf16[2,4,128,512]{3,2,1,0:T(8,128)(2,1)S(1)} %pad_maximum_fusion.1.refs_2_), channel_id=1, source_target_pairs={{0,4},{4,0},{8,12},{12,8},{16,20},{20,16},{24,28},{28,24},{1,5},{5... | collective-permute-start | bytes 3145736 | tf_op jit(solution)/shard_map/ppermute | solution.py:31
  260.5 26.5 %collective-permute-start.39 = (bf16[1,2,4,128,512]{4,3,2,1,0:T(8,128)(2,1)S(1)}, bf16[1,2,4,128,512]{4,3,2,1,0:T(8,128)(2,1)}, u32[]{:S(2)}, u32[]{:S(2)}) collective-permute-start(bf16[1,2,4,128,512]{4,3,2,1,0:T(8,128)(2,1)S(1)} %maximum_bitcast_fusion.refs_0_), channel_id=1, source_target_pairs={{0,2},{1,3},{2,0},{3,1},{4,6},{5,7},{6,4},{7,5},{8,10},{9,11},{10,... | collective-permute-start | bytes 3145736 | tf_op jit(solution)/shard_map/ppermute | solution.py:31
  261.6 25.2 %collective-permute-start.41 = (bf16[272,1024]{1,0:T(8,128)(2,1)}, bf16[272,1024]{1,0:T(8,128)(2,1)S(1)}, u32[]{:S(2)}, u32[]{:S(2)}) collective-permute-start(bf16[272,1024]{1,0:T(8,128)(2,1)} %fusion.7), channel_id=1, source_target_pairs={{0,24},{4,28},{24,0},{28,4},{1,25},{5,29},{25,1},{29,5},{2,26},{6,... | collective-permute-start | bytes 1671176 | tf_op jit(solution)/shard_map/ppermute | solution.py:765
  264.8 21.5 %collective-permute-start.42 = (bf16[256,512]{1,0:T(8,128)(2,1)S(1)}, bf16[256,512]{1,0:T(8,128)(2,1)S(1)}, u32[]{:S(2)}, u32[]{:S(2)}) collective-permute-start(bf16[256,512]{1,0:T(8,128)(2,1)S(1)} %copy-done.30), channel_id=1, source_target_pairs={{0,12},{4,8},{8,4},{12,0},{16,28},{20,24},{24,20},{28,16},{1,13},{... | collective-permute-start | bytes 786440 | tf_op jit(solution)/shard_map/ppermute | solution.py:765
  264.9 21.4 %collective-permute-start.43 = (bf16[256,512]{1,0:T(8,128)(2,1)S(1)}, bf16[256,512]{1,0:T(8,128)(2,1)S(1)}, u32[]{:S(2)}, u32[]{:S(2)}) collective-permute-start(bf16[256,512]{1,0:T(8,128)(2,1)S(1)} %copy-done.29), channel_id=1, source_target_pairs={{0,16},{4,20},{8,24},{12,28},{16,0},{20,4},{24,8},{28,12},{1,17},{... | collective-permute-start | bytes 786440 | tf_op jit(solution)/shard_map/ppermute | solution.py:765
  286.3 5.6 %collective-permute-start.46 = (bf16[2,4,128,512]{3,2,1,0:T(8,128)(2,1)S(1)}, bf16[2,4,128,512]{3,2,1,0:T(8,128)(2,1)}, u32[]{:S(2)}, u32[]{:S(2)}) collective-permute-start(bf16[2,4,128,512]{3,2,1,0:T(8,128)(2,1)S(1)} %pad_maximum_fusion.1.refs_2_), channel_id=1, source_target_pairs={{0,1},{1,0},{2,3},{3,2},{4,5},{5,4},{6,7},{7,6},{8,9},{9,8},{10,11... | collective-permute-start | bytes 3145736 | tf_op jit(solution)/shard_map/ppermute | solution.py:31
  286.3 10.5 %collective-permute-start.44 = (bf16[1,2,4,128,512]{4,3,2,1,0:T(8,128)(2,1)S(1)}, bf16[1,2,4,128,512]{4,3,2,1,0:T(8,128)(2,1)}, u32[]{:S(2)}, u32[]{:S(2)}) collective-permute-start(bf16[1,2,4,128,512]{4,3,2,1,0:T(8,128)(2,1)S(1)} %maximum_bitcast_fusion.refs_0_), channel_id=1, source_target_pairs={{0,1},{1,0},{2,3},{3,2},{4,5},{5,4},{6,7},{7,6},{8,9},{9,8},{10,11... | collective-permute-start | bytes 3145736 | tf_op jit(solution)/shard_map/ppermute | solution.py:31
  287.6 10.5 %collective-permute-start.47 = (bf16[2,4,128,512]{3,2,1,0:T(8,128)(2,1)}, bf16[2,4,128,512]{3,2,1,0:T(8,128)(2,1)}, u32[]{:S(2)}, u32[]{:S(2)}) collective-permute-start(bf16[2,4,128,512]{3,2,1,0:T(8,128)(2,1)} %collective-permute-done.40.refs_3_), channel_id=1, source_target_pairs={{0,1},{1,0},{2,3},{3,2},{4,5},{5,4},{6,7},{7,6},{8,9},{9,8},{10,11... | collective-permute-start | bytes 3145736 | tf_op jit(solution)/shard_map/ppermute | solution.py:31
  287.7 14.9 %collective-permute-start.45 = (bf16[1,2,4,128,512]{4,3,2,1,0:T(8,128)(2,1)}, bf16[1,2,4,128,512]{4,3,2,1,0:T(8,128)(2,1)}, u32[]{:S(2)}, u32[]{:S(2)}) collective-permute-start(bf16[1,2,4,128,512]{4,3,2,1,0:T(8,128)(2,1)} %collective-permute-done.39.refs_1_), channel_id=1, source_target_pairs={{0,1},{1,0},{2,3},{3,2},{4,5},{5,4},{6,7},{7,6},{8,9},{9,8},{10,11... | collective-permute-start | bytes 3145736 | tf_op jit(solution)/shard_map/ppermute | solution.py:31
  290.9 34.6 %collective-permute-start.48 = (bf16[256,512]{1,0:T(8,128)(2,1)S(1)}, bf16[256,512]{1,0:T(8,128)(2,1)}, u32[]{:S(2)}, u32[]{:S(2)}) collective-permute-start(bf16[256,512]{1,0:T(8,128)(2,1)S(1)} %copy-done.28), channel_id=1, source_target_pairs={{0,12},{4,8},{8,4},{12,0},{16,28},{20,24},{24,20},{28,16},{1,13},{... | collective-permute-start | bytes 786440 | tf_op jit(solution)/shard_map/ppermute | solution.py:765
  291.9 33.6 %collective-permute-start.49 = (bf16[256,512]{1,0:T(8,128)(2,1)S(1)}, bf16[256,512]{1,0:T(8,128)(2,1)S(1)}, u32[]{:S(2)}, u32[]{:S(2)}) collective-permute-start(bf16[256,512]{1,0:T(8,128)(2,1)S(1)} %copy-done.27), channel_id=1, source_target_pairs={{0,20},{4,16},{8,28},{12,24},{16,4},{20,0},{24,12},{28,8},{1,21},{... | collective-permute-start | bytes 786440 | tf_op jit(solution)/shard_map/ppermute | solution.py:765
  296.8 28.7 %collective-permute-start.50 = (bf16[256,512]{1,0:T(8,128)(2,1)S(1)}, bf16[256,512]{1,0:T(8,128)(2,1)S(1)}, u32[]{:S(2)}, u32[]{:S(2)}) collective-permute-start(bf16[256,512]{1,0:T(8,128)(2,1)S(1)} %copy-done.26), channel_id=1, source_target_pairs={{0,24},{4,28},{8,16},{12,20},{16,8},{20,12},{24,0},{28,4},{1,25},{... | collective-permute-start | bytes 786440 | tf_op jit(solution)/shard_map/ppermute | solution.py:765
  298.2 27.4 %collective-permute-start.51 = (bf16[256,512]{1,0:T(8,128)(2,1)S(1)}, bf16[256,512]{1,0:T(8,128)(2,1)S(1)}, u32[]{:S(2)}, u32[]{:S(2)}) collective-permute-start(bf16[256,512]{1,0:T(8,128)(2,1)S(1)} %copy-done.25), channel_id=1, source_target_pairs={{0,28},{4,24},{24,4},{28,0},{1,29},{5,25},{25,5},{29,1},{2,30},{6,... | collective-permute-start | bytes 786440 | tf_op jit(solution)/shard_map/ppermute | solution.py:765
  349.2 1.2 collective-permute-start.52
  350.5 3.7 %collective-permute-start.53 = (f32[3,256]{1,0:T(4,128)S(1)}, f32[3,256]{1,0:T(4,128)S(1)}, u32[]{:S(2)}, u32[]{:S(2)}) collective-permute-start(f32[3,256]{1,0:T(4,128)S(1)} %pad_maximum_fusion.7), channel_id=1, source_target_pairs={{0,2},{1,3},{2,0},{3,1},{4,6},{5,7},{6,4},{7,5},{8,10},{9,11},{10,... | collective-permute-start | bytes 9224 | tf_op jit(solution)/shard_map/ppermute | solution.py:31
  (61 other events, 409.1 us)
